TPU v7x, 32 devices: a whole 2x2x4 slice. The times are simulated.
32 devices in a mesh: rollout: 4 (over y, x), context: 4 (over z), head: 2 (over core).
Axes of the slice: x: 2, y: 2, z: 4, core: 2. Of those that a mesh axis runs over, the one named last changes fastest.
Arguments:
- qkv: bfloat16 [3, 4, 512, 32, 128], P(None, 'rollout', 'context', 'head'), may hold values from -18 to 18
- ssd_b: bfloat16 [4, 512, 128], P('rollout', 'context'), may hold values from -5 to 5
- ssd_c: bfloat16 [4, 512, 128], P('rollout', 'context'), may hold values from -0.5 to 0.5
- step_size: float32 [4, 512, 64], P('rollout', 'context', 'head'), may hold values from 0 to 0.3, as said below
- decay_rate: float32 [64], P('head'), may hold values from 0.5 to 2
- value_weight: bfloat16 [4096], P('head'), may hold values from -0.09375 to 0.09375
- returns: float32 [4, 64], P('rollout'), may hold values from -4 to 4
- step_labels: int32 [4, 512], P('rollout', 'context'), may hold values from 0 to 63, never falling along the last dimension, each value on 1 to 128 neighbouring positions
- lengths: int32 [4], replicated, may hold values from 128 to 512, as said below
Outputs:
- loss: float32 [], replicated
- grad_qkv: bfloat16 [3, 4, 512, 32, 128], P(None, 'rollout', 'context', 'head')
- grad_b: float32 [4, 512, 128], P('rollout', 'context')
- grad_c: float32 [4, 512, 128], P('rollout', 'context')
- grad_step: float32 [4, 512, 64], P('rollout', 'context', 'head')
- grad_rate: float32 [64], P('head')
- grad_value: float32 [4096], P('head')
Inputs may be any that keep to these rules, and one draw needn't show every extreme that they name: `step_size`: positive. `lengths`: one rollout in every draw is full. `step_labels`: never falling along a rollout.
All inputs are finite; a program needn't handle non-finite values.
Results may differ from a plain program's by a relative error of at most 0.011.
Values may be sent and summed in bfloat16 or wider, within the bound.
No kernel may reach another device: no remote copies, remote signals or barrier semaphores. Data moves between devices by JAX's collectives and lax.ppermute only.
A program may use at most 192 MiB of HBM per device.

v0:
```python
import math

import jax
import jax.numpy as jnp
from jax import lax
from jax.sharding import PartitionSpec as P

MASK_FILL = -1e30
NORM_EPS = 1e-05
HIGHEST_PREC = lax.Precision.HIGHEST


def block_probs(query_block, key_rows, first_row):
    head_size = query_block.shape[1]
    scores = lax.dot_general(
        query_block, key_rows, (((1,), (1,)), ((), ())), preferred_element_type=jnp.float32
    )
    scores = scores * (1.0 / math.sqrt(head_size))
    row_ids = first_row + jnp.arange(query_block.shape[0], dtype=jnp.int32)[:, None]
    col_ids = jnp.arange(key_rows.shape[0], dtype=jnp.int32)[None, :]
    scores = jnp.where(col_ids <= row_ids, scores, MASK_FILL)
    row_max = lax.stop_gradient(jnp.max(scores, axis=1, keepdims=True))
    weights = jnp.exp(scores - row_max)
    return weights / jnp.sum(weights, axis=1, keepdims=True)


def head_forward(queries, key_rows, values):
    block_rows = min(512, queries.shape[0])
    block_count = queries.shape[0] // block_rows
    blocks = queries.reshape(block_count, block_rows, queries.shape[1])
    starts = jnp.arange(block_count, dtype=jnp.int32) * block_rows

    def one_block(operands):
        probability = block_probs(operands[0], key_rows, operands[1]).astype(jnp.bfloat16)
        return jnp.dot(probability, values, preferred_element_type=jnp.float32).astype(jnp.bfloat16)

    return lax.map(one_block, (blocks, starts)).reshape(queries.shape)


def head_backward(queries, key_rows, values, grad_out):
    head_size = queries.shape[1]
    block_rows = min(512, queries.shape[0])
    block_count = queries.shape[0] // block_rows
    blocks = queries.reshape(block_count, block_rows, head_size)
    grad_blocks = grad_out.reshape(block_count, block_rows, head_size)
    starts = jnp.arange(block_count, dtype=jnp.int32) * block_rows

    def one_block(carried, operands):
        key_grad, value_grad = carried
        query_block, grad_block, first_row = operands
        probability = block_probs(query_block, key_rows, first_row)
        rounded = probability.astype(jnp.bfloat16)
        value_grad = value_grad + lax.dot_general(
            rounded, grad_block, (((0,), (0,)), ((), ())), preferred_element_type=jnp.float32
        )
        prob_grad = lax.dot_general(
            grad_block, values, (((1,), (1,)), ((), ())), preferred_element_type=jnp.float32
        )
        centre = jnp.sum(probability * prob_grad, axis=1, keepdims=True)
        score_grad = (probability * (prob_grad - centre) * (1.0 / math.sqrt(head_size))).astype(
            jnp.bfloat16
        )
        query_grad = jnp.dot(score_grad, key_rows, preferred_element_type=jnp.float32).astype(
            jnp.bfloat16
        )
        key_grad = key_grad + lax.dot_general(
            score_grad, query_block, (((0,), (0,)), ((), ())), preferred_element_type=jnp.float32
        )
        return ((key_grad, value_grad), query_grad)

    zero_grad = jnp.zeros(key_rows.shape, jnp.float32)
    totals, query_grad = lax.scan(one_block, (zero_grad, zero_grad), (blocks, grad_blocks, starts))
    return (query_grad.reshape(queries.shape), totals[0], totals[1])


def attend(queries, key_rows, values):

    def per_head(operands):
        return head_forward(operands[0], operands[1], operands[2])

    result = lax.map(
        per_head,
        (jnp.swapaxes(queries, 0, 1), jnp.swapaxes(key_rows, 0, 1), jnp.swapaxes(values, 0, 1)),
    )
    return jnp.swapaxes(result, 0, 1)


def attend_back(queries, key_rows, values, grad_out):

    def per_head(operands):
        return head_backward(operands[0], operands[1], operands[2], operands[3])

    query_grad, key_grad, value_grad = lax.map(
        per_head,
        (
            jnp.swapaxes(queries, 0, 1),
            jnp.swapaxes(key_rows, 0, 1),
            jnp.swapaxes(values, 0, 1),
            jnp.swapaxes(grad_out, 0, 1),
        ),
    )
    return (
        jnp.swapaxes(query_grad, 0, 1),
        jnp.swapaxes(key_grad, 0, 1),
        jnp.swapaxes(value_grad, 0, 1),
    )


def ssd_parts(inputs, step_dt, rate, b_proj):
    cumulative = jnp.cumsum(-step_dt * rate[None, :], axis=0)
    tail_decay = jnp.exp(cumulative[-1:, :] - cumulative)
    state_term = jnp.einsum("th,thp,tn->hpn", tail_decay, inputs, b_proj, precision=HIGHEST_PREC)
    return (jnp.exp(cumulative[-1]), state_term)


def ssd_output(inputs, step_dt, rate, inner_prod, c_proj, state_in):
    cumulative = jnp.cumsum(-step_dt * rate[None, :], axis=0)
    cum_heads = cumulative.T
    row_count = inputs.shape[0]
    causal = (jnp.arange(row_count)[:, None] >= jnp.arange(row_count)[None, :])[None]
    log_gap = jnp.where(causal, cum_heads[:, :, None] - cum_heads[:, None, :], 0.0)
    decay_mask = jnp.where(causal, jnp.exp(log_gap), 0.0)
    local_out = jnp.einsum(
        "hts,shp->thp", decay_mask * inner_prod[None], inputs, precision=HIGHEST_PREC
    )
    carried = (
        jnp.einsum("tn,hpn->thp", c_proj, state_in, precision=HIGHEST_PREC)
        * jnp.exp(cumulative)[:, :, None]
    )
    return local_out + carried


def value_part(outputs, weight):
    norm_scale = lax.rsqrt(jnp.mean(outputs * outputs, axis=2, keepdims=True) + NORM_EPS)
    normed = (outputs * norm_scale).reshape(outputs.shape[0], -1)
    return jnp.dot(normed, weight, precision=HIGHEST_PREC)


def gathered_prefix(decays, terms, my_index, reverse):
    block_total = decays.shape[0]

    def advance(loop_index, running):
        source = block_total - 1 - loop_index if reverse else loop_index
        use_it = source > my_index if reverse else source < my_index
        updated = decays[source][:, None, None] * running + terms[source]
        return jnp.where(use_it, updated, running)

    return lax.fori_loop(0, block_total, advance, jnp.zeros(terms.shape[1:], jnp.float32))


def local(qkv, ssd_b, ssd_c, step_size, decay_rate, value_weight, returns, step_labels, lengths):
    tokens = qkv.shape[2]
    heads_here = qkv.shape[3]
    head_size = qkv.shape[4]
    context = lax.axis_size("context")
    my_index = lax.axis_index("context")
    offset = my_index * tokens
    spread = lax.all_to_all(qkv, "context", split_axis=3, concat_axis=2, tiled=True)
    queries, key_rows, values = (spread[0, 0], spread[1, 0], spread[2, 0])
    mixed_heads = attend(queries, key_rows, values)
    attended = lax.all_to_all(mixed_heads, "context", split_axis=0, concat_axis=1, tiled=True)
    ssd_heads = step_size.shape[2]
    inputs = attended.reshape(tokens, ssd_heads, -1).astype(jnp.float32)
    step_dt = step_size[0]
    b_proj = ssd_b[0].astype(jnp.float32)
    c_proj = ssd_c[0].astype(jnp.float32)
    inner_prod = jnp.dot(ssd_c[0], ssd_b[0].T, preferred_element_type=jnp.float32)
    (decays, local_state), parts_back = jax.vjp(ssd_parts, inputs, step_dt, decay_rate, b_proj)
    all_decays, all_states = (
        lax.all_gather(decays, "context", axis=0, tiled=True),
        lax.all_gather(local_state, "context", axis=0, tiled=True),
    )
    state_in = gathered_prefix(
        all_decays.reshape(context, ssd_heads),
        all_states.reshape((context,) + local_state.shape),
        my_index,
        False,
    )
    outputs, output_back = jax.vjp(
        ssd_output, inputs, step_dt, decay_rate, inner_prod, c_proj, state_in
    )
    weight_full = value_weight.astype(jnp.float32)
    value_here, value_back = jax.vjp(value_part, outputs, weight_full)
    value = lax.psum(value_here, "head")
    return_table = returns[0]
    onehot = (
        step_labels[0][:, None] == jnp.arange(return_table.shape[0], dtype=jnp.int32)[None, :]
    ).astype(jnp.float32)
    target = jnp.dot(onehot, return_table, precision=HIGHEST_PREC)
    my_length = lax.dynamic_index_in_dim(lengths, lax.axis_index("rollout"), 0, keepdims=False)
    positions = offset + jnp.arange(tokens, dtype=jnp.int32)
    valid_mask = (positions < my_length).astype(jnp.float32)
    error_term = (value - target) * valid_mask
    loss_here = 0.5 * jnp.sum(error_term * error_term)
    output_grad, weight_grad = value_back(error_term)
    exp_cum = jnp.exp(jnp.cumsum(-step_dt * decay_rate[None, :], axis=0))
    carried_grad = jnp.einsum(
        "th,thp,tn->hpn", exp_cum, output_grad, c_proj, precision=HIGHEST_PREC
    )
    grad_decays, grad_states = (
        lax.all_gather(decays, "context", axis=0, tiled=True),
        lax.all_gather(carried_grad, "context", axis=0, tiled=True),
    )
    state_out_grad = gathered_prefix(
        grad_decays.reshape(context, ssd_heads),
        grad_states.reshape((context,) + carried_grad.shape),
        my_index,
        True,
    )
    decay_cot = jnp.sum(state_out_grad * state_in, axis=(1, 2))
    input_first, step_first, rate_first, b_first = parts_back((decay_cot, state_out_grad))
    input_second, step_second, rate_second, inner_grad, c_direct, unused = output_back(output_grad)
    c_second = c_direct + jnp.dot(inner_grad, b_proj, precision=HIGHEST_PREC)
    b_second = jnp.dot(inner_grad.T, c_proj, precision=HIGHEST_PREC)
    input_grad = input_first + input_second
    b_grad, c_grad = (
        lax.psum((b_first + b_second).astype(jnp.bfloat16), "head").astype(jnp.float32),
        lax.psum(c_second.astype(jnp.bfloat16), "head").astype(jnp.float32),
    )
    loss_total, weight_total, rate_total = lax.psum(
        (loss_here, weight_grad, rate_first + rate_second), ("rollout", "context")
    )
    loss = loss_total / jnp.sum(lengths).astype(jnp.float32)
    attended_grad = input_grad.reshape(tokens, heads_here, head_size).astype(jnp.bfloat16)
    spread_grad = lax.all_to_all(attended_grad, "context", split_axis=1, concat_axis=0, tiled=True)
    query_grad, key_grad, value_grad = attend_back(queries, key_rows, values, spread_grad)
    stacked = jnp.stack(
        [query_grad, key_grad.astype(jnp.bfloat16), value_grad.astype(jnp.bfloat16)]
    )[:, None]
    qkv_grad = lax.all_to_all(stacked, "context", split_axis=2, concat_axis=3, tiled=True)
    return (
        loss,
        qkv_grad,
        b_grad[None],
        c_grad[None],
        (step_first + step_second)[None],
        rate_total,
        weight_total,
    )


def solution(mesh):
    in_specs = (
        P(None, "rollout", "context", "head", None),
        P("rollout", "context", None),
        P("rollout", "context", None),
        P("rollout", "context", "head"),
        P("head"),
        P("head"),
        P("rollout", None),
        P("rollout", "context"),
        P(),
    )
    out_specs = (
        P(),
        P(None, "rollout", "context", "head", None),
        P("rollout", "context", None),
        P("rollout", "context", None),
        P("rollout", "context", "head"),
        P("head"),
        P("head"),
    )
    return jax.shard_map(local, mesh=mesh, in_specs=in_specs, out_specs=out_specs, check_vma=False)
```

profile of v0, /device:TPU:0, one launch (start us, length us, event | category | flops | bytes accessed | tf_op | source)
XLA Modules:
  0.0 472.8 jit_solution(13493630451523262832)
XLA Ops:
  7.2 3.0 copy.46
  10.1 6.3 %all-to-all-start = ((bf16[3,1,128,16,128]{4,2,1,0,3:T(8,128)(2,1)}), bf16[3,1,128,16,128]{4,2,1,0,3:T(8,128)(2,1)S(1)}, u32[]{:S(2)}, u32[]{:S(2)}) async-start(bf16[3,1,128,16,128]{4,2,1,0,3:T(8,128)(2,1)} %copy.46), calls=%async_computation | async-start | bytes 3145728 | tf_op jit(solution)/shard_map/all_to_all | solution.py:158
  16.5 37.0 %all-to-all-done = bf16[3,1,128,16,128]{4,2,1,0,3:T(8,128)(2,1)S(1)} async-done(((bf16[3,1,128,16,128]{4,2,1,0,3:T(8,128)(2,1)}), bf16[3,1,128,16,128]{4,2,1,0,3:T(8,128)(2,1)S(1)}, u32[]{:S(2)}, u32[]{:S(2)}) %all-to-all-start) | async-done | bytes 1572896 | tf_op jit(solution)/shard_map/all_to_all | solution.py:158
  54.6 7.5 %while.64 = (s32[]{:T(128)}, bf16[4,512,128]{2,1,0:T(8,128)(2,1)S(1)}, bf16[4,512,128]{2,1,0:T(8,128)(2,1)S(1)}, bf16[4,512,128]{2,1,0:T(8,128)(2,1)}, bf16[4,512,128]{2,1,0:T(8,128)(2,1)S(1)}, /*index=5*/s32[]{:T(128)}) while((s32[]{:T(128)}, bf16[4,512,128]{2,1,0:T(8,128)(2,1)S(1)}, bf16[4,512,128]{2,1,0:T(8,128)(2,1)S(1)}, ...), condition=%wide.region_3.4_spmd, body=%wide.region_0.3_spmd.sunk | while | flops 136641536 | bytes 3682373 | solution.py:81
  63.3 3.5 all-to-all-start.1
  67.3 13.5 %all-to-all-done.1 = bf16[512,4,128]{2,1,0:T(4,128)(2,1)S(1)} async-done(((bf16[512,4,128]{2,1,0:T(4,128)(2,1)}), bf16[512,4,128]{2,1,0:T(4,128)(2,1)S(1)}, u32[]{:S(2)}, u32[]{:S(2)}) %all-to-all-start.1) | async-done | bytes 524320 | tf_op jit(solution)/shard_map/all_to_all | solution.py:161
  81.1 1.6 fusion.65
  84.3 9.9 %all-reduce.2 = f32[128]{0:T(128)S(1)} all-reduce(f32[128]{0:T(128)S(1)} %exponential_dynamic-update-slice_fusion), channel_id=1, replica_groups=mesh['rollout'=4,'context'=4,'head'=2] {'context'}, use_global_device_ids=true, to_apply=%add.2 | all-reduce | flops 128 | bytes 1024
  95.1 67.6 %all-gather.3.cloned.1.call-done = f32[128,64,128]{2,1,0:T(8,128)} async-done(((f32[32,64,128]{2,1,0:T(8,128)}), f32[128,64,128]{2,1,0:T(8,128)}) %all-gather.3.cloned.1.call-update) | async-done | bytes 4194320 | tf_op jit(solution)/shard_map/all_gather | solution.py:171
  162.8 6.0 %while.66 = (s32[]{:T(128)}, f32[32,64,128]{2,1,0:T(8,128)S(1)}, s32[]{:T(128)}, f32[4,32]{1,0:T(4,128)S(1)}, f32[4,32,64,128]{3,2,1,0:T(8,128)}, /*index=5*/s32[]{:T(128)}, s32[]{:T(128)}) while((s32[]{:T(128)}, f32[32,64,128]{2,1,0:T(8,128)S(1)}, s32[]{:T(128)}, f32[4,32]{1,0:T(4,128)S(1)}, f32[4,32,64,128]{3,2,1,0:T(8,128)}, ...), condition=%wide.region_6.7_spmd.clone, body=%wide.region_5.6_spmd.clone.sunk | while | flops 1048580 | bytes 3146217 | solution.py:148
  162.8 1.5 fusion.165
  164.3 1.5 fusion.165
  165.8 1.5 fusion.165
  167.3 1.5 fusion.165
  169.4 2.4 multiply_reduce_fusion.5
  173.4 2.6 psum.42
  176.0 1.5 multiply_reduce_fusion.7
  177.9 1.6 multiply_reduce_fusion.2
  179.6 1.6 fusion.90
  181.2 79.4 %all-gather.5.cloned.1.call-done = f32[128,64,128]{2,1,0:T(8,128)} async-done(((f32[32,64,128]{2,1,0:T(8,128)}), f32[128,64,128]{2,1,0:T(8,128)}) %all-gather.5.cloned.1.call-update) | async-done | bytes 4194320 | tf_op jit(solution)/shard_map/all_gather | solution.py:202
  260.7 8.7 %while.67 = (s32[]{:T(128)}, f32[32,64,128]{2,1,0:T(8,128)S(1)}, s32[]{:T(128)}, f32[4,32]{1,0:T(4,128)}, f32[4,32,64,128]{3,2,1,0:T(8,128)}, /*index=5*/s32[]{:T(128)}, s32[]{:T(128)}, s32[]{:T(128)}, s32[]{:T(128)}) while((s32[]{:T(128)}, f32[32,64,128]{2,1,0:T(8,128)S(1)}, s32[]{:T(128)}, f32[4,32]{1,0:T(4,128)}, ...), condition=%wide.region_14.15_spmd.clone, body=%wide.region_13.14_spmd.clone.sunk | while | flops 1048584 | bytes 3146279 | solution.py:148
  261.3 1.5 fusion.166
  263.5 1.5 fusion.166
  267.9 1.5 fusion.166
  269.4 2.7 fusion.75
  272.1 3.2 fusion.61
  275.3 3.6 all-to-all-start.2
  280.2 13.4 %all-to-all-done.2 = bf16[128,16,128]{0,2,1:T(8,128)(2,1)S(1)} async-done(((bf16[128,16,128]{0,2,1:T(8,128)(2,1)}), bf16[128,16,128]{0,2,1:T(8,128)(2,1)S(1)}, u32[]{:S(2)}, u32[]{:S(2)}) %all-to-all-start.2) | async-done | bytes 524320 | tf_op jit(solution)/shard_map/all_to_all | solution.py:225
  295.5 85.1 %while.65 = (s32[]{:T(128)}, bf16[4,512,128]{2,1,0:T(8,128)(2,1)}, bf16[4,512,128]{2,0,1:T(4,128)(2,1)}, bf16[4,512,128]{2,0,1:T(4,128)(2,1)}, bf16[4,512,128]{2...) while((s32[]{:T(128)}, bf16[4,512,128]{2,1,0:T(8,128)(2,1)}, ...), condition=%wide.region_19.20_spmd, body=%wide.region_15.19_spmd.sunk | while | flops 340589056 | bytes 11560561 | solution.py:93
  298.2 7.4 %dynamic_update_slice.28 = bf16[4,512,128]{2,0,1:T(4,128)(2,1)} dynamic-update-slice(bf16[4,512,128]{2,0,1:T(4,128)(2,1)} %get-tuple-element.712, f32[1,512,128]{2,0,1:T(1,128)S(1)} %bitcast.281, s32[]{:T(128)} %get-tuple-element.709, s32[]{:T(128)} %constant.178.clone.1..sunk, s32[]{:T(128)} %constant.178.clone.1..sunk) | dynamic-update-slice | bytes 524292 | tf_op jit(solution)/shard_map/while/body/jit(dynamic_update_index_in_dim)/dynamic_update_slice | solution.py:93
  307.4 7.4 %dynamic_update_slice.27 = bf16[4,512,128]{2,0,1:T(4,128)(2,1)} dynamic-update-slice(bf16[4,512,128]{2,0,1:T(4,128)(2,1)} %get-tuple-element.711, f32[1,512,128]{2,0,1:T(1,128)S(1)} %bitcast.273, s32[]{:T(128)} %get-tuple-element.709, s32[]{:T(128)} %constant.178.clone.1..sunk, s32[]{:T(128)} %constant.178.clone.1..sunk) | dynamic-update-slice | bytes 524292 | tf_op jit(solution)/shard_map/while/body/jit(dynamic_update_index_in_dim)/dynamic_update_slice | solution.py:93
  314.9 1.9 fusion.162
  319.4 7.4 %dynamic_update_slice.28 = bf16[4,512,128]{2,0,1:T(4,128)(2,1)} dynamic-update-slice(bf16[4,512,128]{2,0,1:T(4,128)(2,1)} %get-tuple-element.712, f32[1,512,128]{2,0,1:T(1,128)S(1)} %bitcast.281, s32[]{:T(128)} %get-tuple-element.709, s32[]{:T(128)} %constant.178.clone.1..sunk, s32[]{:T(128)} %constant.178.clone.1..sunk) | dynamic-update-slice | bytes 524292 | tf_op jit(solution)/shard_map/while/body/jit(dynamic_update_index_in_dim)/dynamic_update_slice | solution.py:93
  328.7 7.4 %dynamic_update_slice.27 = bf16[4,512,128]{2,0,1:T(4,128)(2,1)} dynamic-update-slice(bf16[4,512,128]{2,0,1:T(4,128)(2,1)} %get-tuple-element.711, f32[1,512,128]{2,0,1:T(1,128)S(1)} %bitcast.273, s32[]{:T(128)} %get-tuple-element.709, s32[]{:T(128)} %constant.178.clone.1..sunk, s32[]{:T(128)} %constant.178.clone.1..sunk) | dynamic-update-slice | bytes 524292 | tf_op jit(solution)/shard_map/while/body/jit(dynamic_update_index_in_dim)/dynamic_update_slice | solution.py:93
  336.1 1.9 fusion.162
  340.7 7.4 %dynamic_update_slice.28 = bf16[4,512,128]{2,0,1:T(4,128)(2,1)} dynamic-update-slice(bf16[4,512,128]{2,0,1:T(4,128)(2,1)} %get-tuple-element.712, f32[1,512,128]{2,0,1:T(1,128)S(1)} %bitcast.281, s32[]{:T(128)} %get-tuple-element.709, s32[]{:T(128)} %constant.178.clone.1..sunk, s32[]{:T(128)} %constant.178.clone.1..sunk) | dynamic-update-slice | bytes 524292 | tf_op jit(solution)/shard_map/while/body/jit(dynamic_update_index_in_dim)/dynamic_update_slice | solution.py:93
  350.0 7.4 %dynamic_update_slice.27 = bf16[4,512,128]{2,0,1:T(4,128)(2,1)} dynamic-update-slice(bf16[4,512,128]{2,0,1:T(4,128)(2,1)} %get-tuple-element.711, f32[1,512,128]{2,0,1:T(1,128)S(1)} %bitcast.273, s32[]{:T(128)} %get-tuple-element.709, s32[]{:T(128)} %constant.178.clone.1..sunk, s32[]{:T(128)} %constant.178.clone.1..sunk) | dynamic-update-slice | bytes 524292 | tf_op jit(solution)/shard_map/while/body/jit(dynamic_update_index_in_dim)/dynamic_update_slice | solution.py:93
  357.4 1.9 fusion.162
  361.9 7.4 %dynamic_update_slice.28 = bf16[4,512,128]{2,0,1:T(4,128)(2,1)} dynamic-update-slice(bf16[4,512,128]{2,0,1:T(4,128)(2,1)} %get-tuple-element.712, f32[1,512,128]{2,0,1:T(1,128)S(1)} %bitcast.281, s32[]{:T(128)} %get-tuple-element.709, s32[]{:T(128)} %constant.178.clone.1..sunk, s32[]{:T(128)} %constant.178.clone.1..sunk) | dynamic-update-slice | bytes 524292 | tf_op jit(solution)/shard_map/while/body/jit(dynamic_update_index_in_dim)/dynamic_update_slice | solution.py:93
  371.2 7.4 %dynamic_update_slice.27 = bf16[4,512,128]{2,0,1:T(4,128)(2,1)} dynamic-update-slice(bf16[4,512,128]{2,0,1:T(4,128)(2,1)} %get-tuple-element.711, f32[1,512,128]{2,0,1:T(1,128)S(1)} %bitcast.273, s32[]{:T(128)} %get-tuple-element.709, s32[]{:T(128)} %constant.178.clone.1..sunk, s32[]{:T(128)} %constant.178.clone.1..sunk) | dynamic-update-slice | bytes 524292 | tf_op jit(solution)/shard_map/while/body/jit(dynamic_update_index_in_dim)/dynamic_update_slice | solution.py:93
  378.6 1.9 fusion.162
  382.0 3.6 maximum_bitcast_fusion
  385.6 4.5 all-to-all-start.3
  390.3 3.2 fusion.67
  395.5 3.0 convolution_bitcast_fusion.2
  401.9 2.9 fusion.68
  405.8 52.1 %all-reduce.3 = (f32[]{:T(128)}, f32[32]{0:T(128)}, f32[2048]{0:T(1024)}) all-reduce(f32[]{:T(128)S(6)} %mul_shard_map.3, f32[32]{0:T(128)S(1)} %add.170, f32[2048]{0:T(1024)S(1)} %bitcast.296), channel_id=1, replica_groups=mesh['rollout'=4,'context'=4,'head'=2] {'rollout','context'}, use_global_device_ids=true, to_apply=%region_10.11 | all-reduce | flops 2081 | bytes 16648 | tf_op jit(solution)/shard_map/psum | solution.py:220
  462.0 3.1 copy.61
  (182 shorter events, 50.4 us)
Async XLA Ops:
  7.2 73.9 %copy-start = (bf16[1,128,128]{2,1,0:T(8,128)(2,1)S(1)}, bf16[1,128,128]{2,1,0:T(8,128)(2,1)}, u32[]{:S(2)}) copy-start(bf16[1,128,128]{2,1,0:T(8,128)(2,1)} %param.18) | copy-start | bytes 98308
  10.1 43.3 %all-to-all-start = ((bf16[3,1,128,16,128]{4,2,1,0,3:T(8,128)(2,1)}), bf16[3,1,128,16,128]{4,2,1,0,3:T(8,128)(2,1)S(1)}, u32[]{:S(2)}, u32[]{:S(2)}) async-start(bf16[3,1,128,16,128]{4,2,1,0,3:T(8,128)(2,1)} %copy.46), calls=%async_computation | async-start | bytes 3145728 | tf_op jit(solution)/shard_map/all_to_all | solution.py:158
  62.0 18.7 %copy-start.10 = (bf16[4,512,128]{2,1,0:T(8,128)(2,1)}, bf16[4,512,128]{2,1,0:T(8,128)(2,1)S(1)}, u32[]{:S(2)}) copy-start(bf16[4,512,128]{2,1,0:T(8,128)(2,1)S(1)} %get-tuple-element.746) | copy-start | bytes 1572868
  62.1 20.6 %copy-start.13 = (bf16[4,512,128]{2,1,0:T(8,128)(2,1)}, bf16[4,512,128]{2,1,0:T(8,128)(2,1)S(1)}, u32[]{:S(2)}) copy-start(bf16[4,512,128]{2,1,0:T(8,128)(2,1)S(1)} %get-tuple-element.749) | copy-start | bytes 1572868
  62.1 4.8 %copy-start.18 = (f32[1,128,32]{1,2,0:T(8,128)S(1)}, f32[1,128,32]{1,2,0:T(8,128)}, u32[]{:S(2)}) copy-start(f32[1,128,32]{1,2,0:T(8,128)} %param.20) | copy-start | bytes 49156
  62.1 4.9 %copy-start.28 = (f32[32]{0:T(128)S(1)}, f32[32]{0:T(128)}, u32[]{:S(2)}) copy-start(f32[32]{0:T(128)} %param.21) | copy-start | bytes 388
  63.3 17.4 %all-to-all-start.1 = ((bf16[512,4,128]{2,1,0:T(4,128)(2,1)}), bf16[512,4,128]{2,1,0:T(4,128)(2,1)S(1)}, u32[]{:S(2)}, u32[]{:S(2)}) async-start(bf16[512,4,128]{2,1,0:T(4,128)(2,1)} %bitcast.232), calls=%async_computation.1 | async-start | bytes 1048576 | tf_op jit(solution)/shard_map/all_to_all | solution.py:161
  66.8 96.0 %all-gather.3.cloned.1.call-start = ((), (), s32[]{:S(2)}) async-start(), calls=%async_computation.4 | async-start | bytes 5242880 | tf_op jit(solution)/shard_map/all_gather | solution.py:171
  67.0 15.9 %copy-start.21 = (bf16[2048]{0:T(1024)(128)(2,1)S(1)}, bf16[2048]{0:T(1024)(128)(2,1)}, u32[]{:S(2)}) copy-start(bf16[2048]{0:T(1024)(128)(2,1)} %param.22) | copy-start | bytes 12292
  67.0 15.9 %copy-start.35 = (u32[32]{0:T(128)S(1)}, u32[32]{0:T(128)}, u32[]{:S(2)}) copy-start(u32[32]{0:T(128)} %constant.198) | copy-start | bytes 388
  67.2 15.6 %copy-start.24 = (f32[32]{0:T(128)}, f32[32]{0:T(128)S(1)}, u32[]{:S(2)}) copy-start(f32[32]{0:T(128)S(1)} %slice_bitcast_fusion) | copy-start | bytes 388
  67.2 27.1 %copy-start.33 = (s32[4]{0:T(128)S(1)}, s32[4]{0:T(128)}, u32[]{:S(2)}) copy-start(s32[4]{0:T(128)} %param.25) | copy-start | bytes 52
  67.2 27.8 %copy-start.12 = (bf16[1,128,128]{2,1,0:T(8,128)(2,1)S(1)}, bf16[1,128,128]{2,1,0:T(8,128)(2,1)}, u32[]{:S(2)}) copy-start(bf16[1,128,128]{2,1,0:T(8,128)(2,1)} %param.19) | copy-start | bytes 98308
  81.0 88.3 %copy-start.7 = (bf16[4,128,4,128]{1,3,2,0:T(8,128)(2,1)}, bf16[4,128,4,128]{1,3,2,0:T(8,128)(2,1)S(1)}, u32[]{:S(2)}) copy-start(bf16[4,128,4,128]{1,3,2,0:T(8,128)(2,1)S(1)} %copy.51) | copy-start | bytes 1572868
  82.7 178.0 %all-gather.5.cloned.1.call-start = ((), (), s32[]{:S(2)}) async-start(), calls=%async_computation.5 | async-start | bytes 5242880 | tf_op jit(solution)/shard_map/all_gather | solution.py:202
  94.2 85.3 %copy-start.14 = (f32[128,32]{0,1:T(8,128)}, f32[128,32]{0,1:T(8,128)S(1)}, u32[]{:S(2)}) copy-start(f32[128,32]{0,1:T(8,128)S(1)} %exp.31) | copy-start | bytes 49156
  94.3 75.1 %copy-start.19 = (f32[32,128]{1,0:T(8,128)}, f32[32,128]{1,0:T(8,128)S(1)}, u32[]{:S(2)}) copy-start(f32[32,128]{1,0:T(8,128)S(1)} %copy.53) | copy-start | bytes 49156
  95.0 74.4 %copy-start.22 = (pred[128,128]{1,0:T(8,128)(4,1)}, pred[128,128]{1,0:T(8,128)(4,1)S(1)}, u32[]{:S(2)}) copy-start(pred[128,128]{1,0:T(8,128)(4,1)S(1)} %iota_compare_fusion.3) | copy-start | bytes 49156
  95.1 176.9 %copy-start.16 = (f32[128,128]{1,0:T(8,128)}, f32[128,128]{1,0:T(8,128)S(1)}, u32[]{:S(2)}) copy-start(f32[128,128]{1,0:T(8,128)S(1)} %fusion.106) | copy-start | bytes 196612
  168.7 3.1 copy-start.30
  169.4 2.4 copy-start.9
  171.8 4.2 copy-start.31
  171.8 4.2 copy-start.32
  172.0 1.0 copy-start.3
  177.5 2.0 copy-start.26
  179.6 92.5 %copy-start.5 = (f32[128,32,64]{0,2,1:T(8,128)}, f32[128,32,64]{0,2,1:T(8,128)S(1)}, u32[]{:S(2)}) copy-start(f32[128,32,64]{0,2,1:T(8,128)S(1)} %get-tuple-element.463) | copy-start | bytes 3145732
  269.3 5.9 %copy-start.1 = (f32[32,64,128]{2,1,0:T(8,128)}, f32[32,64,128]{2,1,0:T(8,128)S(1)}, u32[]{:S(2)}) copy-start(f32[32,64,128]{2,1,0:T(8,128)S(1)} %get-tuple-element.345) | copy-start | bytes 3145732
  269.3 2.7 copy-start.20
  269.4 2.7 copy-start.23
  272.0 6.9 %copy-start.34 = (s32[4]{0:T(128)S(1)}, s32[4]{0:T(128)}, u32[]{:S(2)}) copy-start(s32[4]{0:T(128)} %param.25) | copy-start | bytes 52
  275.3 20.2 %copy-start.11 = (bf16[4,512,128]{2,1,0:T(8,128)(2,1)S(1)}, bf16[4,512,128]{2,1,0:T(8,128)(2,1)}, u32[]{:S(2)}) copy-start(bf16[4,512,128]{2,1,0:T(8,128)(2,1)} %copy-done.10) | copy-start | bytes 1572868
  275.3 18.4 %all-to-all-start.2 = ((bf16[128,16,128]{0,2,1:T(8,128)(2,1)}), bf16[128,16,128]{0,2,1:T(8,128)(2,1)S(1)}, u32[]{:S(2)}, u32[]{:S(2)}) async-start(bf16[128,16,128]{0,2,1:T(8,128)(2,1)} %bitcast.293), calls=%async_computation.2 | async-start | bytes 1048576 | tf_op jit(solution)/shard_map/all_to_all | solution.py:225
  385.6 4.8 %copy-start.6 = (f32[128,32,64]{0,2,1:T(8,128)S(1)}, f32[128,32,64]{0,2,1:T(8,128)}, u32[]{:S(2)}) copy-start(f32[128,32,64]{0,2,1:T(8,128)} %copy-done.5) | copy-start | bytes 3145732
  385.6 4.8 %copy-start.8 = (bf16[4,128,4,128]{1,3,2,0:T(8,128)(2,1)S(1)}, bf16[4,128,4,128]{1,3,2,0:T(8,128)(2,1)}, u32[]{:S(2)}) copy-start(bf16[4,128,4,128]{1,3,2,0:T(8,128)(2,1)} %copy-done.7) | copy-start | bytes 1572868
  385.6 4.8 %copy-start.17 = (f32[128,128]{1,0:T(8,128)S(1)}, f32[128,128]{1,0:T(8,128)}, u32[]{:S(2)}) copy-start(f32[128,128]{1,0:T(8,128)} %copy-done.16) | copy-start | bytes 196612
  385.6 76.4 %all-to-all-start.3 = ((bf16[3,1,512,4,128]{4,3,0,1,2:T(4,128)(2,1)}), bf16[3,1,512,4,128]{4,3,0,1,2:T(4,128)(2,1)}, u32[]{:S(2)}, u32[]{:S(2)}) async-start(bf16[3,1,512,4,128]{4,3,0,1,2:T(4,128)(2,1)} %maximum_bitcast_fusion), calls=%async_computation.3 | async-start | bytes 3145728 | tf_op jit(solution)/shard_map/all_to_all | solution.py:230
  390.0 69.2 %all-reduce.7.cloned.1.call-start = ((), (), s32[]{:S(2)}) async-start(), calls=%async_computation.6 | async-start | bytes 131072 | tf_op jit(solution)/shard_map/psum | solution.py:217
  393.5 5.8 %copy-start.4 = (f32[128,32,64]{0,2,1:T(8,128)S(1)}, f32[128,32,64]{0,2,1:T(8,128)}, u32[]{:S(2)}) copy-start(f32[128,32,64]{0,2,1:T(8,128)} %copy-done.3) | copy-start | bytes 3145732
  393.5 6.9 %copy-start.2 = (f32[32,64,128]{2,1,0:T(8,128)S(1)}, f32[32,64,128]{2,1,0:T(8,128)}, u32[]{:S(2)}) copy-start(f32[32,64,128]{2,1,0:T(8,128)} %copy-done.1) | copy-start | bytes 3145732
  394.8 4.5 copy-start.27
  394.8 5.5 %copy-start.15 = (f32[128,32]{0,1:T(8,128)S(1)}, f32[128,32]{0,1:T(8,128)}, u32[]{:S(2)}) copy-start(f32[128,32]{0,1:T(8,128)} %get-tuple-element.477) | copy-start | bytes 49156
  394.8 5.6 %copy-start.25 = (f32[32]{0:T(128)S(1)}, f32[32]{0:T(128)}, u32[]{:S(2)}) copy-start(f32[32]{0:T(128)} %copy-done.24) | copy-start | bytes 388
  400.4 5.3 %copy-start.29 = (f32[32]{0:T(128)S(1)}, f32[32]{0:T(128)}, u32[]{:S(2)}) copy-start(f32[32]{0:T(128)} %param.21) | copy-start | bytes 388
Sparse Core Ops, SparseCore 0:
  82.8 79.8 all-gather.2
  181.3 79.2 all-gather.4
  405.8 18.8 all-reduce.6
where the time goes:
time: 477 us; the launch traced here: 473 us
  waiting for transfers between devices  211 us (44%)
  local copies, waits for them, and re-layouts  77.7 us (16%)
  blocking collectives  64.6 us (14%)
  matrix products  56.2 us (12%)
  other arithmetic  26.4 us (6%)
  starting transfers between devices  18.2 us (4%)
  between operations  18.2 us (4%)
    all_gather x1, waiting for transfers between devices, local(): lax.all_gather(carried_grad, 'context', axis=0, tiled=True)  79.4 us
    all_gather x1, waiting for transfers between devices, local(): lax.all_gather(local_state, 'context', axis=0, tiled=True)  67.6 us
    dynamic_update_slice x8, local copies, waits for them, and re-layouts, attend_back(): lax.map(per_head, (jnp.swapaxes(queries, 0, 1), jnp.swapaxes(key_rows, 0,...  59.2 us
    psum x1, blocking collectives, local(): lax.psum((loss_here, weight_grad, rate_first + rate_second), ('rollout',...  52.1 us
    all_to_all x1, waiting for transfers between devices, local(): lax.all_to_all(qkv, 'context', split_axis=3, concat_axis=2, tiled=True)  37 us
    all_to_all x1, waiting for transfers between devices, local(): lax.all_to_all(mixed_heads, 'context', split_axis=0, concat_axis=1, tiled...  13.5 us
    all_to_all x1, waiting for transfers between devices, local(): lax.all_to_all(attended_grad, 'context', split_axis=1, concat_axis=0, til...  13.4 us
    select_n x8, other arithmetic, advance(): return jnp.where(use_it, updated, running)  11.7 us
  transfers between devices with their start and end apart: 7, of which 5 were waited for; matrix products, arithmetic and copies ran while one was open for 4% of the time, Pallas kernels for 0%

commit v1 on v0

v1 whole, which is shorter than its diff:
```python
import functools
import math

import jax
import jax.numpy as jnp
from jax import lax
from jax.experimental import pallas as pl
from jax.experimental.pallas import tpu as pltpu
from jax.sharding import PartitionSpec as P

MASK_FILL = -1e30
NORM_EPS = 1e-05
HIGHEST = lax.Precision.HIGHEST
LOG2E = 1.4426950408889634
F32 = jnp.float32
BF16 = jnp.bfloat16
VMEM_LIMIT = 56 * 1024 * 1024
ANY = pl.BlockSpec(memory_space=pl.ANY)
VM = pl.BlockSpec(memory_space=pltpu.VMEM)
SM = pl.BlockSpec(memory_space=pltpu.SMEM)


def dot(a, b, precision=None):
    return jnp.dot(a, b, preferred_element_type=F32, precision=precision)


def dot_nt(a, b, precision=None):
    return lax.dot_general(a, b, (((1,), (1,)), ((), ())), preferred_element_type=F32, precision=precision)


def dot_tn(a, b, precision=None):
    return lax.dot_general(a, b, (((0,), (0,)), ((), ())), preferred_element_type=F32, precision=precision)


def iota(shape, dim):
    return lax.broadcasted_iota(jnp.int32, shape, dim)


def mat(cond):
    return jnp.where(cond, 1.0, 0.0).astype(F32)


class Sizes:
    def __init__(self, n, tokens, heads_local, head_dim, ssd_local, state):
        self.n, self.t, self.hl, self.hd, self.ns = n, tokens, heads_local, head_dim, state
        self.s = n * tokens
        self.a = heads_local // n
        self.groups = 2 if self.a % 2 == 0 else 1
        self.ag = self.a // self.groups
        self.h = ssd_local // n
        self.hg = self.h // self.groups
        self.mp = heads_local * head_dim // ssd_local
        self.fg = self.ag * head_dim
        self.f = self.a * head_dim
        self.r = -(-(self.h + 1) // 8) * 8
        self.rows = min(256, self.s)
        self.blocks = self.s // self.rows
        self.static = self.blocks <= 2

    def each_block(self, body):
        if self.static:
            for i in range(self.blocks):
                body(i)
        else:

            @pl.loop(0, self.blocks)
            def _(i):
                body(i)

    def upto(self, i):
        return (i + 1) * self.rows if self.static else self.s

    def onward(self, i):
        return i * self.rows if self.static else 0

    def block(self, i):
        return pl.ds(i * self.rows if self.static else pl.multiple_of(i * self.rows, self.rows), self.rows)


def call(kernel, name, out_shape, in_specs, out_specs, scratch, args, flops=0, nbytes=0):
    return pl.pallas_call(
        kernel,
        name=name,
        out_shape=out_shape,
        in_specs=in_specs,
        out_specs=out_specs,
        scratch_shapes=scratch,
        compiler_params=pltpu.CompilerParams(vmem_limit_bytes=VMEM_LIMIT),
        cost_estimate=pl.CostEstimate(flops=flops, bytes_accessed=nbytes, transcendentals=0),
    )(*args)


def prep_kernel(z, info, qkv, *refs):
    outs, (held, sems) = refs[: z.n * z.groups], refs[z.n * z.groups :]
    for c in range(3):
        held[c] = jnp.swapaxes(qkv[c, 0], 0, 1)
    me = info[0]
    copies = []
    for g in range(z.groups):
        for s in range(z.n):
            first = lax.rem(me + s, z.n) * z.a + g * z.ag
            copies.append(
                pltpu.make_async_copy(
                    held.at[:, pl.ds(first, z.ag)], outs[g * z.n + s], sems.at[g, s]
                )
            )
            copies[-1].start()
    for one in copies:
        one.wait()


def finish_kernel(z, info, *refs):
    count = z.n * z.groups
    ins, out, (held, sems) = refs[:count], refs[count], refs[count + 1 :]
    me = info[0]
    copies = []
    for g in range(z.groups):
        for s in range(z.n):
            first = lax.rem(me + z.n - s, z.n) * z.a + g * z.ag
            copies.append(
                pltpu.make_async_copy(
                    ins[g * z.n + s], held.at[:, pl.ds(first, z.ag)], sems.at[g, s]
                )
            )
            copies[-1].start()
    for one in copies:
        one.wait()
    for c in range(3):
        out[c, 0] = jnp.swapaxes(held[c], 0, 1)


def gather_blocks(z, info, ins, target, sems, slot, rows_dim):
    me = info[0]
    copies = []
    for s in range(z.n):
        source = lax.rem(me + z.n - s, z.n)
        if rows_dim is None:
            place = target.at[source]
        else:
            place = target.at[:, :, pl.ds(pl.multiple_of(source * z.t, z.t), z.t)]
        one = pltpu.make_async_copy(ins[s], place, sems.at[slot, s])
        one.start()
        copies.append(one)
    return copies


def decay_terms(z, dt_rows, rates, g):
    causal = mat(iota((z.t, z.t), 0) >= iota((z.t, z.t), 1))
    spread = mat(iota((z.r, z.fg), 0) == g * z.hg + iota((z.r, z.fg), 1) // z.mp)
    cum = dot(dot_nt(causal, dt_rows, HIGHEST), spread, HIGHEST) * (-rates)
    mid = 0.5 * cum[z.t - 1 : z.t]
    return jnp.exp(cum - mid), jnp.exp(mid - cum), jnp.exp(mid)


def forward_kernel(z, g, info, *refs):
    n = z.n
    qkvs, bcs, pays, wr = refs[:n], refs[n : 2 * n], refs[2 * n : 3 * n], refs[3 * n]
    prob, attended, normed, slope, states, value = refs[3 * n + 1 : 3 * n + 7]
    held, bc, pay, state, sems = refs[3 * n + 7 :]
    first = gather_blocks(z, info, qkvs, held, sems, 0, 2)
    later = gather_blocks(z, info, bcs, bc, sems, 1, None)
    later += gather_blocks(z, info, pays, pay, sems, 2, None)
    for one in first:
        one.wait()
    factor = LOG2E / math.sqrt(z.hd)

    def attend(i):
        width = z.upto(i)
        rows = z.block(i)
        keep = iota((z.rows, width), 1) <= i * z.rows + iota((z.rows, width), 0)
        for a in range(z.ag):
            scores = dot_nt(held[0, a, rows, :], held[1, a, :width, :])
            scores = jnp.where(keep, scores, MASK_FILL)
            weights = jnp.exp2((scores - jnp.max(scores, axis=1, keepdims=True)) * factor)
            weights = weights * (1.0 / jnp.sum(weights, axis=1, keepdims=True))
            weights = weights.astype(BF16)
            prob[a, rows, :width] = weights
            attended[rows, a * z.hd : (a + 1) * z.hd] = dot(weights, held[2, a, :width, :]).astype(BF16)

    z.each_block(attend)
    for one in later:
        one.wait()
    weight, rates = wr[0:1], wr[1:2]
    causal = iota((z.t, z.t), 0) >= iota((z.t, z.t), 1)
    same_head = mat(iota((z.hd, z.hd), 0) // z.mp == iota((z.hd, z.hd), 1) // z.mp).astype(BF16)
    state[...] = jnp.zeros_like(state)

    def chunk(c):
        rows = pl.ds(c * z.t if isinstance(c, int) else pl.multiple_of(c * z.t, z.t), z.t)
        up, down, mid = decay_terms(z, pay[c], rates, g)
        b, cp = bc[c, 0], bc[c, 1]
        inner = jnp.where(causal, dot_nt(cp, b), 0.0).astype(BF16)
        x = (down * attended[rows, :].astype(F32)).astype(BF16)
        carried = (mid * state[...]).astype(BF16)
        states[c] = carried
        y = up * (dot(inner, x) + dot(cp, carried))
        state[...] = mid * (mid * state[...] + dot_tn(b, x))
        total = jnp.zeros((z.t, z.hd), F32)
        for a in range(z.ag):
            lanes = slice(a * z.hd, (a + 1) * z.hd)
            ya = y[:, lanes]
            scale = lax.rsqrt(dot((ya * ya).astype(BF16), same_head) * (1.0 / z.mp) + NORM_EPS)
            unit = ya * scale
            term = unit * weight[:, lanes]
            total = total + term
            high = term.astype(BF16)
            mean = (dot(high, same_head) + dot((term - high.astype(F32)).astype(BF16), same_head)) * (1.0 / z.mp)
            normed[rows, lanes] = unit.astype(BF16)
            slope[rows, lanes] = scale * (weight[:, lanes] - unit * mean)
        row = dot_nt(jnp.ones((8, z.hd), F32), total, HIGHEST)
        value[:, rows] = row[0:1]

    if z.static:
        for c in range(n):
            chunk(c)
    else:
        pl.loop(0, n)(chunk)


def forward(z, g, info, qkvs, bcs, pays, wr):
    shape = jax.ShapeDtypeStruct
    outs = (
        shape((z.ag, z.s, z.s), BF16),
        shape((z.s, z.fg), BF16),
        shape((z.s, z.fg), BF16),
        shape((z.s, z.fg), F32),
        shape((z.n, z.ns, z.fg), BF16),
        shape((1, z.s), F32),
    )
    scratch = [
        pltpu.VMEM((3, z.ag, z.s, z.hd), BF16),
        pltpu.VMEM((z.n, 2, z.t, z.ns), BF16),
        pltpu.VMEM((z.n, z.r, z.t), F32),
        pltpu.VMEM((z.ns, z.fg), F32),
        pltpu.SemaphoreType.DMA((3, z.n)),
    ]
    return call(
        functools.partial(forward_kernel, z, g),
        "forward_%d" % g,
        outs,
        [SM] + [ANY] * (3 * z.n) + [VM],
        [VM] * 6,
        scratch,
        (info, *qkvs, *bcs, *pays, wr),
        flops=z.ag * z.s * z.s * z.hd * 4,
        nbytes=z.ag * z.s * z.s * 8,
    )


def ssd_back_kernel(z, info, *refs):
    n, groups = z.n, z.groups
    values, refs = refs[:n], refs[n:]
    bcs, pays, refs = refs[:n], refs[n : 2 * n], refs[2 * n :]
    wr, rate_rows, refs = refs[0], refs[1], refs[2:]
    saved, refs = [refs[4 * g : 4 * g + 4] for g in range(groups)], refs[4 * groups :]
    grads, refs = refs[:groups], refs[groups:]
    keep_out, give_out, step_out, small_out = refs[:4]
    bc, pay, dstates, sems = refs[4], refs[5], refs[6 : 6 + groups], refs[6 + groups]
    copies = gather_blocks(z, info, bcs, bc, sems, 0, None)
    copies += gather_blocks(z, info, pays, pay, sems, 1, None)
    for one in copies:
        one.wait()
    head, length = info[1], info[2]
    value = values[0][...]
    for s in range(1, n):
        value = value + values[s][...]
    t = z.t
    row_id, col_id = iota((t, t), 0), iota((t, t), 1)
    causal = row_id >= col_id
    after = mat(col_id >= row_id)
    before = mat(col_id < row_id)
    for d in dstates:
        d[...] = jnp.zeros_like(d)
    small_out[...] = jnp.zeros_like(small_out)
    features = z.f // z.hd

    def chunk(step):
        c = n - 1 - step
        if isinstance(c, int):
            rows = pl.ds(c * t, t)
            value_row = value[:, c * t : (c + 1) * t]
        else:
            rows = pl.ds(pl.multiple_of(c * t, t), t)
            value_row = jnp.zeros((1, t), F32)
            for j in range(n):
                value_row = jnp.where(c == j, value[:, j * t : (j + 1) * t], value_row)
        dt_rows = pay[c]
        valid = c * t + iota((1, t), 1) < length
        error = jnp.where(valid, value_row - dt_rows[z.h : z.h + 1], 0.0)
        small_out[features + 1 : features + 2, :] += 0.5 * error * error
        error8 = jnp.broadcast_to(error, (8, t))
        error_col = jnp.transpose(jnp.broadcast_to(error, (t, t)))
        b, cp = bc[c, 0], bc[c, 1]
        inner = jnp.where(causal, dot_nt(cp, b), 0.0)
        inner_low = inner.astype(BF16)
        w_sum = jnp.zeros((t, t), F32)
        grad_c = jnp.zeros((t, z.ns), F32)
        grad_b = jnp.zeros((t, z.ns), F32)
        gain = jnp.zeros((t, t), F32)
        for g in range(groups):
            attended, normed, slope, states = saved[g]
            up, down, mid = decay_terms(z, dt_rows, wr[1:2, g * z.fg : (g + 1) * z.fg], g)
            per_head = mat(iota((z.fg, t), 1) == g * z.hg + iota((z.fg, t), 0) // z.mp)
            unit = normed[rows, :].astype(F32)
            weight_grad = dot(error8, unit, HIGHEST)
            for a in range(z.ag):
                small_out[g * z.ag + a : g * z.ag + a + 1, :] += weight_grad[0:1, a * z.hd : (a + 1) * z.hd]
            x = (down * attended[rows, :].astype(F32)).astype(BF16)
            error_wide = jnp.concatenate([error_col] * z.ag, axis=1)
            d = (up * (error_wide * slope[rows, :])).astype(BF16)
            state_in = states[c]
            dstate = mid * dstates[g][...]
            dstate_low = dstate.astype(BF16)
            local = dot_tn(inner_low, d)
            outer = dot(b, dstate_low)
            carried = dot(cp, state_in)
            grads[g][rows, :] = (down * (local + outer)).astype(BF16)
            dstates[g][...] = mid * (dstate + dot_tn(cp, d))
            grad_c += dot_nt(d, state_in)
            grad_b += dot_nt(x, dstate_low)
            down_sum = dot(d.astype(F32) * carried, per_head, HIGHEST)
            up_sum = dot(x.astype(F32) * outer, per_head, HIGHEST)
            through = jnp.sum(dstate * state_in.astype(F32), axis=0, keepdims=True)
            through = dot(jnp.broadcast_to(through, (8, z.fg)), per_head, HIGHEST)
            gain += dot(after, down_sum, HIGHEST) + dot(before, up_sum, HIGHEST) + through[0:1]
            parts = []
            for k in range(z.hg):
                lanes = slice(k * z.mp // z.hd * z.hd, (k * z.mp // z.hd + 1) * z.hd)
                mine = iota((t, z.hd), 1) // z.mp == k % (z.hd // z.mp)
                d_head = jnp.where(mine, d[:, lanes], jnp.zeros((), BF16))
                w = jnp.where(causal, dot_nt(d_head, x[:, lanes]), 0.0)
                w_sum += w
                parts.append((w * inner).astype(BF16))
            straddle = dot(after.astype(BF16), jnp.concatenate(parts, axis=1))
            for k in range(z.hg):
                strict = jnp.where(col_id < row_id, straddle[:, k * t : (k + 1) * t], 0.0)
                gain += jnp.where(col_id == g * z.hg + k, jnp.sum(strict, axis=1, keepdims=True), 0.0)
        w_low = w_sum.astype(BF16)
        grad_c += dot(w_low, b)
        grad_b += dot_tn(w_low, cp)
        keep_out[c] = jnp.where(head == 0, grad_b, grad_c)
        give_out[c] = jnp.where(head == 0, grad_c, grad_b).astype(BF16)
        gain_rows = jnp.transpose(gain)[: z.r]
        step_out[c] = -rate_rows[...] * gain_rows
        rate_part = jnp.sum(dt_rows * gain_rows, axis=1, keepdims=True)
        lane = iota((z.r, t), 1) == iota((z.r, t), 0)
        small_out[features : features + 1, :] -= jnp.sum(jnp.where(lane, rate_part, 0.0), axis=0, keepdims=True)

    if z.static:
        for step in range(n):
            chunk(step)
    else:
        pl.loop(0, n)(chunk)


def ssd_back(z, info, values, bcs, pays, wr, rate_rows, saved):
    shape = jax.ShapeDtypeStruct
    small_rows = -(-(z.f // z.hd + 2) // 8) * 8
    outs = (
        *[shape((z.s, z.fg), BF16)] * z.groups,
        shape((z.n, z.t, z.ns), F32),
        shape((z.n, z.t, z.ns), BF16),
        shape((z.n, z.r, z.t), F32),
        shape((small_rows, z.t), F32),
    )
    scratch = [
        pltpu.VMEM((z.n, 2, z.t, z.ns), BF16),
        pltpu.VMEM((z.n, z.r, z.t), F32),
        *[pltpu.VMEM((z.ns, z.fg), F32)] * z.groups,
        pltpu.SemaphoreType.DMA((2, z.n)),
    ]
    flat = [x for group in saved for x in group]
    return call(
        functools.partial(ssd_back_kernel, z),
        "ssd_back",
        outs,
        [SM] + [VM] * z.n + [ANY] * (2 * z.n) + [VM] * (2 + len(flat)),
        [VM] * len(outs),
        scratch,
        (info, *values, *bcs, *pays, wr, rate_rows, *flat),
        flops=z.s * z.f * z.ns * 20,
        nbytes=z.s * z.f * 32,
    )


def attend_back_kernel(z, info, *refs):
    n = z.n
    qkvs, prob, grad = refs[:n], refs[n], refs[n + 1]
    outs, (held, result, dscore, sems, out_sems) = refs[n + 2 : 2 * n + 2], refs[2 * n + 2 :]
    for one in gather_blocks(z, info, qkvs, held, sems, 0, 2):
        one.wait()
    factor = 1.0 / math.sqrt(z.hd)
    for a in range(z.ag):
        lanes = slice(a * z.hd, (a + 1) * z.hd)

        def by_query(i):
            width, rows = z.upto(i), z.block(i)
            p = prob[a, rows, :width].astype(F32)
            dp = dot_nt(grad[rows, lanes], held[2, a, :width, :])
            product = p * dp
            ds = (product - p * jnp.sum(product, axis=1, keepdims=True)).astype(BF16)
            dscore[rows, :width] = ds
            result[0, a, rows, :] = (dot(ds, held[1, a, :width, :]) * factor).astype(BF16)

        z.each_block(by_query)

        def by_key(j):
            first, cols = z.onward(j), z.block(j)
            result[1, a, cols, :] = (dot_tn(dscore[first:, cols], held[0, a, first:, :]) * factor).astype(BF16)
            result[2, a, cols, :] = dot_tn(prob[a, first:, cols], grad[first:, lanes]).astype(BF16)

        z.each_block(by_key)
    me = info[0]
    copies = []
    for s in range(n):
        place = pl.ds(pl.multiple_of(lax.rem(me + s, n) * z.t, z.t), z.t)
        copies.append(pltpu.make_async_copy(result.at[:, :, place], outs[s], out_sems.at[s]))
        copies[-1].start()
    for one in copies:
        one.wait()


def attend_back(z, g, info, qkvs, prob, grad):
    shape = jax.ShapeDtypeStruct
    scratch = [
        pltpu.VMEM((3, z.ag, z.s, z.hd), BF16),
        pltpu.VMEM((3, z.ag, z.s, z.hd), BF16),
        pltpu.VMEM((z.s, z.s), BF16),
        pltpu.SemaphoreType.DMA((1, z.n)),
        pltpu.SemaphoreType.DMA((z.n,)),
    ]
    return call(
        functools.partial(attend_back_kernel, z),
        "attend_back_%d" % g,
        [shape((3, z.ag, z.t, z.hd), BF16)] * z.n,
        [SM] + [ANY] * z.n + [VM] * 2,
        [ANY] * z.n,
        scratch,
        (info, *qkvs, prob, grad),
        flops=z.ag * z.s * z.s * z.hd * 8,
        nbytes=z.ag * z.s * z.s * 8,
    )


def shift(x, axis, size, step):
    return lax.ppermute(x, axis, [(i, (i + step) % size) for i in range(size)])


def spread(parts, axis):
    return [parts[0]] + [shift(x, axis, len(parts), s) for s, x in enumerate(parts) if s]


def total_over(x, axis):
    return sum(spread([x] * lax.axis_size(axis), axis))


def local(qkv, ssd_b, ssd_c, step_size, decay_rate, value_weight, returns, step_labels, lengths):
    n = lax.axis_size("context")
    me = lax.axis_index("context")
    head = lax.axis_index("head")
    z = Sizes(n, qkv.shape[2], qkv.shape[3], qkv.shape[4], step_size.shape[2], ssd_b.shape[2])
    my_length = lax.dynamic_index_in_dim(lengths, lax.axis_index("rollout"), 0, keepdims=False)
    info = jnp.stack([me, head, my_length, me]).astype(jnp.int32)
    shape = jax.ShapeDtypeStruct

    sends = call(
        functools.partial(prep_kernel, z),
        "prep",
        [shape((3, z.ag, z.t, z.hd), BF16)] * (n * z.groups),
        [SM, VM],
        [ANY] * (n * z.groups),
        [pltpu.VMEM((3, z.hl, z.t, z.hd), BF16), pltpu.SemaphoreType.DMA((z.groups, n))],
        (info, qkv),
        nbytes=qkv.size * 4,
    )
    both = jnp.stack([ssd_b[0], ssd_c[0]])
    bcs = spread([both] * n, "context")
    table = returns[0]
    onehot = (step_labels[0][:, None] == jnp.arange(table.shape[0], dtype=jnp.int32)[None, :]).astype(F32)
    target = jnp.sum(onehot * table[None, :], axis=1)
    steps = step_size[0].T.reshape(n, z.h, z.t)
    pay = jnp.concatenate(
        [
            steps,
            jnp.broadcast_to(target[None, None, :], (n, 1, z.t)),
            jnp.zeros((n, z.r - z.h - 1, z.t), F32),
        ],
        axis=1,
    )
    pays = spread(
        [lax.dynamic_index_in_dim(pay, (me + s) % n, 0, keepdims=False) for s in range(n)], "context"
    )
    rates = lax.dynamic_slice_in_dim(decay_rate, me * z.h, z.h)
    weights = lax.dynamic_slice_in_dim(value_weight, me * z.f, z.f).astype(F32)
    wr = jnp.stack([weights, jnp.repeat(rates, z.mp)])
    rate_rows = jnp.broadcast_to(jnp.pad(rates, (0, z.r - z.h))[:, None], (z.r, z.t))

    arrived = [spread(sends[g * n : (g + 1) * n], "context") for g in range(z.groups)]
    probs, saved, value = [], [], None
    for g in range(z.groups):
        prob, attended, normed, slope, states, part = forward(
            z, g, info, arrived[g], bcs, pays, wr[:, g * z.fg : (g + 1) * z.fg]
        )
        probs.append(prob)
        saved.append((attended, normed, slope, states))
        value = part if value is None else value + part
    value = total_over(value, "head")
    values = spread([value] * n, "context")
    *grads, keep, give, steps_out, small = ssd_back(z, info, values, bcs, pays, wr, rate_rows, saved)

    mine = (keep + total_over_other(give)).astype(BF16)
    proj = spread(
        [lax.dynamic_index_in_dim(mine, (me + s) % n, 0, keepdims=False) for s in range(n)], "context"
    )
    step_parts = spread(
        [lax.dynamic_index_in_dim(steps_out, (me + s) % n, 0, keepdims=False) for s in range(n)], "context"
    )
    small_parts = spread([small] * n, "context")

    finals = []
    for g in range(z.groups):
        finals += spread(attend_back(z, g, info, arrived[g], probs[g], grads[g]), "context")
    qkv_grad = call(
        functools.partial(finish_kernel, z),
        "finish",
        shape((3, 1, z.t, z.hl, z.hd), BF16),
        [SM] + [ANY] * (n * z.groups),
        VM,
        [pltpu.VMEM((3, z.hl, z.t, z.hd), BF16), pltpu.SemaphoreType.DMA((z.groups, n))],
        (info, *finals),
        nbytes=qkv.size * 4,
    )
    proj_sum = sum(x.astype(F32) for x in proj)
    other = shift(proj_sum, "head", 2, 1)
    b_grad = jnp.where(head == 0, proj_sum, other)
    c_grad = jnp.where(head == 0, other, proj_sum)

    order = (me - jnp.arange(n)) % n
    step_grad = jnp.stack([x[: z.h] for x in step_parts])[order].reshape(n * z.h, z.t).T
    gathered = total_over(jnp.stack(small_parts), "rollout")
    features = z.f // z.hd
    loss = jnp.sum(gathered[0, features + 1]) / jnp.sum(lengths).astype(F32)
    gathered = gathered[order]
    weight_grad = gathered[:, :features].reshape(-1)
    rate_grad = gathered[:, features, : z.h].reshape(-1)
    return loss, qkv_grad, b_grad[None], c_grad[None], step_grad[None], rate_grad, weight_grad


def total_over_other(x):
    return shift(x, "head", 2, 1).astype(F32)


def solution(mesh):
    in_specs = (
        P(None, "rollout", "context", "head", None),
        P("rollout", "context", None),
        P("rollout", "context", None),
        P("rollout", "context", "head"),
        P("head"),
        P("head"),
        P("rollout", None),
        P("rollout", "context"),
        P(),
    )
    out_specs = (
        P(),
        P(None, "rollout", "context", "head", None),
        P("rollout", "context", None),
        P("rollout", "context", None),
        P("rollout", "context", "head"),
        P("head"),
        P("head"),
    )
    return jax.shard_map(local, mesh=mesh, in_specs=in_specs, out_specs=out_specs, check_vma=False)
```

time: 477 us -> 164 us (0.34)
  waiting for transfers between devices: 211 us -> 31.2 us
  local copies, waits for them, and re-layouts: 77.7 us -> 9.33 us
  blocking collectives: 64.6 us -> 0 us
  matrix products: 56.2 us -> 0 us
  Pallas kernels: 0 us -> 48.1 us
  starting transfers between devices: 18.2 us -> 63.2 us
  other arithmetic: 26.4 us -> 7.43 us
  between operations: 18.2 us -> 3.61 us
    all_gather x2 -> x0, waiting for transfers between devices: 147 us -> none  [the longest x1 79.4 us: local(): lax.all_gather(carried_grad, 'context', axis=0, tiled=True)]
    all_to_all x4 -> x0, waiting for transfers between devices: 63.9 us -> none  [the longest x1 37 us: local(): lax.all_to_all(qkv, 'context', split_axis=3, concat_axis=2, tiled=True)]
    ppermute x0 -> x36, starting transfers between devices: none -> 63.2 us  [shift(): return lax.ppermute(x, axis, [(i, (i + step) % size) for i in range(size)])]
    dynamic_update_slice x8 -> x0, local copies, waits for them, and re-layouts: 59.2 us -> none  [attend_back(): lax.map(per_head, (jnp.swapaxes(queries, 0, 1), jnp.swapaxes(key_rows, 0,...]
    dot_general x43 -> x0, matrix products: 56.2 us -> none  [the longest x8 9.79 us: block_probs(): lax.dot_general(query_block, key_rows, (((1,), (1,)), ((), ())), preferre...]
    psum x2 -> x0, blocking collectives: 54.7 us -> none  [the longest x1 52.1 us: local(): lax.psum((loss_here, weight_grad, rate_first + rate_second), ('rollout',...]
    pallas_call x0 -> x7, Pallas kernels: none -> 48.1 us  [call(): pl.pallas_call(kernel, name=name, out_shape=out_shape, in_specs=in_specs,...]
    ppermute x0 -> x36, waiting for transfers between devices: none -> 31.2 us  [shift(): return lax.ppermute(x, axis, [(i, (i + step) % size) for i in range(size)])]
  transfers between devices with their start and end apart: 7 -> 36, of which waited for: 5 -> 9; matrix products, arithmetic and copies ran while one was open for 4% -> 6% of each run, Pallas kernels for 0% -> 16%
where the time goes in v1:
time: 164 us; the launch traced here: 163 us
  starting transfers between devices  63.2 us (39%)
  Pallas kernels  48.1 us (29%)
  waiting for transfers between devices  31.2 us (19%)
  local copies, waits for them, and re-layouts  9.33 us (6%)
  other arithmetic  7.43 us (5%)
  between operations  3.61 us (2%)
    ppermute x36, starting transfers between devices, shift(): return lax.ppermute(x, axis, [(i, (i + step) % size) for i in range(size)])  63.2 us
    pallas_call x7, Pallas kernels, call(): pl.pallas_call(kernel, name=name, out_shape=out_shape, in_specs=in_specs,...  48.1 us
    ppermute x36, waiting for transfers between devices, shift(): return lax.ppermute(x, axis, [(i, (i + step) % size) for i in range(size)])  31.2 us
  transfers between devices with their start and end apart: 36, of which 9 were waited for; matrix products, arithmetic and copies ran while one was open for 6% of the time, Pallas kernels for 16%

profile of v1, /device:TPU:0, one launch (start us, length us, event | category | flops | bytes accessed | tf_op | source)
XLA Modules:
  0.0 162.8 jit_solution(16111239062150872591)
XLA Ops:
  0.7 0.8 select_reduce_fusion
  1.6 0.8 maximum_maximum_fusion
  3.0 3.0 %collective-permute-start.6 = (f32[16,128]{1,0:T(8,128)S(1)}, f32[16,128]{1,0:T(8,128)S(1)}, u32[]{:S(2)}, u32[]{:S(2)}) collective-permute-start(f32[16,128]{1,0:T(8,128)S(1)} %get-tuple-element.85), channel_id=1, source_target_pairs={{0,2},{2,4},{4,6},{6,0},{1,3},{3,5},{5,7},{7,1},{8,10},{10,12},{12... | collective-permute-start | bytes 24584 | tf_op jit(solution)/shard_map/ppermute | solution.py:446
  6.0 2.6 %collective-permute-start.7 = (f32[16,128]{1,0:T(8,128)S(1)}, f32[16,128]{1,0:T(8,128)S(1)}, u32[]{:S(2)}, u32[]{:S(2)}) collective-permute-start(f32[16,128]{1,0:T(8,128)S(1)} %get-tuple-element.84), channel_id=1, source_target_pairs={{0,4},{2,6},{4,0},{6,2},{1,5},{3,7},{5,1},{7,3},{8,12},{10,14},{12... | collective-permute-start | bytes 24584 | tf_op jit(solution)/shard_map/ppermute | solution.py:446
  8.6 1.2 dynamic_slice.48
  9.8 1.3 pad_add_fusion.info
  11.1 3.1 %prep.1 = (bf16[3,2,128,128]{3,2,1,0:T(8,128)(2,1)}, bf16[3,2,128,128]{3,2,1,0:T(8,128)(2,1)}, bf16[3,2,128,128]{3,2,1,0:T(8,128)(2,1)}, bf16[3,2,128,128]{3,2,1...) custom-call(s32[4]{0:T(128)} %pad_add_fusion.info, ...), custom_call_target="tpu_custom_call" | custom-call | bytes 3145728 | tf_op jit(solution)/shard_map/prep/pallas_call | solution.py:81
  14.7 1.6 %collective-permute-start.3 = (bf16[2,128,128]{2,1,0:T(8,128)(2,1)S(1)}, bf16[2,128,128]{2,1,0:T(8,128)(2,1)S(1)}, u32[]{:S(2)}, u32[]{:S(2)}) collective-permute-start(bf16[2,128,128]{2,1,0:T(8,128)(2,1)S(1)} %constant_dynamic-update-slice_fusion.refs_4_), channel_id=1, source_target_pairs={{0,2},{2,4},{4,6},{6,0},{1,3},{3,5},{5,7},{7,1},{8,10},{10,12},{12... | collective-permute-start | bytes 196616 | tf_op jit(solution)/shard_map/ppermute | solution.py:446
  16.3 1.1 collective-permute-start.4
  17.4 2.8 %collective-permute-start.5 = (bf16[2,128,128]{2,1,0:T(8,128)(2,1)S(1)}, bf16[2,128,128]{2,1,0:T(8,128)(2,1)S(1)}, u32[]{:S(2)}, u32[]{:S(2)}) collective-permute-start(bf16[2,128,128]{2,1,0:T(8,128)(2,1)S(1)} %constant_dynamic-update-slice_fusion.refs_4_), channel_id=1, source_target_pairs={{0,6},{2,0},{4,2},{6,4},{1,7},{3,1},{5,3},{7,5},{8,14},{10,8},{12,... | collective-permute-start | bytes 196616 | tf_op jit(solution)/shard_map/ppermute | solution.py:446
  20.7 0.8 dynamic-slice_convert_fusion
  21.7 2.5 %collective-permute-done.8.refs_11_ = f32[16,128]{1,0:T(8,128)S(1)} collective-permute-done((f32[16,128]{1,0:T(8,128)S(1)}, f32[16,128]{1,0:T(8,128)S(1)}, u32[]{:S(2)}, u32[]{:S(2)}) %collective-permute-start.8) | collective-permute-done | bytes 8224 | tf_op jit(solution)/shard_map/ppermute | solution.py:446
  24.3 2.9 %collective-permute-start.11 = (bf16[3,2,128,128]{3,2,1,0:T(8,128)(2,1)}, bf16[3,2,128,128]{3,2,1,0:T(8,128)(2,1)S(1)}, u32[]{:S(2)}, u32[]{:S(2)}) collective-permute-start(bf16[3,2,128,128]{3,2,1,0:T(8,128)(2,1)} %get-tuple-element.49), channel_id=1, source_target_pairs={{0,6},{2,0},{4,2},{6,4},{1,7},{3,1},{5,3},{7,5},{8,14},{10,8},{12,... | collective-permute-start | bytes 589832 | tf_op jit(solution)/shard_map/ppermute | solution.py:446
  27.2 5.6 %collective-permute-start.9 = (bf16[3,2,128,128]{3,2,1,0:T(8,128)(2,1)}, bf16[3,2,128,128]{3,2,1,0:T(8,128)(2,1)S(1)}, u32[]{:S(2)}, u32[]{:S(2)}) collective-permute-start(bf16[3,2,128,128]{3,2,1,0:T(8,128)(2,1)} %get-tuple-element.47), channel_id=1, source_target_pairs={{0,2},{2,4},{4,6},{6,0},{1,3},{3,5},{5,7},{7,1},{8,10},{10,12},{12... | collective-permute-start | bytes 589832 | tf_op jit(solution)/shard_map/ppermute | solution.py:446
  32.8 2.5 %collective-permute-start = (bf16[3,2,128,128]{3,2,1,0:T(8,128)(2,1)}, bf16[3,2,128,128]{3,2,1,0:T(8,128)(2,1)S(1)}, u32[]{:S(2)}, u32[]{:S(2)}) collective-permute-start(bf16[3,2,128,128]{3,2,1,0:T(8,128)(2,1)} %get-tuple-element.42), channel_id=1, source_target_pairs={{0,2},{2,4},{4,6},{6,0},{1,3},{3,5},{5,7},{7,1},{8,10},{10,12},{12... | collective-permute-start | bytes 589832 | tf_op jit(solution)/shard_map/ppermute | solution.py:446
  35.3 2.2 %collective-permute-start.1 = (bf16[3,2,128,128]{3,2,1,0:T(8,128)(2,1)}, bf16[3,2,128,128]{3,2,1,0:T(8,128)(2,1)S(1)}, u32[]{:S(2)}, u32[]{:S(2)}) collective-permute-start(bf16[3,2,128,128]{3,2,1,0:T(8,128)(2,1)} %get-tuple-element.43), channel_id=1, source_target_pairs={{0,4},{2,6},{4,0},{6,2},{1,5},{3,7},{5,1},{7,3},{8,12},{10,14},{12... | collective-permute-start | bytes 589832 | tf_op jit(solution)/shard_map/ppermute | solution.py:446
  39.0 3.6 %collective-permute-done.9.refs_1_ = bf16[3,2,128,128]{3,2,1,0:T(8,128)(2,1)S(1)} collective-permute-done((bf16[3,2,128,128]{3,2,1,0:T(8,128)(2,1)}, bf16[3,2,128,128]{3,2,1,0:T(8,128)(2,1)S(1)}, u32[]{:S(2)}, u32[]{:S(2)}) %collective-permute-start.9) | collective-permute-done | bytes 196640 | tf_op jit(solution)/shard_map/ppermute | solution.py:446
  43.3 8.6 %forward_1.1 = (bf16[2,512,512]{2,1,0:T(8,128)(2,1)}, bf16[512,256]{1,0:T(8,128)(2,1)}, bf16[512,256]{1,0:T(8,128)(2,1)}, f32[512,256]{1,0:T(8,128)}, bf16[4,128,256]{2,1,0:T(8,128)(2,1)}, /*index=5*/f32[1,512]{1,0:T(1,128)}) custom-call(s32[4]{0:T(128)} %pad_add_fusion.info, bf16[3,2,128,128]{3,2,1,0:T(8,128)(2,1)} %get-tuple-element.46.refs_0_, ...), custom_call_target="tpu_custom_call" | custom-call | flops 268435456 | bytes 4194304 | tf_op jit(solution)/shard_map/forward_1/pallas_call | solution.py:81
  51.9 4.0 %collective-permute-done.1.refs_2_ = bf16[3,2,128,128]{3,2,1,0:T(8,128)(2,1)S(1)} collective-permute-done((bf16[3,2,128,128]{3,2,1,0:T(8,128)(2,1)}, bf16[3,2,128,128]{3,2,1,0:T(8,128)(2,1)S(1)}, u32[]{:S(2)}, u32[]{:S(2)}) %collective-permute-start.1) | collective-permute-done | bytes 196640 | tf_op jit(solution)/shard_map/ppermute | solution.py:446
  56.7 8.6 %forward_0.1 = (bf16[2,512,512]{2,1,0:T(8,128)(2,1)}, bf16[512,256]{1,0:T(8,128)(2,1)}, bf16[512,256]{1,0:T(8,128)(2,1)}, f32[512,256]{1,0:T(8,128)}, bf16[4,128,256]{2,1,0:T(8,128)(2,1)}, /*index=5*/f32[1,512]{1,0:T(1,128)}) custom-call(s32[4]{0:T(128)} %pad_add_fusion.info, bf16[3,2,128,128]{3,2,1,0:T(8,128)(2,1)} %get-tuple-element.41.refs_0_, ...), custom_call_target="tpu_custom_call" | custom-call | flops 268435456 | bytes 4194304 | tf_op jit(solution)/shard_map/forward_0/pallas_call | solution.py:81
  65.4 0.7 add.135
  66.1 1.1 collective-permute-done.12
  67.2 5.8 %collective-permute-start.13 = (f32[1,512]{1,0:T(1,128)S(1)}, f32[1,512]{1,0:T(1,128)S(1)}, u32[]{:S(2)}, u32[]{:S(2)}) collective-permute-start(f32[1,512]{1,0:T(1,128)S(1)} %add.136.refs_0_), channel_id=1, source_target_pairs={{0,2},{2,4},{4,6},{6,0},{1,3},{3,5},{5,7},{7,1},{8,10},{10,12},{12... | collective-permute-start | bytes 6152 | tf_op jit(solution)/shard_map/ppermute | solution.py:446
  73.0 2.4 %collective-permute-start.15 = (f32[1,512]{1,0:T(1,128)S(1)}, f32[1,512]{1,0:T(1,128)S(1)}, u32[]{:S(2)}, u32[]{:S(2)}) collective-permute-start(f32[1,512]{1,0:T(1,128)S(1)} %add.136.refs_0_), channel_id=1, source_target_pairs={{0,6},{2,0},{4,2},{6,4},{1,7},{3,1},{5,3},{7,5},{8,14},{10,8},{12,... | collective-permute-start | bytes 6152 | tf_op jit(solution)/shard_map/ppermute | solution.py:446
  76.8 0.7 collective-permute-done.14.refs_2_
  78.2 13.3 %ssd_back.1 = (bf16[512,256]{1,0:T(8,128)(2,1)}, bf16[512,256]{1,0:T(8,128)(2,1)}, f32[4,128,128]{2,1,0:T(8,128)}, bf16[4,128,128]{2,1,0:T(8,128)(2,1)}, f32[4,16,128]{2,1,0:T(8,128)}, /*index=5*/f32[8,128]{1,0:T(8,128)}) custom-call(s32[4]{0:T(128)} %pad_add_fusion.info, f32[1,512]{1,0:T(1,128)} %copy-done.23, f32[1,512]{1,0:T(1,128)} %copy-done.24, ...), custom_call_target="tpu_custom_call" | custom-call | flops 671088640 | bytes 8388608 | tf_op jit(solution)/shard_map/ssd_back/pallas_call | solution.py:81
  91.6 0.7 dynamic-slice_bitcast_fusion.5
  93.6 3.3 %collective-permute-start.17 = (f32[8,128]{1,0:T(8,128)}, f32[8,128]{1,0:T(8,128)S(1)}, u32[]{:S(2)}, u32[]{:S(2)}) collective-permute-start(f32[8,128]{1,0:T(8,128)} %get-tuple-element.59), channel_id=1, source_target_pairs={{0,4},{2,6},{4,0},{6,2},{1,5},{3,7},{5,1},{7,3},{8,12},{10,14},{12... | collective-permute-start | bytes 12296 | tf_op jit(solution)/shard_map/ppermute | solution.py:446
  96.8 1.1 collective-permute-start.18
  98.3 2.0 %collective-permute-start.34 = (f32[16,128]{1,0:T(8,128)S(1)}, f32[16,128]{1,0:T(8,128)S(1)}, u32[]{:S(2)}, u32[]{:S(2)}) collective-permute-start(f32[16,128]{1,0:T(8,128)S(1)} %get-tuple-element.82), channel_id=1, source_target_pairs={{0,4},{2,6},{4,0},{6,2},{1,5},{3,7},{5,1},{7,3},{8,12},{10,14},{12... | collective-permute-start | bytes 24584 | tf_op jit(solution)/shard_map/ppermute | solution.py:446
  100.3 5.2 %attend_back_1.1 = (bf16[3,2,128,128]{3,2,1,0:T(8,128)(2,1)}, bf16[3,2,128,128]{3,2,1,0:T(8,128)(2,1)}, bf16[3,2,128,128]{3,2,1,0:T(8,128)(2,1)}, bf16[3,2,128,128]{3,2,1,0:T(8,128)(2,1)}) custom-call(s32[4]{0:T(128)} %pad_add_fusion.info, bf16[3,2,128,128]{3,2,1,0:T(8,128)(2,1)} %get-tuple-element.46.refs_0_, bf16[3,2,128,128]{3,2,1,0:T(8,128)(2,1)} %copy-done.4, ...), custom_call_target="tpu_custom_call" | custom-call | flops 536870912 | bytes 4194304 | tf_op jit(solution)/shard_map/attend_back_1/pallas_call | solution.py:81
  105.6 5.3 %attend_back_0.1 = (bf16[3,2,128,128]{3,2,1,0:T(8,128)(2,1)}, bf16[3,2,128,128]{3,2,1,0:T(8,128)(2,1)}, bf16[3,2,128,128]{3,2,1,0:T(8,128)(2,1)}, bf16[3,2,128,128]{3,2,1,0:T(8,128)(2,1)}) custom-call(s32[4]{0:T(128)} %pad_add_fusion.info, bf16[3,2,128,128]{3,2,1,0:T(8,128)(2,1)} %get-tuple-element.41.refs_0_, bf16[3,2,128,128]{3,2,1,0:T(8,128)(2,1)} %copy-done.3, ...), custom_call_target="tpu_custom_call" | custom-call | flops 536870912 | bytes 4194304 | tf_op jit(solution)/shard_map/attend_back_0/pallas_call | solution.py:81
  111.5 1.0 collective-permute-start.25
  112.5 1.5 collective-permute-start.19
  114.1 1.5 collective-permute-start.20
  115.6 0.8 collective-permute-done.33
  116.5 2.4 %collective-permute-start.21 = (f32[4,8,128]{2,1,0:T(8,128)S(1)}, f32[4,8,128]{2,1,0:T(8,128)S(1)}, u32[]{:S(2)}, u32[]{:S(2)}) collective-permute-start(f32[4,8,128]{2,1,0:T(8,128)S(1)} %pad_maximum_fusion), channel_id=1, source_target_pairs={{0,24},{8,0},{16,8},{24,16},{1,25},{9,1},{17,9},{25,17},{2,26},{10... | collective-permute-start | bytes 49160 | tf_op jit(solution)/shard_map/ppermute | solution.py:446
  118.9 1.2 gather_fusion
  120.1 1.1 collective-permute-start.26
  122.4 1.4 collective-permute-start.30
  123.8 2.8 %collective-permute-start.31 = (bf16[128,128]{1,0:T(8,128)(2,1)S(1)}, bf16[128,128]{1,0:T(8,128)(2,1)S(1)}, u32[]{:S(2)}, u32[]{:S(2)}) collective-permute-start(bf16[128,128]{1,0:T(8,128)(2,1)S(1)} %get-tuple-element.78), channel_id=1, source_target_pairs={{0,6},{2,0},{4,2},{6,4},{1,7},{3,1},{5,3},{7,5},{8,14},{10,8},{12,... | collective-permute-start | bytes 98312 | tf_op jit(solution)/shard_map/ppermute | solution.py:446
  128.0 4.2 %collective-permute-done.30 = bf16[128,128]{1,0:T(8,128)(2,1)S(1)} collective-permute-done((bf16[128,128]{1,0:T(8,128)(2,1)S(1)}, bf16[128,128]{1,0:T(8,128)(2,1)S(1)}, u32[]{:S(2)}, u32[]{:S(2)}) %collective-permute-start.30) | collective-permute-done | bytes 32800 | tf_op jit(solution)/shard_map/ppermute | solution.py:446
  132.2 4.3 %collective-permute-start.22 = (bf16[3,2,128,128]{3,2,1,0:T(8,128)(2,1)}, bf16[3,2,128,128]{3,2,1,0:T(8,128)(2,1)S(1)}, u32[]{:S(2)}, u32[]{:S(2)}) collective-permute-start(bf16[3,2,128,128]{3,2,1,0:T(8,128)(2,1)} %get-tuple-element.63), channel_id=1, source_target_pairs={{0,2},{2,4},{4,6},{6,0},{1,3},{3,5},{5,7},{7,1},{8,10},{10,12},{12... | collective-permute-start | bytes 589832 | tf_op jit(solution)/shard_map/ppermute | solution.py:446
  136.5 3.6 %collective-permute-start.23 = (bf16[3,2,128,128]{3,2,1,0:T(8,128)(2,1)}, bf16[3,2,128,128]{3,2,1,0:T(8,128)(2,1)S(1)}, u32[]{:S(2)}, u32[]{:S(2)}) collective-permute-start(bf16[3,2,128,128]{3,2,1,0:T(8,128)(2,1)} %get-tuple-element.64), channel_id=1, source_target_pairs={{0,4},{2,6},{4,0},{6,2},{1,5},{3,7},{5,1},{7,3},{8,12},{10,14},{12... | collective-permute-start | bytes 589832 | tf_op jit(solution)/shard_map/ppermute | solution.py:446
  140.1 1.0 collective-permute-start.24
  142.5 7.1 %collective-permute-done.22.refs_1_ = bf16[3,2,128,128]{3,2,1,0:T(8,128)(2,1)S(1)} collective-permute-done((bf16[3,2,128,128]{3,2,1,0:T(8,128)(2,1)}, bf16[3,2,128,128]{3,2,1,0:T(8,128)(2,1)S(1)}, u32[]{:S(2)}, u32[]{:S(2)}) %collective-permute-start.22) | collective-permute-done | bytes 196640 | tf_op jit(solution)/shard_map/ppermute | solution.py:446
  149.6 6.8 %collective-permute-done.23.refs_2_ = bf16[3,2,128,128]{3,2,1,0:T(8,128)(2,1)S(1)} collective-permute-done((bf16[3,2,128,128]{3,2,1,0:T(8,128)(2,1)}, bf16[3,2,128,128]{3,2,1,0:T(8,128)(2,1)S(1)}, u32[]{:S(2)}, u32[]{:S(2)}) %collective-permute-start.23) | collective-permute-done | bytes 196640 | tf_op jit(solution)/shard_map/ppermute | solution.py:446
  157.2 3.8 %finish.1 = bf16[3,1,128,16,128]{4,3,2,1,0:T(8,128)(2,1)} custom-call(s32[4]{0:T(128)} %pad_add_fusion.info, bf16[3,2,128,128]{3,2,1,0:T(8,128)(2,1)} %get-tuple-element.62.refs_0_, bf16[3,2,128,128]{3,2,1,0:T(8,128)(2,1)} %copy-done.14, bf16[3,2,128,128]{3,2,1,0:T(8,128)(2,1)} %copy-done.15, bf16[3,2,128,128]{3,2,1,0:T(8,128)(2,1)} %copy-done.16, ...), custom_call_target="tpu_custom_call" | custom-call | bytes 3145728 | tf_op jit(solution)/shard_map/finish/pallas_call | solution.py:81
  (138 shorter events, 12.8 us)
Async XLA Ops:
  0.7 20.8 %copy-start.31 = (f32[32]{0:T(128)S(1)}, f32[32]{0:T(128)}, u32[]{:S(2)}) copy-start(f32[32]{0:T(128)} %param.13) | copy-start | bytes 388
  3.0 14.5 %collective-permute-start.6 = (f32[16,128]{1,0:T(8,128)S(1)}, f32[16,128]{1,0:T(8,128)S(1)}, u32[]{:S(2)}, u32[]{:S(2)}) collective-permute-start(f32[16,128]{1,0:T(8,128)S(1)} %get-tuple-element.85), channel_id=1, source_target_pairs={{0,2},{2,4},{4,6},{6,0},{1,3},{3,5},{5,7},{7,1},{8,10},{10,12},{12... | collective-permute-start | bytes 24584 | tf_op jit(solution)/shard_map/ppermute | solution.py:446
  6.0 14.3 %collective-permute-start.7 = (f32[16,128]{1,0:T(8,128)S(1)}, f32[16,128]{1,0:T(8,128)S(1)}, u32[]{:S(2)}, u32[]{:S(2)}) collective-permute-start(f32[16,128]{1,0:T(8,128)S(1)} %get-tuple-element.84), channel_id=1, source_target_pairs={{0,4},{2,6},{4,0},{6,2},{1,5},{3,7},{5,1},{7,3},{8,12},{10,14},{12... | collective-permute-start | bytes 24584 | tf_op jit(solution)/shard_map/ppermute | solution.py:446
  14.2 61.2 %copy-start.32 = (s32[4]{0:T(128)S(1)}, s32[4]{0:T(128)}, u32[]{:S(2)}) copy-start(s32[4]{0:T(128)} %param.17) | copy-start | bytes 52
  14.3 23.3 %collective-permute-start.10 = (bf16[3,2,128,128]{3,2,1,0:T(8,128)(2,1)}, bf16[3,2,128,128]{3,2,1,0:T(8,128)(2,1)S(1)}, u32[]{:S(2)}, u32[]{:S(2)}) collective-permute-start(bf16[3,2,128,128]{3,2,1,0:T(8,128)(2,1)} %get-tuple-element.48), channel_id=1, source_target_pairs={{0,4},{2,6},{4,0},{6,2},{1,5},{3,7},{5,1},{7,3},{8,12},{10,14},{12... | collective-permute-start | bytes 589832 | tf_op jit(solution)/shard_map/ppermute | solution.py:446
  14.7 27.9 %copy-start = (bf16[2,128,128]{2,1,0:T(8,128)(2,1)}, bf16[2,128,128]{2,1,0:T(8,128)(2,1)S(1)}, u32[]{:S(2)}) copy-start(bf16[2,128,128]{2,1,0:T(8,128)(2,1)S(1)} %constant_dynamic-update-slice_fusion.refs_4_) | copy-start | bytes 196612
  14.7 12.5 %collective-permute-start.3 = (bf16[2,128,128]{2,1,0:T(8,128)(2,1)S(1)}, bf16[2,128,128]{2,1,0:T(8,128)(2,1)S(1)}, u32[]{:S(2)}, u32[]{:S(2)}) collective-permute-start(bf16[2,128,128]{2,1,0:T(8,128)(2,1)S(1)} %constant_dynamic-update-slice_fusion.refs_4_), channel_id=1, source_target_pairs={{0,2},{2,4},{4,6},{6,0},{1,3},{3,5},{5,7},{7,1},{8,10},{10,12},{12... | collective-permute-start | bytes 196616 | tf_op jit(solution)/shard_map/ppermute | solution.py:446
  16.3 16.5 %collective-permute-start.4 = (bf16[2,128,128]{2,1,0:T(8,128)(2,1)S(1)}, bf16[2,128,128]{2,1,0:T(8,128)(2,1)S(1)}, u32[]{:S(2)}, u32[]{:S(2)}) collective-permute-start(bf16[2,128,128]{2,1,0:T(8,128)(2,1)S(1)} %constant_dynamic-update-slice_fusion.refs_4_), channel_id=1, source_target_pairs={{0,4},{2,6},{4,0},{6,2},{1,5},{3,7},{5,1},{7,3},{8,12},{10,14},{12... | collective-permute-start | bytes 196616 | tf_op jit(solution)/shard_map/ppermute | solution.py:446
  17.4 25.2 %copy-start.17 = (f32[16,128]{1,0:T(8,128)}, f32[16,128]{1,0:T(8,128)S(1)}, u32[]{:S(2)}) copy-start(f32[16,128]{1,0:T(8,128)S(1)} %collective-permute-done.6.refs_9_) | copy-start | bytes 24580
  17.4 17.9 %collective-permute-start.5 = (bf16[2,128,128]{2,1,0:T(8,128)(2,1)S(1)}, bf16[2,128,128]{2,1,0:T(8,128)(2,1)S(1)}, u32[]{:S(2)}, u32[]{:S(2)}) collective-permute-start(bf16[2,128,128]{2,1,0:T(8,128)(2,1)S(1)} %constant_dynamic-update-slice_fusion.refs_4_), channel_id=1, source_target_pairs={{0,6},{2,0},{4,2},{6,4},{1,7},{3,1},{5,3},{7,5},{8,14},{10,8},{12,... | collective-permute-start | bytes 196616 | tf_op jit(solution)/shard_map/ppermute | solution.py:446
  20.3 22.3 %copy-start.18 = (f32[16,128]{1,0:T(8,128)}, f32[16,128]{1,0:T(8,128)S(1)}, u32[]{:S(2)}) copy-start(f32[16,128]{1,0:T(8,128)S(1)} %collective-permute-done.7.refs_10_) | copy-start | bytes 24580
  20.3 4.0 %collective-permute-start.8 = (f32[16,128]{1,0:T(8,128)S(1)}, f32[16,128]{1,0:T(8,128)S(1)}, u32[]{:S(2)}, u32[]{:S(2)}) collective-permute-start(f32[16,128]{1,0:T(8,128)S(1)} %get-tuple-element.83), channel_id=1, source_target_pairs={{0,6},{2,0},{4,2},{6,4},{1,7},{3,1},{5,3},{7,5},{8,14},{10,8},{12,... | collective-permute-start | bytes 24584 | tf_op jit(solution)/shard_map/ppermute | solution.py:446
  24.3 18.4 %copy-start.19 = (f32[16,128]{1,0:T(8,128)}, f32[16,128]{1,0:T(8,128)S(1)}, u32[]{:S(2)}) copy-start(f32[16,128]{1,0:T(8,128)S(1)} %collective-permute-done.8.refs_11_) | copy-start | bytes 24580
  24.3 14.7 %collective-permute-start.11 = (bf16[3,2,128,128]{3,2,1,0:T(8,128)(2,1)}, bf16[3,2,128,128]{3,2,1,0:T(8,128)(2,1)S(1)}, u32[]{:S(2)}, u32[]{:S(2)}) collective-permute-start(bf16[3,2,128,128]{3,2,1,0:T(8,128)(2,1)} %get-tuple-element.49), channel_id=1, source_target_pairs={{0,6},{2,0},{4,2},{6,4},{1,7},{3,1},{5,3},{7,5},{8,14},{10,8},{12,... | collective-permute-start | bytes 589832 | tf_op jit(solution)/shard_map/ppermute | solution.py:446
  27.2 15.4 %copy-start.7 = (bf16[2,128,128]{2,1,0:T(8,128)(2,1)}, bf16[2,128,128]{2,1,0:T(8,128)(2,1)S(1)}, u32[]{:S(2)}) copy-start(bf16[2,128,128]{2,1,0:T(8,128)(2,1)S(1)} %collective-permute-done.3.refs_5_) | copy-start | bytes 196612
  27.2 15.4 %collective-permute-start.9 = (bf16[3,2,128,128]{3,2,1,0:T(8,128)(2,1)}, bf16[3,2,128,128]{3,2,1,0:T(8,128)(2,1)S(1)}, u32[]{:S(2)}, u32[]{:S(2)}) collective-permute-start(bf16[3,2,128,128]{3,2,1,0:T(8,128)(2,1)} %get-tuple-element.47), channel_id=1, source_target_pairs={{0,2},{2,4},{4,6},{6,0},{1,3},{3,5},{5,7},{7,1},{8,10},{10,12},{12... | collective-permute-start | bytes 589832 | tf_op jit(solution)/shard_map/ppermute | solution.py:446
  32.8 19.1 %collective-permute-start = (bf16[3,2,128,128]{3,2,1,0:T(8,128)(2,1)}, bf16[3,2,128,128]{3,2,1,0:T(8,128)(2,1)S(1)}, u32[]{:S(2)}, u32[]{:S(2)}) collective-permute-start(bf16[3,2,128,128]{3,2,1,0:T(8,128)(2,1)} %get-tuple-element.42), channel_id=1, source_target_pairs={{0,2},{2,4},{4,6},{6,0},{1,3},{3,5},{5,7},{7,1},{8,10},{10,12},{12... | collective-permute-start | bytes 589832 | tf_op jit(solution)/shard_map/ppermute | solution.py:446
  35.3 20.6 %collective-permute-start.1 = (bf16[3,2,128,128]{3,2,1,0:T(8,128)(2,1)}, bf16[3,2,128,128]{3,2,1,0:T(8,128)(2,1)S(1)}, u32[]{:S(2)}, u32[]{:S(2)}) collective-permute-start(bf16[3,2,128,128]{3,2,1,0:T(8,128)(2,1)} %get-tuple-element.43), channel_id=1, source_target_pairs={{0,4},{2,6},{4,0},{6,2},{1,5},{3,7},{5,1},{7,3},{8,12},{10,14},{12... | collective-permute-start | bytes 589832 | tf_op jit(solution)/shard_map/ppermute | solution.py:446
  37.5 18.4 %collective-permute-start.2 = (bf16[3,2,128,128]{3,2,1,0:T(8,128)(2,1)}, bf16[3,2,128,128]{3,2,1,0:T(8,128)(2,1)S(1)}, u32[]{:S(2)}, u32[]{:S(2)}) collective-permute-start(bf16[3,2,128,128]{3,2,1,0:T(8,128)(2,1)} %get-tuple-element.44), channel_id=1, source_target_pairs={{0,6},{2,0},{4,2},{6,4},{1,7},{3,1},{5,3},{7,5},{8,14},{10,8},{12,... | collective-permute-start | bytes 589832 | tf_op jit(solution)/shard_map/ppermute | solution.py:446
  66.0 1.2 collective-permute-start.12
  67.2 9.6 %collective-permute-start.13 = (f32[1,512]{1,0:T(1,128)S(1)}, f32[1,512]{1,0:T(1,128)S(1)}, u32[]{:S(2)}, u32[]{:S(2)}) collective-permute-start(f32[1,512]{1,0:T(1,128)S(1)} %add.136.refs_0_), channel_id=1, source_target_pairs={{0,2},{2,4},{4,6},{6,0},{1,3},{3,5},{5,7},{7,1},{8,10},{10,12},{12... | collective-permute-start | bytes 6152 | tf_op jit(solution)/shard_map/ppermute | solution.py:446
  73.0 4.5 %collective-permute-start.14 = (f32[1,512]{1,0:T(1,128)S(1)}, f32[1,512]{1,0:T(1,128)S(1)}, u32[]{:S(2)}, u32[]{:S(2)}) collective-permute-start(f32[1,512]{1,0:T(1,128)S(1)} %add.136.refs_0_), channel_id=1, source_target_pairs={{0,4},{2,6},{4,0},{6,2},{1,5},{3,7},{5,1},{7,3},{8,12},{10,14},{12... | collective-permute-start | bytes 6152 | tf_op jit(solution)/shard_map/ppermute | solution.py:446
  73.0 4.5 %collective-permute-start.15 = (f32[1,512]{1,0:T(1,128)S(1)}, f32[1,512]{1,0:T(1,128)S(1)}, u32[]{:S(2)}, u32[]{:S(2)}) collective-permute-start(f32[1,512]{1,0:T(1,128)S(1)} %add.136.refs_0_), channel_id=1, source_target_pairs={{0,6},{2,0},{4,2},{6,4},{1,7},{3,1},{5,3},{7,5},{8,14},{10,8},{12,... | collective-permute-start | bytes 6152 | tf_op jit(solution)/shard_map/ppermute | solution.py:446
  93.0 18.0 %collective-permute-start.16 = (f32[8,128]{1,0:T(8,128)}, f32[8,128]{1,0:T(8,128)S(1)}, u32[]{:S(2)}, u32[]{:S(2)}) collective-permute-start(f32[8,128]{1,0:T(8,128)} %get-tuple-element.59), channel_id=1, source_target_pairs={{0,2},{2,4},{4,6},{6,0},{1,3},{3,5},{5,7},{7,1},{8,10},{10,12},{12... | collective-permute-start | bytes 12296 | tf_op jit(solution)/shard_map/ppermute | solution.py:446
  93.6 17.9 %collective-permute-start.17 = (f32[8,128]{1,0:T(8,128)}, f32[8,128]{1,0:T(8,128)S(1)}, u32[]{:S(2)}, u32[]{:S(2)}) collective-permute-start(f32[8,128]{1,0:T(8,128)} %get-tuple-element.59), channel_id=1, source_target_pairs={{0,4},{2,6},{4,0},{6,2},{1,5},{3,7},{5,1},{7,3},{8,12},{10,14},{12... | collective-permute-start | bytes 12296 | tf_op jit(solution)/shard_map/ppermute | solution.py:446
  96.8 14.7 %collective-permute-start.18 = (f32[8,128]{1,0:T(8,128)}, f32[8,128]{1,0:T(8,128)S(1)}, u32[]{:S(2)}, u32[]{:S(2)}) collective-permute-start(f32[8,128]{1,0:T(8,128)} %get-tuple-element.59), channel_id=1, source_target_pairs={{0,6},{2,0},{4,2},{6,4},{1,7},{3,1},{5,3},{7,5},{8,14},{10,8},{12,... | collective-permute-start | bytes 12296 | tf_op jit(solution)/shard_map/ppermute | solution.py:446
  97.9 14.6 %collective-permute-start.35 = (f32[16,128]{1,0:T(8,128)S(1)}, f32[16,128]{1,0:T(8,128)S(1)}, u32[]{:S(2)}, u32[]{:S(2)}) collective-permute-start(f32[16,128]{1,0:T(8,128)S(1)} %get-tuple-element.81), channel_id=1, source_target_pairs={{0,6},{2,0},{4,2},{6,4},{1,7},{3,1},{5,3},{7,5},{8,14},{10,8},{12,... | collective-permute-start | bytes 24584 | tf_op jit(solution)/shard_map/ppermute | solution.py:446
  98.3 15.8 %collective-permute-start.34 = (f32[16,128]{1,0:T(8,128)S(1)}, f32[16,128]{1,0:T(8,128)S(1)}, u32[]{:S(2)}, u32[]{:S(2)}) collective-permute-start(f32[16,128]{1,0:T(8,128)S(1)} %get-tuple-element.82), channel_id=1, source_target_pairs={{0,4},{2,6},{4,0},{6,2},{1,5},{3,7},{5,1},{7,3},{8,12},{10,14},{12... | collective-permute-start | bytes 24584 | tf_op jit(solution)/shard_map/ppermute | solution.py:446
  105.6 14.5 %copy-start.28 = (bf16[3,2,128,128]{3,2,1,0:T(8,128)(2,1)S(1)}, bf16[3,2,128,128]{3,2,1,0:T(8,128)(2,1)}, u32[]{:S(2)}) copy-start(bf16[3,2,128,128]{3,2,1,0:T(8,128)(2,1)} %get-tuple-element.70) | copy-start | bytes 589828
  105.6 16.2 %copy-start.10 = (f32[4,128,128]{2,1,0:T(8,128)S(1)}, f32[4,128,128]{2,1,0:T(8,128)}, u32[]{:S(2)}) copy-start(f32[4,128,128]{2,1,0:T(8,128)} %get-tuple-element.72) | copy-start | bytes 786436
  105.6 22.3 %copy-start.27 = (bf16[3,2,128,128]{3,2,1,0:T(8,128)(2,1)S(1)}, bf16[3,2,128,128]{3,2,1,0:T(8,128)(2,1)}, u32[]{:S(2)}) copy-start(bf16[3,2,128,128]{3,2,1,0:T(8,128)(2,1)} %get-tuple-element.71) | copy-start | bytes 589828
  110.9 5.5 %collective-permute-start.33 = (f32[16,128]{1,0:T(8,128)S(1)}, f32[16,128]{1,0:T(8,128)S(1)}, u32[]{:S(2)}, u32[]{:S(2)}) collective-permute-start(f32[16,128]{1,0:T(8,128)S(1)} %get-tuple-element.80), channel_id=1, source_target_pairs={{0,2},{2,4},{4,6},{6,0},{1,3},{3,5},{5,7},{7,1},{8,10},{10,12},{12... | collective-permute-start | bytes 24584 | tf_op jit(solution)/shard_map/ppermute | solution.py:446
  111.5 10.2 %collective-permute-start.28 = (bf16[4,128,128]{2,1,0:T(8,128)(2,1)S(1)}, bf16[4,128,128]{2,1,0:T(8,128)(2,1)S(1)}, u32[]{:S(2)}, u32[]{:S(2)}) collective-permute-start(bf16[4,128,128]{2,1,0:T(8,128)(2,1)S(1)} %copy-done.30), channel_id=1, source_target_pairs={{0,1},{1,0},{2,3},{3,2},{4,5},{5,4},{6,7},{7,6},{8,9},{9,8},{10,11... | collective-permute-start | bytes 393224 | tf_op jit(solution)/shard_map/ppermute | solution.py:446
  111.5 28.6 %collective-permute-start.25 = (bf16[3,2,128,128]{3,2,1,0:T(8,128)(2,1)S(1)}, bf16[3,2,128,128]{3,2,1,0:T(8,128)(2,1)S(1)}, u32[]{:S(2)}, u32[]{:S(2)}) collective-permute-start(bf16[3,2,128,128]{3,2,1,0:T(8,128)(2,1)S(1)} %copy-done.29), channel_id=1, source_target_pairs={{0,2},{2,4},{4,6},{6,0},{1,3},{3,5},{5,7},{7,1},{8,10},{10,12},{12... | collective-permute-start | bytes 589832 | tf_op jit(solution)/shard_map/ppermute | solution.py:446
  112.5 7.5 %collective-permute-start.19 = (f32[4,8,128]{2,1,0:T(8,128)S(1)}, f32[4,8,128]{2,1,0:T(8,128)S(1)}, u32[]{:S(2)}, u32[]{:S(2)}) collective-permute-start(f32[4,8,128]{2,1,0:T(8,128)S(1)} %pad_maximum_fusion), channel_id=1, source_target_pairs={{0,8},{8,16},{16,24},{24,0},{1,9},{9,17},{17,25},{25,1},{2,10},{10... | collective-permute-start | bytes 49160 | tf_op jit(solution)/shard_map/ppermute | solution.py:446
  114.1 7.1 %collective-permute-start.20 = (f32[4,8,128]{2,1,0:T(8,128)S(1)}, f32[4,8,128]{2,1,0:T(8,128)S(1)}, u32[]{:S(2)}, u32[]{:S(2)}) collective-permute-start(f32[4,8,128]{2,1,0:T(8,128)S(1)} %pad_maximum_fusion), channel_id=1, source_target_pairs={{0,16},{8,24},{16,0},{24,8},{1,17},{9,25},{17,1},{25,9},{2,18},{10... | collective-permute-start | bytes 49160 | tf_op jit(solution)/shard_map/ppermute | solution.py:446
  116.5 4.7 %collective-permute-start.21 = (f32[4,8,128]{2,1,0:T(8,128)S(1)}, f32[4,8,128]{2,1,0:T(8,128)S(1)}, u32[]{:S(2)}, u32[]{:S(2)}) collective-permute-start(f32[4,8,128]{2,1,0:T(8,128)S(1)} %pad_maximum_fusion), channel_id=1, source_target_pairs={{0,24},{8,0},{16,8},{24,16},{1,25},{9,1},{17,9},{25,17},{2,26},{10... | collective-permute-start | bytes 49160 | tf_op jit(solution)/shard_map/ppermute | solution.py:446
  120.1 21.1 %collective-permute-start.26 = (bf16[3,2,128,128]{3,2,1,0:T(8,128)(2,1)S(1)}, bf16[3,2,128,128]{3,2,1,0:T(8,128)(2,1)S(1)}, u32[]{:S(2)}, u32[]{:S(2)}) collective-permute-start(bf16[3,2,128,128]{3,2,1,0:T(8,128)(2,1)S(1)} %copy-done.28), channel_id=1, source_target_pairs={{0,4},{2,6},{4,0},{6,2},{1,5},{3,7},{5,1},{7,3},{8,12},{10,14},{12... | collective-permute-start | bytes 589832 | tf_op jit(solution)/shard_map/ppermute | solution.py:446
  121.8 6.0 %collective-permute-start.29 = (bf16[128,128]{1,0:T(8,128)(2,1)S(1)}, bf16[128,128]{1,0:T(8,128)(2,1)S(1)}, u32[]{:S(2)}, u32[]{:S(2)}) collective-permute-start(bf16[128,128]{1,0:T(8,128)(2,1)S(1)} %get-tuple-element.77), channel_id=1, source_target_pairs={{0,2},{2,4},{4,6},{6,0},{1,3},{3,5},{5,7},{7,1},{8,10},{10,12},{12... | collective-permute-start | bytes 98312 | tf_op jit(solution)/shard_map/ppermute | solution.py:446
  122.4 9.8 %collective-permute-start.30 = (bf16[128,128]{1,0:T(8,128)(2,1)S(1)}, bf16[128,128]{1,0:T(8,128)(2,1)S(1)}, u32[]{:S(2)}, u32[]{:S(2)}) collective-permute-start(bf16[128,128]{1,0:T(8,128)(2,1)S(1)} %get-tuple-element.79), channel_id=1, source_target_pairs={{0,4},{2,6},{4,0},{6,2},{1,5},{3,7},{5,1},{7,3},{8,12},{10,14},{12... | collective-permute-start | bytes 98312 | tf_op jit(solution)/shard_map/ppermute | solution.py:446
  123.8 12.8 %collective-permute-start.31 = (bf16[128,128]{1,0:T(8,128)(2,1)S(1)}, bf16[128,128]{1,0:T(8,128)(2,1)S(1)}, u32[]{:S(2)}, u32[]{:S(2)}) collective-permute-start(bf16[128,128]{1,0:T(8,128)(2,1)S(1)} %get-tuple-element.78), channel_id=1, source_target_pairs={{0,6},{2,0},{4,2},{6,4},{1,7},{3,1},{5,3},{7,5},{8,14},{10,8},{12,... | collective-permute-start | bytes 98312 | tf_op jit(solution)/shard_map/ppermute | solution.py:446
  127.9 14.6 %collective-permute-start.27 = (bf16[3,2,128,128]{3,2,1,0:T(8,128)(2,1)S(1)}, bf16[3,2,128,128]{3,2,1,0:T(8,128)(2,1)S(1)}, u32[]{:S(2)}, u32[]{:S(2)}) collective-permute-start(bf16[3,2,128,128]{3,2,1,0:T(8,128)(2,1)S(1)} %copy-done.27), channel_id=1, source_target_pairs={{0,6},{2,0},{4,2},{6,4},{1,7},{3,1},{5,3},{7,5},{8,14},{10,8},{12,... | collective-permute-start | bytes 589832 | tf_op jit(solution)/shard_map/ppermute | solution.py:446
  132.2 17.4 %collective-permute-start.22 = (bf16[3,2,128,128]{3,2,1,0:T(8,128)(2,1)}, bf16[3,2,128,128]{3,2,1,0:T(8,128)(2,1)S(1)}, u32[]{:S(2)}, u32[]{:S(2)}) collective-permute-start(bf16[3,2,128,128]{3,2,1,0:T(8,128)(2,1)} %get-tuple-element.63), channel_id=1, source_target_pairs={{0,2},{2,4},{4,6},{6,0},{1,3},{3,5},{5,7},{7,1},{8,10},{10,12},{12... | collective-permute-start | bytes 589832 | tf_op jit(solution)/shard_map/ppermute | solution.py:446
  136.5 19.9 %collective-permute-start.23 = (bf16[3,2,128,128]{3,2,1,0:T(8,128)(2,1)}, bf16[3,2,128,128]{3,2,1,0:T(8,128)(2,1)S(1)}, u32[]{:S(2)}, u32[]{:S(2)}) collective-permute-start(bf16[3,2,128,128]{3,2,1,0:T(8,128)(2,1)} %get-tuple-element.64), channel_id=1, source_target_pairs={{0,4},{2,6},{4,0},{6,2},{1,5},{3,7},{5,1},{7,3},{8,12},{10,14},{12... | collective-permute-start | bytes 589832 | tf_op jit(solution)/shard_map/ppermute | solution.py:446
  140.1 16.3 %copy-start.11 = (bf16[3,2,128,128]{3,2,1,0:T(8,128)(2,1)}, bf16[3,2,128,128]{3,2,1,0:T(8,128)(2,1)S(1)}, u32[]{:S(2)}) copy-start(bf16[3,2,128,128]{3,2,1,0:T(8,128)(2,1)S(1)} %collective-permute-done.25.refs_5_) | copy-start | bytes 589828
  140.1 16.3 %collective-permute-start.24 = (bf16[3,2,128,128]{3,2,1,0:T(8,128)(2,1)}, bf16[3,2,128,128]{3,2,1,0:T(8,128)(2,1)S(1)}, u32[]{:S(2)}, u32[]{:S(2)}) collective-permute-start(bf16[3,2,128,128]{3,2,1,0:T(8,128)(2,1)} %get-tuple-element.65), channel_id=1, source_target_pairs={{0,6},{2,0},{4,2},{6,4},{1,7},{3,1},{5,3},{7,5},{8,14},{10,8},{12,... | collective-permute-start | bytes 589832 | tf_op jit(solution)/shard_map/ppermute | solution.py:446
  141.1 15.3 %copy-start.12 = (bf16[3,2,128,128]{3,2,1,0:T(8,128)(2,1)}, bf16[3,2,128,128]{3,2,1,0:T(8,128)(2,1)S(1)}, u32[]{:S(2)}) copy-start(bf16[3,2,128,128]{3,2,1,0:T(8,128)(2,1)S(1)} %collective-permute-done.26.refs_6_) | copy-start | bytes 589828
  141.1 19.9 %collective-permute-start.32 = (f32[128,128]{1,0:T(8,128)S(1)}, f32[128,128]{1,0:T(8,128)S(1)}, u32[]{:S(2)}, u32[]{:S(2)}) collective-permute-start(f32[128,128]{1,0:T(8,128)S(1)} %fusion.1), channel_id=1, source_target_pairs={{0,1},{1,0},{2,3},{3,2},{4,5},{5,4},{6,7},{7,6},{8,9},{9,8},{10,11... | collective-permute-start | bytes 196616 | tf_op jit(solution)/shard_map/ppermute | solution.py:446
  (21 other events, 115.1 us)

commit v2 on v0

v2 whole, which is shorter than its diff:
```python
import functools
import math

import jax
import jax.numpy as jnp
from jax import lax
from jax.experimental import pallas as pl
from jax.experimental.pallas import tpu as pltpu
from jax.sharding import PartitionSpec as P

MASK_FILL = -1e30
NORM_EPS = 1e-05
HIGHEST = lax.Precision.HIGHEST
LOG2E = 1.4426950408889634
GROUPS = (2, 2)
F32 = jnp.float32
BF16 = jnp.bfloat16

ANY = pl.BlockSpec(memory_space=pl.ANY)
SHAPE = jax.ShapeDtypeStruct
VM = pl.BlockSpec(memory_space=pltpu.VMEM)
SM = pl.BlockSpec(memory_space=pltpu.SMEM)


def dot(a, b, precision=None):
    return jnp.dot(a, b, preferred_element_type=F32, precision=precision)


def dot_nt(a, b, precision=None):
    return lax.dot_general(a, b, (((1,), (1,)), ((), ())), preferred_element_type=F32, precision=precision)


def dot_tn(a, b, precision=None):
    return lax.dot_general(a, b, (((0,), (0,)), ((), ())), preferred_element_type=F32, precision=precision)


def iota(shape, dim):
    return lax.broadcasted_iota(jnp.int32, shape, dim)


def mat(cond):
    return jnp.where(cond, 1.0, 0.0).astype(F32)


class Sizes:
    def __init__(self, n, tokens, heads_local, head_dim, ssd_local, state):
        self.n, self.t, self.hl, self.hd, self.ns = n, tokens, heads_local, head_dim, state
        self.s = n * tokens
        self.a = heads_local // n
        self.sizes = GROUPS if sum(GROUPS) == self.a else (self.a,)
        self.first = [sum(self.sizes[:g]) for g in range(len(self.sizes))]
        self.groups = len(self.sizes)
        self.h = ssd_local // n
        self.hl_ssd = ssd_local
        self.mp = heads_local * head_dim // ssd_local
        self.f = self.a * head_dim
        self.r = -(-(self.h + 1) // 8) * 8
        self.rp = -(-self.r // 16) * 16
        self.features = self.f // head_dim
        self.v = -(-(self.features + 2) // 8) * 8
        self.rows = min(256, self.s)
        self.blocks = self.s // self.rows
        self.static = self.blocks <= 2
        self.up, self.down, self.mid = 0, self.s, 2 * self.s
        self.pay = self.mid + 8 * n
        self.rate = self.pay + self.r * n
        self.weight = self.rate + self.r
        self.term_rows = self.weight + 8
        self.pay_rows = tokens + 2 * self.rp

    def sent_rows(self, g):
        return 3 * self.sizes[g] * self.t + (0 if g else self.pay_rows)

    def back_rows(self, g):
        rows = 3 * self.sizes[g] * self.t
        if g == 0:
            rows += self.t + self.rp + 2 * self.v
        return rows

    def rows_of(self, g, k, a):
        first = (k * self.sizes[g] + a) * self.t
        return slice(first, first + self.t)

    def lanes(self, g):
        return pl.ds(self.first[g] * self.hd, self.sizes[g] * self.hd)

    def each_block(self, body):
        if self.static:
            for i in range(self.blocks):
                body(i)
        else:

            @pl.loop(0, self.blocks)
            def _(i):
                body(i)

    def upto(self, i):
        return (i + 1) * self.rows if self.static else self.s

    def onward(self, i):
        return i * self.rows if self.static else 0

    def each_chunk(self, body):
        if self.static:
            for c in range(self.n):
                body(c)
        else:

            @pl.loop(0, self.n)
            def _(c):
                body(c)

    def chunk(self, c, base=0):
        return pl.ds(base + c * self.t if isinstance(c, int) else pl.multiple_of(base + c * self.t, self.t), self.t)

    def small(self, c, base, rows):
        return pl.ds(base + c * rows if isinstance(c, int) else pl.multiple_of(base + c * rows, 8), rows)

    def block(self, i):
        return pl.ds(i * self.rows if self.static else pl.multiple_of(i * self.rows, self.rows), self.rows)


def call(z, kernel, name, out_shape, in_specs, out_specs, scratch, args, flops=0, nbytes=0):
    return pl.pallas_call(
        functools.partial(kernel, z),
        name=name,
        out_shape=out_shape,
        in_specs=in_specs,
        out_specs=out_specs,
        scratch_shapes=scratch,
        compiler_params=pltpu.CompilerParams(vmem_limit_bytes=(14 if z.static else 56) * 1024 * 1024),
        cost_estimate=pl.CostEstimate(flops=flops, bytes_accessed=nbytes, transcendentals=0),
    )(*args)


def in_hbm(x):
    return pltpu.with_memory_space_constraint(x, pltpu.HBM)


class Copies:
    def __init__(self, sems):
        self.sems, self.count = sems, 0

    def start(self, source, target):
        one = pltpu.make_async_copy(source, target, self.sems.at[self.count])
        self.count += 1
        one.start()
        return one


def wait_all(copies):
    for one in copies:
        one.wait()


def split3(x):
    high = x.astype(BF16)
    rest = x - high.astype(F32)
    middle = rest.astype(BF16)
    return high, middle, (rest - middle.astype(F32)).astype(BF16)


def split2_dot(x, exact):
    high, low = split3(x)[:2]
    return dot(high, exact) + dot(low, exact)


def prep_kernel(z, qkv, b_in, c_in, step_in, labels_in, table_in, *refs):
    outs, refs = refs[: z.n * z.groups], refs[z.n * z.groups :]
    held, (parts, b, c, step, labels, table, sems) = refs[: z.groups], refs[z.groups :]
    me, core = lax.axis_index("context"), lax.axis_index("head")
    mover = Copies(sems)
    loads = [mover.start(qkv.at[k, 0], parts.at[k]) for k in range(3)]
    tiny = [
        mover.start(b_in.at[0], b),
        mover.start(c_in.at[0], c),
        mover.start(step_in.at[0], step),
        mover.start(labels_in, labels),
        mover.start(table_in, table),
    ]
    wait_all(tiny)
    onehot = mat(iota((table.shape[1], z.t), 0) == labels[...])
    target = dot(table[...], onehot, HIGHEST)
    mine = jnp.where(core == 0, b[...], c[...])
    end = 3 * z.sizes[0] * z.t
    for j in range(z.n):
        row = iota((z.r, z.hl_ssd), 0)
        pick = mat((iota((z.r, z.hl_ssd), 1) == j * z.h + row) & (row < z.h))
        pay = dot(pick, step[...], HIGHEST)
        pay = jnp.where(iota((z.r, z.t), 0) == z.h, target, pay)
        held[0][j, end : end + z.t] = mine
        held[0][j, end + z.t :] = jnp.zeros((2 * z.rp, z.t), BF16)
        for i, term in enumerate(split3(pay)[:2]):
            start = end + z.t + i * z.rp
            held[0][j, start : start + z.r] = term
    for k in range(3):
        loads[k].wait()
        turned = jnp.swapaxes(parts[k], 0, 1)
        for g in range(z.groups):
            for j in range(z.n):
                for a in range(z.sizes[g]):
                    held[g][j, z.rows_of(g, k, a), :] = turned[j * z.a + z.first[g] + a]
    copies = []
    for g in range(z.groups):
        for s in range(z.n):
            copies.append(mover.start(held[g].at[lax.rem(me + s, z.n)], outs[g * z.n + s]))
    wait_all(copies)


def prep(z, qkv, b, c, step, labels, table):
    args = [in_hbm(x) for x in (qkv, b, c, step, labels, table)]
    return call(
        z,
        prep_kernel,
        "prep",
        [SHAPE((z.sent_rows(g), z.hd), BF16) for g in range(z.groups) for _ in range(z.n)],
        [ANY] * 6,
        [ANY] * (z.n * z.groups),
        [
            *[pltpu.VMEM((z.n, z.sent_rows(g), z.hd), BF16) for g in range(z.groups)],
            pltpu.VMEM((3, z.t, z.hl, z.hd), BF16),
            pltpu.VMEM((z.t, z.ns), BF16),
            pltpu.VMEM((z.t, z.ns), BF16),
            pltpu.VMEM(step.shape[1:], F32),
            pltpu.VMEM(labels.shape, jnp.int32),
            pltpu.VMEM(table.shape, F32),
            pltpu.SemaphoreType.DMA((8 + z.n * z.groups,)),
        ],
        args,
        nbytes=qkv.size * 4,
    )


def pick_kernel(z, *refs):
    ins, (mine, pay, parts, sems) = refs[: z.n], refs[z.n :]
    me = lax.axis_index("context")
    mover = Copies(sems)
    rows = pl.ds(3 * z.sizes[0] * z.t, z.pay_rows)
    wait_all([mover.start(ins[s].at[rows], parts.at[s]) for s in range(z.n)])
    for s in range(z.n):
        source = lax.rem(me + z.n - s, z.n)
        mine[source] = parts[s, : z.t]
        terms = [parts[s, z.t + k * z.rp : z.t + k * z.rp + z.r].astype(F32) for k in range(2)]
        pay[source] = terms[0] + terms[1]


def pick(z, ins):
    return call(
        z,
        pick_kernel,
        "pick",
        (SHAPE((z.n, z.t, z.ns), BF16), SHAPE((z.n, z.r, z.t), F32)),
        [ANY] * z.n,
        [VM] * 2,
        [pltpu.VMEM((z.n, z.pay_rows, z.t), BF16), pltpu.SemaphoreType.DMA((z.n,))],
        ins,
    )


def decay_kernel(z, mine, theirs, pay, rate, weight, terms, bc):
    n, t = z.n, z.t
    me, core = lax.axis_index("context"), lax.axis_index("head")
    heads = z.hl_ssd
    row, col = iota((z.r, heads), 0), iota((z.r, heads), 1)
    pick = mat((col == me * z.h + row) & (row < z.h))
    terms[z.rate : z.rate + z.r, :t] = dot_nt(pick, jnp.broadcast_to(rate[...], (t, heads)), HIGHEST)
    pick = mat(iota((8, z.hl), 1) == me * z.a + iota((8, z.hl), 0))
    terms[z.weight : z.weight + 8, : z.hd] = dot(pick, weight[...].astype(F32))
    rates = jnp.broadcast_to(rate[...], (8, heads))
    rates = dot(rates, mat(iota((heads, z.f), 0) == me * z.h + iota((heads, z.f), 1) // z.mp), HIGHEST)
    rates = rates[0:1]
    for c in range(n):
        bc[c, 0] = jnp.where(core == 0, mine[c], theirs[c])
        bc[c, 1] = jnp.where(core == 0, theirs[c], mine[c])
        terms[z.pay + c * z.r : z.pay + (c + 1) * z.r, :t] = pay[c]
    causal = iota((t, t), 0) >= iota((t, t), 1)
    lower = mat(causal)
    spread_heads = mat(iota((z.r, z.f), 0) == iota((z.r, z.f), 1) // z.mp)

    def chunk(c):
        steps = terms[z.small(c, z.pay, z.r), :t]
        cum = dot(dot_nt(lower, steps, HIGHEST), spread_heads, HIGHEST) * (-rates)
        half = 0.5 * cum[t - 1 : t]
        terms[z.chunk(c, z.up), :] = jnp.exp(cum - half)
        terms[z.chunk(c, z.down), :] = jnp.exp(half - cum)
        terms[z.small(c, z.mid, 8), :] = jnp.broadcast_to(jnp.exp(half), (8, z.f))
        inner = split3(jnp.where(causal, dot_nt(bc[c, 1], bc[c, 0]), 0.0))
        bc[c, 2] = inner[0]
        bc[c, 3] = inner[1]

    z.each_chunk(chunk)


def decay(z, mine, theirs, pay, rate, weight):
    return call(
        z,
        decay_kernel,
        "decay",
        (SHAPE((z.term_rows, z.f), F32), SHAPE((z.n, 4, z.t, z.ns), BF16)),
        [VM] * 5,
        [VM] * 2,
        [],
        (mine, theirs, pay, rate, weight),
        nbytes=8 * z.s * z.f,
    )


def attend_kernel(z, g, *refs):
    n, t, count = z.n, z.t, z.sizes[g]
    ins, refs = refs[:n], refs[n + (1 if g else 0) :]
    prob_out, attended_out, qkv_out, held, prob, attended, sems = refs
    mover = Copies(sems)
    me = lax.axis_index("context")
    rows = pl.ds(0, 3 * count * t)
    wait_all([mover.start(ins[s].at[rows], held.at[lax.rem(me + n - s, n)]) for s in range(n)])
    stores = [mover.start(held, qkv_out)]

    def rows_upto(k, a, width):
        return held[: width // t, z.rows_of(g, k, a), :].reshape(width, z.hd)

    def rows_block(k, a, i):
        per = z.rows // t
        return held[pl.ds(i * per, per), z.rows_of(g, k, a), :].reshape(z.rows, z.hd)

    factor = LOG2E / math.sqrt(z.hd)
    for a in range(count):

        def attend(i):
            width = z.upto(i)
            rows = z.block(i)
            scores = dot_nt(rows_block(0, a, i), rows_upto(1, a, width))
            keep = iota((z.rows, width), 1) <= i * z.rows + iota((z.rows, width), 0)
            scores = jnp.where(keep, scores, MASK_FILL)
            weight = jnp.exp2((scores - jnp.max(scores, axis=1, keepdims=True)) * factor)
            weight = (weight * (1.0 / jnp.sum(weight, axis=1, keepdims=True))).astype(BF16)
            prob[a, rows, :width] = weight
            attended[rows, a * z.hd : (a + 1) * z.hd] = dot(weight, rows_upto(2, a, width)).astype(BF16)

        z.each_block(attend)
        stores.append(mover.start(prob.at[a], prob_out.at[a]))
    stores.append(mover.start(attended, attended_out))
    wait_all(stores)


def attend(z, g, ins, after):
    count = z.sizes[g]
    outs = (
        SHAPE((count, z.s, z.s), BF16),
        SHAPE((z.s, count * z.hd), BF16),
        SHAPE((z.n, 3 * count * z.t, z.hd), BF16),
    )
    scratch = [
        pltpu.VMEM((z.n, 3 * count * z.t, z.hd), BF16),
        pltpu.VMEM((count, z.s, z.s), BF16),
        pltpu.VMEM((z.s, count * z.hd), BF16),
        pltpu.SemaphoreType.DMA((z.n + 2 + count,)),
    ]
    return call(
        z,
        lambda z, *refs: attend_kernel(z, g, *refs),
        "attend_%d" % g,
        outs,
        [ANY] * (z.n + len(after)),
        [ANY] * 3,
        scratch,
        (*ins, *after),
        flops=count * z.s * z.s * z.hd * 4,
        nbytes=count * z.s * z.s * 8,
    )


def ssd_kernel(z, *refs):
    n, t = z.n, z.t
    ins, refs = refs[: z.groups], refs[z.groups :]
    terms, bc, saved_out, value, attended, saved, state_low, adds, sems = refs
    mover = Copies(sems)
    wait_all([mover.start(ins[g], attended.at[:, z.lanes(g)]) for g in range(z.groups)])
    same_head = mat(iota((z.hd, z.hd), 0) // z.mp == iota((z.hd, z.hd), 1) // z.mp).astype(BF16)

    def enter(c):
        rows = z.chunk(c)
        high, low = split3(terms[z.chunk(c, z.down), :] * attended[rows, :].astype(F32))[:2]
        saved[0, rows, :] = high
        saved[5, rows, :] = low
        adds[rows, :] = dot_tn(bc[c, 0], high) + dot_tn(bc[c, 0], low)

    z.each_chunk(enter)

    def step(c, state):
        m = terms[z.small(c, z.mid, 8), :][0:1]
        state = m * state
        high, low = split3(state)[:2]
        saved[3, z.chunk(c), :] = high
        state_low[z.chunk(c), :] = low
        return m * (state + adds[z.chunk(c), :])

    state = jnp.zeros((z.ns, z.f), F32)
    if z.static:
        for c in range(n):
            state = step(c, state)
    else:
        lax.fori_loop(0, n, step, state)

    def leave(c):
        rows = z.chunk(c)
        up = terms[z.chunk(c, z.up), :]
        left = [bc[c, k] for k in (2, 2, 3, 1, 1)]
        right = [saved[0, rows, :], saved[5, rows, :], saved[0, rows, :], saved[3, rows, :], state_low[rows, :]]
        y = up * dot(jnp.concatenate(left, axis=1), jnp.concatenate(right, axis=0))
        total = jnp.zeros((t, z.hd), F32)
        for a in range(z.a):
            part = slice(a * z.hd, (a + 1) * z.hd)
            ya = y[:, part]
            weight = terms[z.weight + a : z.weight + a + 1, : z.hd]
            scale = lax.rsqrt(split2_dot(ya * ya, same_head) * (1.0 / z.mp) + NORM_EPS)
            unit = ya * scale
            term = unit * weight
            total = total + term
            mean = split2_dot(term, same_head) * (1.0 / z.mp)
            saved[1, rows, part] = unit.astype(BF16)
            slope = split3(up[:, part] * scale * (weight - unit * mean))
            saved[2, rows, part] = slope[0]
            saved[4, rows, part] = slope[1]
        high, low = split3(total)[:2]
        ones = jnp.ones((8, z.hd), BF16)
        value[:, rows] = (dot_nt(ones, high) + dot_nt(ones, low))[0:1]

    z.each_chunk(leave)
    mover.start(saved, saved_out).wait()


def ssd(z, ins, terms, bc):
    return call(
        z,
        ssd_kernel,
        "ssd",
        (SHAPE((6, z.s, z.f), BF16), SHAPE((1, z.s), F32)),
        [ANY] * z.groups + [VM] * 2,
        [ANY, VM],
        [
            pltpu.VMEM((z.s, z.f), BF16),
            pltpu.VMEM((6, z.s, z.f), BF16),
            pltpu.VMEM((z.s, z.f), BF16),
            pltpu.VMEM((z.n * z.ns, z.f), F32),
            pltpu.SemaphoreType.DMA((1 + z.groups,)),
        ],
        (*ins, terms, bc),
        flops=z.s * z.f * z.ns * 20,
        nbytes=z.s * z.f * 32,
    )


def ssd_back_kernel(z, *refs):
    n, t = z.n, z.t
    lengths, values, refs = refs[0], refs[1 : n + 1], refs[n + 1 :]
    terms, bc_in, refs = refs[0], refs[1], refs[2:]
    saved_in, refs = refs[0], refs[1:]
    grad_out, keep_out, give_out, step_out, vec, refs = *refs[:5], refs[5:]
    down, small, bc, saved, d, adds, dstates, through, grads, sems = refs
    mover = Copies(sems)

    def load(k):
        return [mover.start(saved_in.at[k], saved.at[k])]

    loads = load(2) + load(4) + [
        mover.start(bc_in, bc),
        mover.start(terms.at[pl.ds(z.mid, z.term_rows - z.mid)], small),
    ]
    later = load(3) + load(1)
    last = load(0) + load(5) + [mover.start(terms.at[pl.ds(z.down, z.s)], down)]
    me, core = lax.axis_index("context"), lax.axis_index("head")
    length = lengths[lax.axis_index("rollout")]
    value = values[0][...]
    for s in range(1, n):
        value = value + values[s][...]
    row_id, col_id = iota((t, t), 0), iota((t, t), 1)
    causal = row_id >= col_id
    strict = row_id > col_id
    after = mat(col_id >= row_id).astype(BF16)
    before = mat(strict).astype(BF16)
    per_head = mat(iota((z.f, t), 1) == iota((z.f, t), 0) // z.mp).astype(BF16)
    per_row = mat(iota((z.h * t, t), 1) == iota((z.h * t, t), 0) // t).astype(BF16)
    vec[...] = jnp.zeros_like(vec)
    wait_all(loads)

    def pays(c):
        return small[z.small(c, z.pay - z.mid, z.r), :t]

    def enter(c):
        rows = z.chunk(c)
        if z.static:
            value_row = value[:, c * t : (c + 1) * t]
        else:
            value_row = jnp.zeros((1, t), F32)
            for j in range(n):
                value_row = jnp.where(c == j, value[:, j * t : (j + 1) * t], value_row)
        valid = c * t + iota((1, t), 1) < length
        error = jnp.where(valid, value_row - pays(c)[z.h : z.h + 1], 0.0)
        vec[z.features + 1 : z.features + 2, :] += 0.5 * error * error
        column = jnp.transpose(jnp.broadcast_to(error, (t, t)))
        wide = jnp.concatenate([column] * (z.f // t), axis=1)
        dc = split3(wide * (saved[2, rows, :].astype(F32) + saved[4, rows, :].astype(F32)))[:2]
        d[0, rows, :] = dc[0]
        d[1, rows, :] = dc[1]
        adds[rows, :] = dot_tn(bc[c, 1], dc[0]) + dot_tn(bc[c, 1], dc[1])
        high, low = split3(error)[:2]
        pair = jnp.concatenate([high, low, jnp.zeros((6, t), BF16)], axis=0)
        weight_grad = dot(pair, saved[1, rows, :])
        weight_grad = weight_grad[0:1] + weight_grad[1:2]
        for a in range(z.features):
            vec[a : a + 1, :] += weight_grad[:, a * z.hd : (a + 1) * z.hd]

    wait_all(later)
    z.each_chunk(enter)

    def carry(c, dstate):
        m = small[z.small(c, 0, 8), :][0:1]
        rows = z.chunk(c)
        dstate = m * dstate
        dstates[rows, :] = dstate.astype(BF16)
        sums = jnp.sum(dstate * saved[3, rows, :].astype(F32), axis=0, keepdims=True)
        through[z.small(c, 0, 8), :] = jnp.broadcast_to(sums, (8, z.f))
        return m * (dstate + adds[rows, :])

    dstate = jnp.zeros((z.ns, z.f), F32)
    if z.static:
        for c in range(n - 1, -1, -1):
            dstate = carry(c, dstate)
    else:
        lax.fori_loop(0, n, lambda k, v: carry(n - 1 - k, v), dstate)
    wait_all(last)

    def leave(c):
        rows = z.chunk(c)
        b, cp, inner = bc[c, 0], bc[c, 1], bc[c, 2]
        dc, dl = d[0, rows, :], d[1, rows, :]
        xc, xl, state_in, dstate_in = saved[0, rows, :], saved[5, rows, :], saved[3, rows, :], dstates[rows, :]
        local = dot_tn(inner, dc) + dot_tn(inner, dl)
        outer = dot(b, dstate_in)
        carried = dot(cp, state_in)
        grads[rows, :] = (down[rows, :] * (local + outer)).astype(BF16)
        grad_c = dot_nt(dc, state_in) + dot_nt(dl, state_in)
        grad_b = dot_nt(xc, dstate_in)
        down_sum = dot(((dc.astype(F32) + dl.astype(F32)) * carried).astype(BF16), per_head)
        up_sum = dot((xc.astype(F32) * outer).astype(BF16), per_head)
        inner_wide = inner.astype(F32)
        w_sum = jnp.zeros((t, t), F32)
        parts = []
        for k in range(z.h):
            first = k * z.mp // z.hd * z.hd
            mine = iota((t, z.hd), 1) // z.mp == k % (z.hd // z.mp)
            pair = slice(first, first + z.hd)
            x_head = jnp.where(mine, xc[:, pair], jnp.zeros((), BF16))
            x_low = jnp.where(mine, xl[:, pair], jnp.zeros((), BF16))
            left = jnp.concatenate([dc[:, pair], dl[:, pair], dc[:, pair]], axis=1)
            w = jnp.where(causal, dot_nt(left, jnp.concatenate([x_head, x_head, x_low], axis=1)), 0.0)
            w_sum += w
            parts.append((w * inner_wide).astype(BF16))
        straddle = dot(after, jnp.concatenate(parts, axis=1))
        straddle = jnp.concatenate(
            [jnp.where(strict, straddle[:, k * t : (k + 1) * t], 0.0).astype(BF16) for k in range(z.h)], axis=1
        )
        sums = [*split3(down_sum)[:2], *split3(up_sum)[:2]]
        gain = dot(
            jnp.concatenate([after, after, before, before], axis=1), jnp.concatenate(sums, axis=0)
        ) + dot(straddle, per_row)
        gain = gain + split2_dot(through[z.small(c, 0, 8), :], per_head)[0:1]
        w_low = w_sum.astype(BF16)
        grad_c += dot(w_low, b)
        grad_b += dot_tn(w_low, cp)
        keep_out[c] = jnp.where(core == 0, grad_b, grad_c)
        give_out[c] = jnp.where(core == 0, grad_c, grad_b).astype(BF16)
        gain_rows = jnp.transpose(gain)[: z.r]
        step_out[c] = -small[z.rate - z.mid : z.rate - z.mid + z.r, :t] * gain_rows
        rate_part = jnp.sum(pays(c) * gain_rows, axis=1, keepdims=True)
        lane = (iota((z.r, t), 1) == me * z.h + iota((z.r, t), 0)) & (iota((z.r, t), 0) < z.h)
        vec[z.features : z.features + 1, :] -= jnp.sum(jnp.where(lane, rate_part, 0.0), axis=0, keepdims=True)

    z.each_chunk(leave)
    mover.start(grads, grad_out).wait()


def ssd_back(z, lengths, values, terms, bc, saved):
    outs = (
        SHAPE((z.s, z.f), BF16),
        SHAPE((z.n, z.t, z.ns), F32),
        SHAPE((z.n, z.t, z.ns), BF16),
        SHAPE((z.n, z.r, z.t), F32),
        SHAPE((z.v, z.t), F32),
    )
    scratch = [
        pltpu.VMEM((z.s, z.f), F32),
        pltpu.VMEM((z.term_rows - z.mid, z.f), F32),
        pltpu.VMEM((z.n, 4, z.t, z.ns), BF16),
        pltpu.VMEM((6, z.s, z.f), BF16),
        pltpu.VMEM((2, z.s, z.f), BF16),
        pltpu.VMEM((z.n * z.ns, z.f), F32),
        pltpu.VMEM((z.n * z.ns, z.f), BF16),
        pltpu.VMEM((z.n * 8, z.f), F32),
        pltpu.VMEM((z.s, z.f), BF16),
        pltpu.SemaphoreType.DMA((10,)),
    ]
    return call(
        z,
        ssd_back_kernel,
        "ssd_back",
        outs,
        [SM] + [VM] * z.n + [ANY] * 3,
        [ANY] + [VM] * 4,
        scratch,
        (lengths, *values, terms, bc, saved),
        flops=z.s * z.f * z.ns * 20,
        nbytes=z.s * z.f * 32,
    )


def attend_back_kernel(z, g, *refs):
    n, t, count = z.n, z.t, z.sizes[g]
    qkv, prob_in, grad_in, refs = *refs[:3], refs[3:]
    if g == 0:
        keep, other, step, vec, refs = *refs[:4], refs[4:]
    else:
        refs = refs[1:]
    outs, refs = refs[:n], refs[n:]
    held, prob, grad, result, dscore, sems = refs
    mover = Copies(sems)
    me = lax.axis_index("context")
    first = [mover.start(grad_in.at[:, z.lanes(g)], grad), mover.start(qkv, held)]
    probs = [mover.start(prob_in.at[a], prob.at[a]) for a in range(count)]
    if g == 0:
        end = 3 * count * t
        for j in range(n):
            result[j, end : end + t] = (keep[j] + other[j].astype(F32)).astype(BF16)
            result[j, end + t :] = jnp.zeros((z.rp + 2 * z.v, t), BF16)
            result[j, end + t : end + t + z.r] = step[j].astype(BF16)
            result[j, end + t + z.rp :] = jnp.concatenate(split3(vec[...])[:2], axis=0)
    wait_all(first)
    factor = 1.0 / math.sqrt(z.hd)
    per = z.rows // t

    def rows_span(k, a, first, last):
        return held[first // t : last // t, z.rows_of(g, k, a), :].reshape(last - first, z.hd)

    def store(k, a, i, x):
        result[pl.ds(i * per, per), z.rows_of(g, k, a), :] = x.astype(BF16).reshape(per, t, z.hd)

    for a in range(count):
        lanes = slice(a * z.hd, (a + 1) * z.hd)
        probs[a].wait()

        def by_query(i):
            width, rows = z.upto(i), z.block(i)
            p = prob[a, rows, :width].astype(F32)
            dp = dot_nt(grad[rows, lanes], rows_span(2, a, 0, width))
            product = p * dp
            ds = (product - p * jnp.sum(product, axis=1, keepdims=True)).astype(BF16)
            dscore[a, rows, :width] = ds
            store(0, a, i, dot(ds, rows_span(1, a, 0, width)) * factor)

        z.each_block(by_query)

        def by_key(j):
            start, cols = z.onward(j), z.block(j)
            store(1, a, j, dot_tn(dscore[a, start:, cols], rows_span(0, a, start, z.s)) * factor)
            store(2, a, j, dot_tn(prob[a, start:, cols], grad[start:, lanes]))

        z.each_block(by_key)
    wait_all([mover.start(result.at[lax.rem(me + s, n)], outs[s]) for s in range(n)])


def attend_back(z, g, qkv, prob, grad, small):
    count = z.sizes[g]
    rows = z.back_rows(g)
    scratch = [
        pltpu.VMEM((z.n, 3 * count * z.t, z.hd), BF16),
        pltpu.VMEM((count, z.s, z.s), BF16),
        pltpu.VMEM((z.s, count * z.hd), BF16),
        pltpu.VMEM((z.n, rows, z.hd), BF16),
        pltpu.VMEM((count, z.s, z.s), BF16),
        pltpu.SemaphoreType.DMA((2 + z.n + count,)),
    ]
    return call(
        z,
        lambda z, *refs: attend_back_kernel(z, g, *refs),
        "attend_back_%d" % g,
        [SHAPE((rows, z.hd), BF16)] * z.n,
        [ANY] * 3 + ([ANY] if g else [VM] * len(small)),
        [ANY] * z.n,
        scratch,
        (qkv, prob, grad, *small),
        flops=count * z.s * z.s * z.hd * 8,
        nbytes=count * z.s * z.s * 8,
    )


def unpack_kernel(z, *refs):
    n, t = z.n, z.t
    ins, (proj, step, vecs, parts, sems) = refs[:n], refs[n:]
    me = lax.axis_index("context")
    mover = Copies(sems)
    rows = pl.ds(3 * z.sizes[0] * t, t + z.rp + 2 * z.v)
    wait_all([mover.start(ins[s].at[rows], parts.at[s]) for s in range(n)])
    total = jnp.zeros((t, z.ns), F32)
    steps = jnp.zeros((n * z.h, t), F32)
    for s in range(n):
        total = total + parts[s, :t].astype(F32)
        source = lax.rem(me + n - s, n)
        row, col = iota((n * z.h, z.r), 0), iota((n * z.h, z.r), 1)
        place = mat((row == source * z.h + col) & (col < z.h)).astype(BF16)
        steps = steps + dot(place, parts[s, t : t + z.r])
        vec = parts[s, t + z.rp :].astype(F32)
        vecs[source] = vec[: z.v] + vec[z.v :]
    proj[...] = total
    step[0] = steps


def unpack(z, parts):
    return call(
        z,
        unpack_kernel,
        "unpack",
        (SHAPE((z.t, z.ns), F32), SHAPE((1, z.n * z.h, z.t), F32), SHAPE((z.n, z.v, z.t), F32)),
        [ANY] * z.n,
        [VM] * 3,
        [pltpu.VMEM((z.n, z.t + z.rp + 2 * z.v, z.t), BF16), pltpu.SemaphoreType.DMA((z.n,))],
        parts,
    )


def choose_kernel(z, lengths, mine, theirs, vecs, b, c, weight, rate, loss):
    core = lax.axis_index("head")
    b[0] = jnp.where(core == 0, mine[...], theirs[...])
    c[0] = jnp.where(core == 0, theirs[...], mine[...])
    valid = lengths[0]
    for k in range(1, lengths.shape[0]):
        valid = valid + lengths[k]
    rates = jnp.zeros((1, z.t), F32)
    for j in range(z.n):
        weight[j] = vecs[j, : z.features]
        rates = rates + vecs[j, z.features : z.features + 1]
    losses = vecs[0, z.features + 1 : z.features + 2]
    loss[...] = jnp.sum(losses, axis=1, keepdims=True) / valid.astype(F32)
    rate[...] = rates[:, : z.n * z.h]


def choose(z, lengths, mine, theirs, vecs):
    return call(
        z,
        choose_kernel,
        "choose",
        (
            SHAPE((1, z.t, z.ns), F32),
            SHAPE((1, z.t, z.ns), F32),
            SHAPE((z.n, z.features, z.hd), F32),
            SHAPE((1, z.n * z.h), F32),
            SHAPE((1, 1), F32),
        ),
        [SM] + [VM] * 3,
        [VM] * 5,
        [],
        (lengths, mine, theirs, vecs),
    )


def finish_kernel(z, *refs):
    count = z.n * z.groups
    ins, out, refs = refs[:count], refs[count + 1], refs[count + 2 :]
    held, (turned, sems) = refs[: z.groups], refs[z.groups :]
    me = lax.axis_index("context")
    mover = Copies(sems)
    loads = []
    for g in range(z.groups):
        for s in range(z.n):
            rows = pl.ds(0, 3 * z.sizes[g] * z.t)
            loads.append(mover.start(ins[g * z.n + s].at[rows], held[g].at[lax.rem(me + z.n - s, z.n)]))
    wait_all(loads)
    stores = []
    for k in range(3):
        heads = [
            held[g][j, z.rows_of(g, k, a), :]
            for j in range(z.n)
            for g in range(z.groups)
            for a in range(z.sizes[g])
        ]
        turned[k] = jnp.swapaxes(jnp.stack(heads), 0, 1)
        stores.append(mover.start(turned.at[k], out.at[k, 0]))
    wait_all(stores)


def finish(z, parts, after):
    return call(
        z,
        finish_kernel,
        "finish",
        SHAPE((3, 1, z.t, z.hl, z.hd), BF16),
        [ANY] * (z.n * z.groups + 1),
        ANY,
        [
            *[pltpu.VMEM((z.n, 3 * k * z.t, z.hd), BF16) for k in z.sizes],
            pltpu.VMEM((3, z.t, z.hl, z.hd), BF16),
            pltpu.SemaphoreType.DMA((z.n * z.groups + 3,)),
        ],
        (*parts, after),
        nbytes=12 * z.t * z.hl * z.hd,
    )


def shift(x, axis, size, step):
    return lax.ppermute(x, axis, [(i, (i + step) % size) for i in range(size)])


def spread(parts, axis):
    return [parts[0]] + [shift(x, axis, len(parts), s) for s, x in enumerate(parts) if s]


def local(qkv, ssd_b, ssd_c, step_size, decay_rate, value_weight, returns, step_labels, lengths):
    n = lax.axis_size("context")
    z = Sizes(n, qkv.shape[2], qkv.shape[3], qkv.shape[4], step_size.shape[2], ssd_b.shape[2])

    sends = prep(z, qkv, ssd_b, ssd_c, jnp.swapaxes(step_size, 1, 2), step_labels, returns)
    arrived = [spread(sends[g * n : (g + 1) * n], "context") for g in range(z.groups)]
    mine, pay = pick(z, arrived[0])
    theirs = shift(mine, "head", 2, 1)
    attended = [attend(z, 0, arrived[0], [])]
    terms, bc = decay(z, mine, theirs, pay, decay_rate.reshape(1, -1), value_weight.reshape(z.hl, z.hd))
    for g in range(1, z.groups):
        attended.append(attend(z, g, arrived[g], [bc]))
    saved, value = ssd(z, [x[1] for x in attended], terms, bc)
    value = value + shift(value, "head", 2, 1)
    values = spread([value] * n, "context")
    grad, keep, give, steps, vec = ssd_back(z, lengths, values, terms, bc, saved)
    finals, small = [], [keep, shift(give, "head", 2, 1), steps, vec]
    for g in range(z.groups):
        back = attend_back(z, g, attended[g][2], attended[g][0], grad, small)
        finals.append(spread(back, "context"))
        small = back[:1]
    proj, step_grad, vecs = unpack(z, finals[0])
    other = shift(proj, "head", 2, 1)
    step = 1
    while step < lax.axis_size("rollout"):
        pairs = [(i, i ^ step) for i in range(lax.axis_size("rollout"))]
        vecs = vecs + lax.ppermute(vecs, "rollout", pairs)
        step *= 2
    b_grad, c_grad, weight_grad, rate_grad, loss = choose(z, lengths, proj, other, vecs)
    qkv_grad = finish(z, [x for part in finals for x in part], rate_grad)
    return (
        loss.reshape(()),
        qkv_grad,
        b_grad,
        c_grad,
        jnp.swapaxes(step_grad, 1, 2),
        rate_grad.reshape(-1),
        weight_grad.reshape(-1),
    )


def solution(mesh):
    in_specs = (
        P(None, "rollout", "context", "head", None),
        P("rollout", "context", None),
        P("rollout", "context", None),
        P("rollout", "context", "head"),
        P("head"),
        P("head"),
        P("rollout", None),
        P("rollout", "context"),
        P(),
    )
    out_specs = (
        P(),
        P(None, "rollout", "context", "head", None),
        P("rollout", "context", None),
        P("rollout", "context", None),
        P("rollout", "context", "head"),
        P("head"),
        P("head"),
    )
    return jax.shard_map(local, mesh=mesh, in_specs=in_specs, out_specs=out_specs, check_vma=False)
```

time: 477 us -> 120 us (0.25)
  the two profiles are of different devices: /device:TPU:0 before, /device:TPU:10 now
where the time goes in v2:
time: 120 us
  waiting for transfers between devices  57.2 us (48%)
  Pallas kernels  35.1 us (29%)
  starting transfers between devices  25.8 us (22%)
    ppermute x19, waiting for transfers between devices, shift(): return lax.ppermute(x, axis, [(i, (i + step) % size) for i in range(size)])  51.8 us
    pallas_call x12, Pallas kernels, call(): pl.pallas_call(functools.partial(kernel, z), name=name, out_shape=out_sha...  35.1 us
    ppermute x19, starting transfers between devices, shift(): return lax.ppermute(x, axis, [(i, (i + step) % size) for i in range(size)])  23.7 us
    ppermute x2, waiting for transfers between devices, local(): vecs = vecs + lax.ppermute(vecs, 'rollout', pairs)  5.43 us
  transfers between devices with their start and end apart: 21, of which 13 were waited for; matrix products, arithmetic and copies ran while one was open for 0% of the time, Pallas kernels for 9%

profile of v2, /device:TPU:10, one launch (start us, length us, event | category | flops | bytes accessed | tf_op | source)
XLA Modules:
  0.0 119.8 jit_solution(15545025066961196177)
XLA Ops:
  0.7 4.5 %prep.1 = (bf16[928,128]{1,0:T(8,128)(2,1)S(1)}, bf16[928,128]{1,0:T(8,128)(2,1)S(1)}, bf16[928,128]{1,0:T(8,128)(2,1)S(1)}, bf16[928,128]{1,0:T(8,128)(2,1)S(1)...) custom-call(bf16[3,1,128,16,128]{4,3,2,1,0:T(8,128)(2,1)} %qkv.1, ...), custom_call_target="tpu_custom_call" | custom-call | bytes 3145728 | tf_op jit(solution)/shard_map/prep/pallas_call | solution.py:124
  5.2 1.6 %collective-permute-start = (bf16[928,128]{1,0:T(8,128)(2,1)S(1)}, bf16[928,128]{1,0:T(8,128)(2,1)S(1)}, u32[]{:S(2)}, u32[]{:S(2)}) collective-permute-start(bf16[928,128]{1,0:T(8,128)(2,1)S(1)} %get-tuple-element.49), channel_id=1, source_target_pairs={{0,2},{2,4},{4,6},{6,0},{1,3},{3,5},{5,7},{7,1},{8,10},{10,12},{12... | collective-permute-start | bytes 712712 | tf_op jit(solution)/shard_map/ppermute | solution.py:809
  6.8 1.2 %collective-permute-start.1 = (bf16[928,128]{1,0:T(8,128)(2,1)S(1)}, bf16[928,128]{1,0:T(8,128)(2,1)S(1)}, u32[]{:S(2)}, u32[]{:S(2)}) collective-permute-start(bf16[928,128]{1,0:T(8,128)(2,1)S(1)} %get-tuple-element.50), channel_id=1, source_target_pairs={{0,4},{2,6},{4,0},{6,2},{1,5},{3,7},{5,1},{7,3},{8,12},{10,14},{12... | collective-permute-start | bytes 712712 | tf_op jit(solution)/shard_map/ppermute | solution.py:809
  8.1 1.8 %collective-permute-start.2 = (bf16[928,128]{1,0:T(8,128)(2,1)S(1)}, bf16[928,128]{1,0:T(8,128)(2,1)S(1)}, u32[]{:S(2)}, u32[]{:S(2)}) collective-permute-start(bf16[928,128]{1,0:T(8,128)(2,1)S(1)} %get-tuple-element.51), channel_id=1, source_target_pairs={{0,6},{2,0},{4,2},{6,4},{1,7},{3,1},{5,3},{7,5},{8,14},{10,8},{12,... | collective-permute-start | bytes 712712 | tf_op jit(solution)/shard_map/ppermute | solution.py:809
  9.9 0.2 collective-permute-start.3
  10.1 3.5 %collective-permute-start.4 = (bf16[768,128]{1,0:T(8,128)(2,1)S(1)}, bf16[768,128]{1,0:T(8,128)(2,1)S(1)}, u32[]{:S(2)}, u32[]{:S(2)}) collective-permute-start(bf16[768,128]{1,0:T(8,128)(2,1)S(1)} %get-tuple-element.57), channel_id=1, source_target_pairs={{0,4},{2,6},{4,0},{6,2},{1,5},{3,7},{5,1},{7,3},{8,12},{10,14},{12... | collective-permute-start | bytes 589832 | tf_op jit(solution)/shard_map/ppermute | solution.py:809
  13.6 9.2 %collective-permute-done.refs_1_ = bf16[928,128]{1,0:T(8,128)(2,1)S(1)} collective-permute-done((bf16[928,128]{1,0:T(8,128)(2,1)S(1)}, bf16[928,128]{1,0:T(8,128)(2,1)S(1)}, u32[]{:S(2)}, u32[]{:S(2)}) %collective-permute-start) | collective-permute-done | bytes 237600 | tf_op jit(solution)/shard_map/ppermute | solution.py:809
  22.8 13.9 %collective-permute-done.1.refs_2_ = bf16[928,128]{1,0:T(8,128)(2,1)S(1)} collective-permute-done((bf16[928,128]{1,0:T(8,128)(2,1)S(1)}, bf16[928,128]{1,0:T(8,128)(2,1)S(1)}, u32[]{:S(2)}, u32[]{:S(2)}) %collective-permute-start.1) | collective-permute-done | bytes 237600 | tf_op jit(solution)/shard_map/ppermute | solution.py:809
  36.7 0.8 collective-permute-done.2.refs_3_
  37.5 0.2 pick.1
  37.7 0.1 collective-permute-start.6
  37.8 3.2 %attend_0.1 = (bf16[2,512,512]{2,1,0:T(8,128)(2,1)S(1)}, bf16[512,256]{1,0:T(8,128)(2,1)S(1)}, bf16[4,768,128]{2,1,0:T(8,128)(2,1)S(1)}) custom-call(bf16[928,128]{1,0:T(8,128)(2,1)S(1)} %get-tuple-element.48.refs_0_, bf16[928,128]{1,0:T(8,128)(2,1)S(1)} %collective-permute-done.refs_1_, bf16[928,128]{1,0:T(8,128)(2,1)S(1)} %collective-permute-done.1.refs_2_, ...), custom_call_target="tpu_custom_call" | custom-call | flops 268435456 | bytes 4194304 | tf_op jit(solution)/shard_map/attend_0/pallas_call | solution.py:124
  41.0 2.0 %decay.1 = (f32[1144,512]{1,0:T(8,128)S(1)}, bf16[4,4,128,128]{3,2,1,0:T(8,128)(2,1)S(1)}) custom-call(bf16[4,128,128]{2,1,0:T(8,128)(2,1)S(1)} %get-tuple-element.59.mine, bf16[4,128,128]{2,1,0:T(8,128)(2,1)S(1)} %collective-permute-done.6.theirs, f32[4,16,128]{2,1,0:T(8,128)S(1)} %get-tuple-element.60.pay, f32[1,32]{1,0:T(1,128)S(1)} %bitcast.8, ...), custom_call_target="tpu_custom_call" | custom-call | bytes 2097152 | tf_op jit(solution)/shard_map/decay/pallas_call | solution.py:124
  43.1 0.0 collective-permute-done.3.refs_1_
  43.1 0.9 collective-permute-done.4.refs_2_
  44.0 1.8 %collective-permute-done.5.refs_3_ = bf16[768,128]{1,0:T(8,128)(2,1)S(1)} collective-permute-done((bf16[768,128]{1,0:T(8,128)(2,1)S(1)}, bf16[768,128]{1,0:T(8,128)(2,1)S(1)}, u32[]{:S(2)}, u32[]{:S(2)}) %collective-permute-start.5) | collective-permute-done | bytes 196640 | tf_op jit(solution)/shard_map/ppermute | solution.py:809
  45.8 3.2 %attend_1.1 = (bf16[2,512,512]{2,1,0:T(8,128)(2,1)S(1)}, bf16[512,256]{1,0:T(8,128)(2,1)S(1)}, bf16[4,768,128]{2,1,0:T(8,128)(2,1)S(1)}) custom-call(bf16[768,128]{1,0:T(8,128)(2,1)S(1)} %get-tuple-element.55.refs_0_, bf16[768,128]{1,0:T(8,128)(2,1)S(1)} %collective-permute-done.3.refs_1_, bf16[768,128]{1,0:T(8,128)(2,1)S(1)} %collective-permute-done.4.refs_2_, ...), custom_call_target="tpu_custom_call" | custom-call | flops 268435456 | bytes 4194304 | tf_op jit(solution)/shard_map/attend_1/pallas_call | solution.py:124
  49.0 3.0 %ssd.1 = (bf16[6,512,512]{2,1,0:T(8,128)(2,1)S(1)}, f32[1,512]{1,0:T(1,128)S(1)}) custom-call(bf16[512,256]{1,0:T(8,128)(2,1)S(1)} %get-tuple-element.54.refs_0_, bf16[512,256]{1,0:T(8,128)(2,1)S(1)} %get-tuple-element.62.refs_1_, f32[1144,512]{1,0:T(8,128)S(1)} %get-tuple-element.63.refs_2_.refs_5_, ...), custom_call_target="tpu_custom_call" | custom-call | flops 671088640 | bytes 8388608 | tf_op jit(solution)/shard_map/ssd/pallas_call | solution.py:124
  52.0 0.1 collective-permute-start.7
  52.1 1.1 collective-permute-done.7
  53.2 1.6 %collective-permute-start.9 = (f32[1,512]{1,0:T(1,128)S(1)}, f32[1,512]{1,0:T(1,128)S(1)}, u32[]{:S(2)}, u32[]{:S(2)}) collective-permute-start(f32[1,512]{1,0:T(1,128)S(1)} %add.9.refs_1_), channel_id=1, source_target_pairs={{0,4},{2,6},{4,0},{6,2},{1,5},{3,7},{5,1},{7,3},{8,12},{10,14},{12... | collective-permute-start | bytes 6152 | tf_op jit(solution)/shard_map/ppermute | solution.py:809
  54.9 2.9 %collective-permute-start.8 = (f32[1,512]{1,0:T(1,128)S(1)}, f32[1,512]{1,0:T(1,128)S(1)}, u32[]{:S(2)}, u32[]{:S(2)}) collective-permute-start(f32[1,512]{1,0:T(1,128)S(1)} %add.9.refs_1_), channel_id=1, source_target_pairs={{0,2},{2,4},{4,6},{6,0},{1,3},{3,5},{5,7},{7,1},{8,10},{10,12},{12... | collective-permute-start | bytes 6152 | tf_op jit(solution)/shard_map/ppermute | solution.py:809
  57.7 0.0 collective-permute-done.10.refs_4_
  57.7 0.1 collective-permute-done.9.refs_3_
  57.8 1.2 %collective-permute-done.8.refs_2_ = f32[1,512]{1,0:T(1,128)S(1)} collective-permute-done((f32[1,512]{1,0:T(1,128)S(1)}, f32[1,512]{1,0:T(1,128)S(1)}, u32[]{:S(2)}, u32[]{:S(2)}) %collective-permute-start.8) | collective-permute-done | bytes 2080 | tf_op jit(solution)/shard_map/ppermute | solution.py:809
  59.0 6.7 %ssd_back.1 = (bf16[512,512]{1,0:T(8,128)(2,1)S(1)}, f32[4,128,128]{2,1,0:T(8,128)S(1)}, bf16[4,128,128]{2,1,0:T(8,128)(2,1)S(1)}, f32[4,16,128]{2,1,0:T(8,128)S(1)}, f32[8,128]{1,0:T(8,128)S(1)}) custom-call(s32[4]{0:T(128)S(1)} %copy-done.1, f32[1,512]{1,0:T(1,128)S(1)} %add.9.refs_1_, f32[1,512]{1,0:T(1,128)S(1)} %collective-permute-done.8.refs_2_, ...), custom_call_target="tpu_custom_call" | custom-call | flops 671088640 | bytes 8388608 | tf_op jit(solution)/shard_map/ssd_back/pallas_call | solution.py:124
  65.8 0.1 collective-permute-start.11
  65.9 1.3 %collective-permute-done.11.refs_4_ = bf16[4,128,128]{2,1,0:T(8,128)(2,1)S(1)} collective-permute-done((bf16[4,128,128]{2,1,0:T(8,128)(2,1)S(1)}, bf16[4,128,128]{2,1,0:T(8,128)(2,1)S(1)}, u32[]{:S(2)}, u32[]{:S(2)}) %collective-permute-start.11) | collective-permute-done | bytes 131104 | tf_op jit(solution)/shard_map/ppermute | solution.py:809
  67.2 3.4 %attend_back_0.1 = (bf16[928,128]{1,0:T(8,128)(2,1)S(1)}, bf16[928,128]{1,0:T(8,128)(2,1)S(1)}, bf16[928,128]{1,0:T(8,128)(2,1)S(1)}, bf16[928,128]{1,0:T(8,128)(2,1)S(1)}) custom-call(bf16[4,768,128]{2,1,0:T(8,128)(2,1)S(1)} %get-tuple-element.52.refs_0_, bf16[2,512,512]{2,1,0:T(8,128)(2,1)S(1)} %get-tuple-element.53.refs_1_, ...), custom_call_target="tpu_custom_call" | custom-call | flops 536870912 | bytes 4194304 | tf_op jit(solution)/shard_map/attend_back_0/pallas_call | solution.py:124
  70.6 2.3 %collective-permute-start.12 = (bf16[928,128]{1,0:T(8,128)(2,1)S(1)}, bf16[928,128]{1,0:T(8,128)(2,1)S(1)}, u32[]{:S(2)}, u32[]{:S(2)}) collective-permute-start(bf16[928,128]{1,0:T(8,128)(2,1)S(1)} %get-tuple-element.72), channel_id=1, source_target_pairs={{0,2},{2,4},{4,6},{6,0},{1,3},{3,5},{5,7},{7,1},{8,10},{10,12},{12... | collective-permute-start | bytes 712712 | tf_op jit(solution)/shard_map/ppermute | solution.py:809
  72.9 3.2 %collective-permute-start.13 = (bf16[928,128]{1,0:T(8,128)(2,1)S(1)}, bf16[928,128]{1,0:T(8,128)(2,1)S(1)}, u32[]{:S(2)}, u32[]{:S(2)}) collective-permute-start(bf16[928,128]{1,0:T(8,128)(2,1)S(1)} %get-tuple-element.73), channel_id=1, source_target_pairs={{0,4},{2,6},{4,0},{6,2},{1,5},{3,7},{5,1},{7,3},{8,12},{10,14},{12... | collective-permute-start | bytes 712712 | tf_op jit(solution)/shard_map/ppermute | solution.py:809
  76.1 0.0 collective-permute-start.14
  76.1 3.2 %attend_back_1.1 = (bf16[768,128]{1,0:T(8,128)(2,1)S(1)}, bf16[768,128]{1,0:T(8,128)(2,1)S(1)}, bf16[768,128]{1,0:T(8,128)(2,1)S(1)}, bf16[768,128]{1,0:T(8,128)(2,1)S(1)}) custom-call(bf16[4,768,128]{2,1,0:T(8,128)(2,1)S(1)} %get-tuple-element.78.refs_0_, bf16[2,512,512]{2,1,0:T(8,128)(2,1)S(1)} %get-tuple-element.79.refs_1_, ...), custom_call_target="tpu_custom_call" | custom-call | flops 536870912 | bytes 4194304 | tf_op jit(solution)/shard_map/attend_back_1/pallas_call | solution.py:124
  79.3 2.1 %collective-permute-start.18 = (bf16[768,128]{1,0:T(8,128)(2,1)S(1)}, bf16[768,128]{1,0:T(8,128)(2,1)S(1)}, u32[]{:S(2)}, u32[]{:S(2)}) collective-permute-start(bf16[768,128]{1,0:T(8,128)(2,1)S(1)} %get-tuple-element.81), channel_id=1, source_target_pairs={{0,2},{2,4},{4,6},{6,0},{1,3},{3,5},{5,7},{7,1},{8,10},{10,12},{12... | collective-permute-start | bytes 589832 | tf_op jit(solution)/shard_map/ppermute | solution.py:809
  81.4 1.8 %collective-permute-start.19 = (bf16[768,128]{1,0:T(8,128)(2,1)S(1)}, bf16[768,128]{1,0:T(8,128)(2,1)S(1)}, u32[]{:S(2)}, u32[]{:S(2)}) collective-permute-start(bf16[768,128]{1,0:T(8,128)(2,1)S(1)} %get-tuple-element.82), channel_id=1, source_target_pairs={{0,4},{2,6},{4,0},{6,2},{1,5},{3,7},{5,1},{7,3},{8,12},{10,14},{12... | collective-permute-start | bytes 589832 | tf_op jit(solution)/shard_map/ppermute | solution.py:809
  83.2 1.1 collective-permute-start.20
  84.3 18.5 %collective-permute-done.13.refs_2_ = bf16[928,128]{1,0:T(8,128)(2,1)S(1)} collective-permute-done((bf16[928,128]{1,0:T(8,128)(2,1)S(1)}, bf16[928,128]{1,0:T(8,128)(2,1)S(1)}, u32[]{:S(2)}, u32[]{:S(2)}) %collective-permute-start.13) | collective-permute-done | bytes 237600 | tf_op jit(solution)/shard_map/ppermute | solution.py:809
  102.8 2.9 %collective-permute-done.14.refs_3_ = bf16[928,128]{1,0:T(8,128)(2,1)S(1)} collective-permute-done((bf16[928,128]{1,0:T(8,128)(2,1)S(1)}, bf16[928,128]{1,0:T(8,128)(2,1)S(1)}, u32[]{:S(2)}, u32[]{:S(2)}) %collective-permute-start.14) | collective-permute-done | bytes 237600 | tf_op jit(solution)/shard_map/ppermute | solution.py:809
  105.7 1.0 unpack.1
  106.7 0.1 collective-permute-start.15
  106.7 0.6 collective-permute-start.16
  107.3 3.2 %collective-permute-done.16 = f32[4,8,128]{2,1,0:T(8,128)S(1)} collective-permute-done((f32[4,8,128]{2,1,0:T(8,128)S(1)}, f32[4,8,128]{2,1,0:T(8,128)S(1)}, u32[]{:S(2)}, u32[]{:S(2)}) %collective-permute-start.16) | collective-permute-done | bytes 16416 | tf_op jit(solution)/shard_map/ppermute | solution.py:842
  110.6 1.5 %collective-permute-start.17 = (f32[4,8,128]{2,1,0:T(8,128)S(1)}, f32[4,8,128]{2,1,0:T(8,128)S(1)}, u32[]{:S(2)}, u32[]{:S(2)}) collective-permute-start(f32[4,8,128]{2,1,0:T(8,128)S(1)} %add.10), channel_id=1, source_target_pairs={{0,16},{8,24},{16,0},{24,8},{1,17},{9,25},{17,1},{25,9},{2,18},{10... | collective-permute-start | bytes 49160 | tf_op jit(solution)/shard_map/ppermute | solution.py:842
  112.1 2.2 %collective-permute-done.17 = f32[4,8,128]{2,1,0:T(8,128)S(1)} collective-permute-done((f32[4,8,128]{2,1,0:T(8,128)S(1)}, f32[4,8,128]{2,1,0:T(8,128)S(1)}, u32[]{:S(2)}, u32[]{:S(2)}) %collective-permute-start.17) | collective-permute-done | bytes 16416 | tf_op jit(solution)/shard_map/ppermute | solution.py:842
  114.3 1.2 %choose.1 = (f32[1,128,128]{2,1,0:T(8,128)}, f32[1,128,128]{2,1,0:T(8,128)}, f32[4,4,128]{2,1,0:T(4,128)}, f32[1,32]{1,0:T(1,128)}, f32[1,1]{1,0:T(1,128)}) custom-call(s32[4]{0:T(128)S(1)} %copy-done.1, f32[128,128]{1,0:T(8,128)S(1)} %get-tuple-element.75.mine, f32[128,128]{1,0:T(8,128)S(1)} %collective-permute-done.15.theirs, f32[4,8,128]{2,1,0:T(8,128)S(1)} %add.11.vecs), custom_call_target="tpu_custom_call" | custom-call | tf_op jit(solution)/shard_map/choose/pallas_call | solution.py:124
  115.5 0.0 copy-start.3
  115.5 0.6 copy-done.3
  116.2 3.4 %finish.1 = bf16[3,1,128,16,128]{4,3,2,1,0:T(8,128)(2,1)} custom-call(bf16[928,128]{1,0:T(8,128)(2,1)S(1)} %get-tuple-element.71.refs_0_.refs_3_, bf16[928,128]{1,0:T(8,128)(2,1)S(1)} %collective-permute-done.12.refs_1_, bf16[928,128]{1,0:T(8,128)(2,1)S(1)} %collective-permute-done.13.refs_2_, bf16[928,128]{1,0:T(8,128)(2,1)S(1)} %collective-permute-done.14.refs_3_, ...), custom_call_target="tpu_custom_call" | custom-call | bytes 3145728 | tf_op jit(solution)/shard_map/finish/pallas_call | solution.py:124
  (17 shorter events, 0.0 us)
Async XLA Ops:
  0.6 40.4 %copy-start = (bf16[2048]{0:T(1024)(128)(2,1)S(1)}, bf16[2048]{0:T(1024)(128)(2,1)}, u32[]{:S(2)}) copy-start(bf16[2048]{0:T(1024)(128)(2,1)} %param.14) | copy-start | bytes 12292
  0.6 40.4 %copy-start.2 = (f32[32]{0:T(128)S(1)}, f32[32]{0:T(128)}, u32[]{:S(2)}) copy-start(f32[32]{0:T(128)} %param.13) | copy-start | bytes 388
  5.2 17.6 %collective-permute-start = (bf16[928,128]{1,0:T(8,128)(2,1)S(1)}, bf16[928,128]{1,0:T(8,128)(2,1)S(1)}, u32[]{:S(2)}, u32[]{:S(2)}) collective-permute-start(bf16[928,128]{1,0:T(8,128)(2,1)S(1)} %get-tuple-element.49), channel_id=1, source_target_pairs={{0,2},{2,4},{4,6},{6,0},{1,3},{3,5},{5,7},{7,1},{8,10},{10,12},{12... | collective-permute-start | bytes 712712 | tf_op jit(solution)/shard_map/ppermute | solution.py:809
  6.8 29.9 %collective-permute-start.1 = (bf16[928,128]{1,0:T(8,128)(2,1)S(1)}, bf16[928,128]{1,0:T(8,128)(2,1)S(1)}, u32[]{:S(2)}, u32[]{:S(2)}) collective-permute-start(bf16[928,128]{1,0:T(8,128)(2,1)S(1)} %get-tuple-element.50), channel_id=1, source_target_pairs={{0,4},{2,6},{4,0},{6,2},{1,5},{3,7},{5,1},{7,3},{8,12},{10,14},{12... | collective-permute-start | bytes 712712 | tf_op jit(solution)/shard_map/ppermute | solution.py:809
  8.1 29.4 %collective-permute-start.2 = (bf16[928,128]{1,0:T(8,128)(2,1)S(1)}, bf16[928,128]{1,0:T(8,128)(2,1)S(1)}, u32[]{:S(2)}, u32[]{:S(2)}) collective-permute-start(bf16[928,128]{1,0:T(8,128)(2,1)S(1)} %get-tuple-element.51), channel_id=1, source_target_pairs={{0,6},{2,0},{4,2},{6,4},{1,7},{3,1},{5,3},{7,5},{8,14},{10,8},{12,... | collective-permute-start | bytes 712712 | tf_op jit(solution)/shard_map/ppermute | solution.py:809
  9.9 33.2 %collective-permute-start.3 = (bf16[768,128]{1,0:T(8,128)(2,1)S(1)}, bf16[768,128]{1,0:T(8,128)(2,1)S(1)}, u32[]{:S(2)}, u32[]{:S(2)}) collective-permute-start(bf16[768,128]{1,0:T(8,128)(2,1)S(1)} %get-tuple-element.56), channel_id=1, source_target_pairs={{0,2},{2,4},{4,6},{6,0},{1,3},{3,5},{5,7},{7,1},{8,10},{10,12},{12... | collective-permute-start | bytes 589832 | tf_op jit(solution)/shard_map/ppermute | solution.py:809
  10.1 33.9 %collective-permute-start.4 = (bf16[768,128]{1,0:T(8,128)(2,1)S(1)}, bf16[768,128]{1,0:T(8,128)(2,1)S(1)}, u32[]{:S(2)}, u32[]{:S(2)}) collective-permute-start(bf16[768,128]{1,0:T(8,128)(2,1)S(1)} %get-tuple-element.57), channel_id=1, source_target_pairs={{0,4},{2,6},{4,0},{6,2},{1,5},{3,7},{5,1},{7,3},{8,12},{10,14},{12... | collective-permute-start | bytes 589832 | tf_op jit(solution)/shard_map/ppermute | solution.py:809
  22.8 23.1 %collective-permute-start.5 = (bf16[768,128]{1,0:T(8,128)(2,1)S(1)}, bf16[768,128]{1,0:T(8,128)(2,1)S(1)}, u32[]{:S(2)}, u32[]{:S(2)}) collective-permute-start(bf16[768,128]{1,0:T(8,128)(2,1)S(1)} %get-tuple-element.58), channel_id=1, source_target_pairs={{0,6},{2,0},{4,2},{6,4},{1,7},{3,1},{5,3},{7,5},{8,14},{10,8},{12,... | collective-permute-start | bytes 589832 | tf_op jit(solution)/shard_map/ppermute | solution.py:809
  37.7 3.3 %collective-permute-start.6 = (bf16[4,128,128]{2,1,0:T(8,128)(2,1)S(1)}, bf16[4,128,128]{2,1,0:T(8,128)(2,1)S(1)}, u32[]{:S(2)}, u32[]{:S(2)}) collective-permute-start(bf16[4,128,128]{2,1,0:T(8,128)(2,1)S(1)} %get-tuple-element.59.mine), channel_id=1, source_target_pairs={{0,1},{1,0},{2,3},{3,2},{4,5},{5,4},{6,7},{7,6},{8,9},{9,8},{10,11... | collective-permute-start | bytes 393224 | tf_op jit(solution)/shard_map/ppermute | solution.py:809
  45.8 13.2 %copy-start.1 = (s32[4]{0:T(128)S(1)}, s32[4]{0:T(128)}, u32[]{:S(2)}) copy-start(s32[4]{0:T(128)} %lengths.1) | copy-start | bytes 52
  52.0 1.2 %collective-permute-start.7 = (f32[1,512]{1,0:T(1,128)S(1)}, f32[1,512]{1,0:T(1,128)S(1)}, u32[]{:S(2)}, u32[]{:S(2)}) collective-permute-start(f32[1,512]{1,0:T(1,128)S(1)} %get-tuple-element.64), channel_id=1, source_target_pairs={{0,1},{1,0},{2,3},{3,2},{4,5},{5,4},{6,7},{7,6},{8,9},{9,8},{10,11... | collective-permute-start | bytes 6152 | tf_op jit(solution)/shard_map/ppermute | solution.py:809
  53.2 4.5 %collective-permute-start.10 = (f32[1,512]{1,0:T(1,128)S(1)}, f32[1,512]{1,0:T(1,128)S(1)}, u32[]{:S(2)}, u32[]{:S(2)}) collective-permute-start(f32[1,512]{1,0:T(1,128)S(1)} %add.9.refs_1_), channel_id=1, source_target_pairs={{0,6},{2,0},{4,2},{6,4},{1,7},{3,1},{5,3},{7,5},{8,14},{10,8},{12,... | collective-permute-start | bytes 6152 | tf_op jit(solution)/shard_map/ppermute | solution.py:809
  53.2 4.5 %collective-permute-start.9 = (f32[1,512]{1,0:T(1,128)S(1)}, f32[1,512]{1,0:T(1,128)S(1)}, u32[]{:S(2)}, u32[]{:S(2)}) collective-permute-start(f32[1,512]{1,0:T(1,128)S(1)} %add.9.refs_1_), channel_id=1, source_target_pairs={{0,4},{2,6},{4,0},{6,2},{1,5},{3,7},{5,1},{7,3},{8,12},{10,14},{12... | collective-permute-start | bytes 6152 | tf_op jit(solution)/shard_map/ppermute | solution.py:809
  54.9 4.2 %collective-permute-start.8 = (f32[1,512]{1,0:T(1,128)S(1)}, f32[1,512]{1,0:T(1,128)S(1)}, u32[]{:S(2)}, u32[]{:S(2)}) collective-permute-start(f32[1,512]{1,0:T(1,128)S(1)} %add.9.refs_1_), channel_id=1, source_target_pairs={{0,2},{2,4},{4,6},{6,0},{1,3},{3,5},{5,7},{7,1},{8,10},{10,12},{12... | collective-permute-start | bytes 6152 | tf_op jit(solution)/shard_map/ppermute | solution.py:809
  65.8 1.4 %collective-permute-start.11 = (bf16[4,128,128]{2,1,0:T(8,128)(2,1)S(1)}, bf16[4,128,128]{2,1,0:T(8,128)(2,1)S(1)}, u32[]{:S(2)}, u32[]{:S(2)}) collective-permute-start(bf16[4,128,128]{2,1,0:T(8,128)(2,1)S(1)} %get-tuple-element.68), channel_id=1, source_target_pairs={{0,1},{1,0},{2,3},{3,2},{4,5},{5,4},{6,7},{7,6},{8,9},{9,8},{10,11... | collective-permute-start | bytes 393224 | tf_op jit(solution)/shard_map/ppermute | solution.py:809
  70.6 12.6 %collective-permute-start.12 = (bf16[928,128]{1,0:T(8,128)(2,1)S(1)}, bf16[928,128]{1,0:T(8,128)(2,1)S(1)}, u32[]{:S(2)}, u32[]{:S(2)}) collective-permute-start(bf16[928,128]{1,0:T(8,128)(2,1)S(1)} %get-tuple-element.72), channel_id=1, source_target_pairs={{0,2},{2,4},{4,6},{6,0},{1,3},{3,5},{5,7},{7,1},{8,10},{10,12},{12... | collective-permute-start | bytes 712712 | tf_op jit(solution)/shard_map/ppermute | solution.py:809
  72.9 29.8 %collective-permute-start.13 = (bf16[928,128]{1,0:T(8,128)(2,1)S(1)}, bf16[928,128]{1,0:T(8,128)(2,1)S(1)}, u32[]{:S(2)}, u32[]{:S(2)}) collective-permute-start(bf16[928,128]{1,0:T(8,128)(2,1)S(1)} %get-tuple-element.73), channel_id=1, source_target_pairs={{0,4},{2,6},{4,0},{6,2},{1,5},{3,7},{5,1},{7,3},{8,12},{10,14},{12... | collective-permute-start | bytes 712712 | tf_op jit(solution)/shard_map/ppermute | solution.py:809
  76.1 29.6 %collective-permute-start.14 = (bf16[928,128]{1,0:T(8,128)(2,1)S(1)}, bf16[928,128]{1,0:T(8,128)(2,1)S(1)}, u32[]{:S(2)}, u32[]{:S(2)}) collective-permute-start(bf16[928,128]{1,0:T(8,128)(2,1)S(1)} %get-tuple-element.74), channel_id=1, source_target_pairs={{0,6},{2,0},{4,2},{6,4},{1,7},{3,1},{5,3},{7,5},{8,14},{10,8},{12,... | collective-permute-start | bytes 712712 | tf_op jit(solution)/shard_map/ppermute | solution.py:809
  79.3 36.2 %collective-permute-start.18 = (bf16[768,128]{1,0:T(8,128)(2,1)S(1)}, bf16[768,128]{1,0:T(8,128)(2,1)S(1)}, u32[]{:S(2)}, u32[]{:S(2)}) collective-permute-start(bf16[768,128]{1,0:T(8,128)(2,1)S(1)} %get-tuple-element.81), channel_id=1, source_target_pairs={{0,2},{2,4},{4,6},{6,0},{1,3},{3,5},{5,7},{7,1},{8,10},{10,12},{12... | collective-permute-start | bytes 589832 | tf_op jit(solution)/shard_map/ppermute | solution.py:809
  81.4 34.1 %collective-permute-start.19 = (bf16[768,128]{1,0:T(8,128)(2,1)S(1)}, bf16[768,128]{1,0:T(8,128)(2,1)S(1)}, u32[]{:S(2)}, u32[]{:S(2)}) collective-permute-start(bf16[768,128]{1,0:T(8,128)(2,1)S(1)} %get-tuple-element.82), channel_id=1, source_target_pairs={{0,4},{2,6},{4,0},{6,2},{1,5},{3,7},{5,1},{7,3},{8,12},{10,14},{12... | collective-permute-start | bytes 589832 | tf_op jit(solution)/shard_map/ppermute | solution.py:809
  83.2 32.3 %collective-permute-start.20 = (bf16[768,128]{1,0:T(8,128)(2,1)S(1)}, bf16[768,128]{1,0:T(8,128)(2,1)S(1)}, u32[]{:S(2)}, u32[]{:S(2)}) collective-permute-start(bf16[768,128]{1,0:T(8,128)(2,1)S(1)} %get-tuple-element.83), channel_id=1, source_target_pairs={{0,6},{2,0},{4,2},{6,4},{1,7},{3,1},{5,3},{7,5},{8,14},{10,8},{12,... | collective-permute-start | bytes 589832 | tf_op jit(solution)/shard_map/ppermute | solution.py:809
  106.7 7.6 %collective-permute-start.15 = (f32[128,128]{1,0:T(8,128)S(1)}, f32[128,128]{1,0:T(8,128)S(1)}, u32[]{:S(2)}, u32[]{:S(2)}) collective-permute-start(f32[128,128]{1,0:T(8,128)S(1)} %get-tuple-element.75.mine), channel_id=1, source_target_pairs={{0,1},{1,0},{2,3},{3,2},{4,5},{5,4},{6,7},{7,6},{8,9},{9,8},{10,11... | collective-permute-start | bytes 196616 | tf_op jit(solution)/shard_map/ppermute | solution.py:809
  106.7 3.8 %collective-permute-start.16 = (f32[4,8,128]{2,1,0:T(8,128)S(1)}, f32[4,8,128]{2,1,0:T(8,128)S(1)}, u32[]{:S(2)}, u32[]{:S(2)}) collective-permute-start(f32[4,8,128]{2,1,0:T(8,128)S(1)} %get-tuple-element.76), channel_id=1, source_target_pairs={{0,8},{8,0},{16,24},{24,16},{1,9},{9,1},{17,25},{25,17},{2,10},{10... | collective-permute-start | bytes 49160 | tf_op jit(solution)/shard_map/ppermute | solution.py:842
  110.6 3.7 %collective-permute-start.17 = (f32[4,8,128]{2,1,0:T(8,128)S(1)}, f32[4,8,128]{2,1,0:T(8,128)S(1)}, u32[]{:S(2)}, u32[]{:S(2)}) collective-permute-start(f32[4,8,128]{2,1,0:T(8,128)S(1)} %add.10), channel_id=1, source_target_pairs={{0,16},{8,24},{16,0},{24,8},{1,17},{9,25},{17,1},{25,9},{2,18},{10... | collective-permute-start | bytes 49160 | tf_op jit(solution)/shard_map/ppermute | solution.py:842
  115.5 0.7 copy-start.3

commit v3 on v2

--- a/solution.py
+++ b/solution.py
@@ -13,6 +13,7 @@
 HIGHEST = lax.Precision.HIGHEST
 LOG2E = 1.4426950408889634
 GROUPS = (2, 2)
+VMEM_MIB = 24
 F32 = jnp.float32
 BF16 = jnp.bfloat16
 
@@ -46,6 +47,8 @@
     def __init__(self, n, tokens, heads_local, head_dim, ssd_local, state):
         self.n, self.t, self.hl, self.hd, self.ns = n, tokens, heads_local, head_dim, state
         self.s = n * tokens
+        self.shifts = list(range(n))
+        self.back_shifts = sorted(range(n), key=lambda s: (min(s, n - s), s))
         self.a = heads_local // n
         self.sizes = GROUPS if sum(GROUPS) == self.a else (self.a,)
         self.first = [sum(self.sizes[:g]) for g in range(len(self.sizes))]
@@ -128,7 +131,7 @@
         in_specs=in_specs,
         out_specs=out_specs,
         scratch_shapes=scratch,
-        compiler_params=pltpu.CompilerParams(vmem_limit_bytes=(14 if z.static else 56) * 1024 * 1024),
+        compiler_params=pltpu.CompilerParams(vmem_limit_bytes=(VMEM_MIB if z.static else 56) * 1024 * 1024),
         cost_estimate=pl.CostEstimate(flops=flops, bytes_accessed=nbytes, transcendentals=0),
     )(*args)
 
@@ -170,7 +173,6 @@
     held, (parts, b, c, step, labels, table, sems) = refs[: z.groups], refs[z.groups :]
     me, core = lax.axis_index("context"), lax.axis_index("head")
     mover = Copies(sems)
-    loads = [mover.start(qkv.at[k, 0], parts.at[k]) for k in range(3)]
     tiny = [
         mover.start(b_in.at[0], b),
         mover.start(c_in.at[0], c),
@@ -178,6 +180,7 @@
         mover.start(labels_in, labels),
         mover.start(table_in, table),
     ]
+    loads = [mover.start(qkv.at[k, 0], parts.at[k]) for k in range(3)]
     wait_all(tiny)
     onehot = mat(iota((table.shape[1], z.t), 0) == labels[...])
     target = dot(table[...], onehot, HIGHEST)
@@ -200,11 +203,9 @@
             for j in range(z.n):
                 for a in range(z.sizes[g]):
                     held[g][j, z.rows_of(g, k, a), :] = turned[j * z.a + z.first[g] + a]
-    copies = []
     for g in range(z.groups):
         for s in range(z.n):
-            copies.append(mover.start(held[g].at[lax.rem(me + s, z.n)], outs[g * z.n + s]))
-    wait_all(copies)
+            outs[g * z.n + s][...] = held[g][lax.rem(me + z.shifts[s], z.n)]
 
 
 def prep(z, qkv, b, c, step, labels, table):
@@ -215,7 +216,7 @@
         "prep",
         [SHAPE((z.sent_rows(g), z.hd), BF16) for g in range(z.groups) for _ in range(z.n)],
         [ANY] * 6,
-        [ANY] * (z.n * z.groups),
+        [VM] * (z.n * z.groups),
         [
             *[pltpu.VMEM((z.n, z.sent_rows(g), z.hd), BF16) for g in range(z.groups)],
             pltpu.VMEM((3, z.t, z.hl, z.hd), BF16),
@@ -224,7 +225,7 @@
             pltpu.VMEM(step.shape[1:], F32),
             pltpu.VMEM(labels.shape, jnp.int32),
             pltpu.VMEM(table.shape, F32),
-            pltpu.SemaphoreType.DMA((8 + z.n * z.groups,)),
+            pltpu.SemaphoreType.DMA((8,)),
         ],
         args,
         nbytes=qkv.size * 4,
@@ -232,15 +233,14 @@
 
 
 def pick_kernel(z, *refs):
-    ins, (mine, pay, parts, sems) = refs[: z.n], refs[z.n :]
+    ins, (mine, pay) = refs[: z.n], refs[z.n :]
     me = lax.axis_index("context")
-    mover = Copies(sems)
-    rows = pl.ds(3 * z.sizes[0] * z.t, z.pay_rows)
-    wait_all([mover.start(ins[s].at[rows], parts.at[s]) for s in range(z.n)])
+    first = 3 * z.sizes[0] * z.t
     for s in range(z.n):
-        source = lax.rem(me + z.n - s, z.n)
-        mine[source] = parts[s, : z.t]
-        terms = [parts[s, z.t + k * z.rp : z.t + k * z.rp + z.r].astype(F32) for k in range(2)]
+        source = lax.rem(me + z.n - z.shifts[s], z.n)
+        mine[source] = ins[s][first : first + z.t]
+        start = first + z.t
+        terms = [ins[s][start + k * z.rp : start + k * z.rp + z.r].astype(F32) for k in range(2)]
         pay[source] = terms[0] + terms[1]
 
 
@@ -250,9 +250,9 @@
         pick_kernel,
         "pick",
         (SHAPE((z.n, z.t, z.ns), BF16), SHAPE((z.n, z.r, z.t), F32)),
-        [ANY] * z.n,
+        [VM] * z.n,
         [VM] * 2,
-        [pltpu.VMEM((z.n, z.pay_rows, z.t), BF16), pltpu.SemaphoreType.DMA((z.n,))],
+        [],
         ins,
     )
 
@@ -308,12 +308,10 @@
 def attend_kernel(z, g, *refs):
     n, t, count = z.n, z.t, z.sizes[g]
     ins, refs = refs[:n], refs[n + (1 if g else 0) :]
-    prob_out, attended_out, qkv_out, held, prob, attended, sems = refs
-    mover = Copies(sems)
+    prob, attended, held = refs
     me = lax.axis_index("context")
-    rows = pl.ds(0, 3 * count * t)
-    wait_all([mover.start(ins[s].at[rows], held.at[lax.rem(me + n - s, n)]) for s in range(n)])
-    stores = [mover.start(held, qkv_out)]
+    for s in range(n):
+        held[lax.rem(me + n - z.shifts[s], n)] = ins[s][: 3 * count * t]
 
     def rows_upto(k, a, width):
         return held[: width // t, z.rows_of(g, k, a), :].reshape(width, z.hd)
@@ -337,9 +335,6 @@
             attended[rows, a * z.hd : (a + 1) * z.hd] = dot(weight, rows_upto(2, a, width)).astype(BF16)
 
         z.each_block(attend)
-        stores.append(mover.start(prob.at[a], prob_out.at[a]))
-    stores.append(mover.start(attended, attended_out))
-    wait_all(stores)
 
 
 def attend(z, g, ins, after):
@@ -349,20 +344,14 @@
         SHAPE((z.s, count * z.hd), BF16),
         SHAPE((z.n, 3 * count * z.t, z.hd), BF16),
     )
-    scratch = [
-        pltpu.VMEM((z.n, 3 * count * z.t, z.hd), BF16),
-        pltpu.VMEM((count, z.s, z.s), BF16),
-        pltpu.VMEM((z.s, count * z.hd), BF16),
-        pltpu.SemaphoreType.DMA((z.n + 2 + count,)),
-    ]
     return call(
         z,
         lambda z, *refs: attend_kernel(z, g, *refs),
         "attend_%d" % g,
         outs,
-        [ANY] * (z.n + len(after)),
-        [ANY] * 3,
-        scratch,
+        [VM] * z.n + [ANY] * len(after),
+        [VM] * 3,
+        [],
         (*ins, *after),
         flops=count * z.s * z.s * z.hd * 4,
         nbytes=count * z.s * z.s * 8,
@@ -372,14 +361,13 @@
 def ssd_kernel(z, *refs):
     n, t = z.n, z.t
     ins, refs = refs[: z.groups], refs[z.groups :]
-    terms, bc, saved_out, value, attended, saved, state_low, adds, sems = refs
-    mover = Copies(sems)
-    wait_all([mover.start(ins[g], attended.at[:, z.lanes(g)]) for g in range(z.groups)])
+    terms, bc, saved, value, state_low, adds = refs
     same_head = mat(iota((z.hd, z.hd), 0) // z.mp == iota((z.hd, z.hd), 1) // z.mp).astype(BF16)
 
     def enter(c):
         rows = z.chunk(c)
-        high, low = split3(terms[z.chunk(c, z.down), :] * attended[rows, :].astype(F32))[:2]
+        attended = jnp.concatenate([one[rows, :] for one in ins], axis=1)
+        high, low = split3(terms[z.chunk(c, z.down), :] * attended.astype(F32))[:2]
         saved[0, rows, :] = high
         saved[5, rows, :] = low
         adds[rows, :] = dot_tn(bc[c, 0], high) + dot_tn(bc[c, 0], low)
@@ -426,7 +414,6 @@
         value[:, rows] = (dot_nt(ones, high) + dot_nt(ones, low))[0:1]
 
     z.each_chunk(leave)
-    mover.start(saved, saved_out).wait()
 
 
 def ssd(z, ins, terms, bc):
@@ -435,14 +422,11 @@
         ssd_kernel,
         "ssd",
         (SHAPE((6, z.s, z.f), BF16), SHAPE((1, z.s), F32)),
-        [ANY] * z.groups + [VM] * 2,
-        [ANY, VM],
+        [VM] * (z.groups + 2),
+        [VM] * 2,
         [
             pltpu.VMEM((z.s, z.f), BF16),
-            pltpu.VMEM((6, z.s, z.f), BF16),
-            pltpu.VMEM((z.s, z.f), BF16),
             pltpu.VMEM((z.n * z.ns, z.f), F32),
-            pltpu.SemaphoreType.DMA((1 + z.groups,)),
         ],
         (*ins, terms, bc),
         flops=z.s * z.f * z.ns * 20,
@@ -453,21 +437,9 @@
 def ssd_back_kernel(z, *refs):
     n, t = z.n, z.t
     lengths, values, refs = refs[0], refs[1 : n + 1], refs[n + 1 :]
-    terms, bc_in, refs = refs[0], refs[1], refs[2:]
-    saved_in, refs = refs[0], refs[1:]
-    grad_out, keep_out, give_out, step_out, vec, refs = *refs[:5], refs[5:]
-    down, small, bc, saved, d, adds, dstates, through, grads, sems = refs
-    mover = Copies(sems)
-
-    def load(k):
-        return [mover.start(saved_in.at[k], saved.at[k])]
-
-    loads = load(2) + load(4) + [
-        mover.start(bc_in, bc),
-        mover.start(terms.at[pl.ds(z.mid, z.term_rows - z.mid)], small),
-    ]
-    later = load(3) + load(1)
-    last = load(0) + load(5) + [mover.start(terms.at[pl.ds(z.down, z.s)], down)]
+    terms, bc, saved, refs = *refs[:3], refs[3:]
+    grads, keep_out, give_out, step_out, vec, refs = *refs[:5], refs[5:]
+    d, adds, dstates, through = refs
     me, core = lax.axis_index("context"), lax.axis_index("head")
     length = lengths[lax.axis_index("rollout")]
     value = values[0][...]
@@ -481,10 +453,9 @@
     per_head = mat(iota((z.f, t), 1) == iota((z.f, t), 0) // z.mp).astype(BF16)
     per_row = mat(iota((z.h * t, t), 1) == iota((z.h * t, t), 0) // t).astype(BF16)
     vec[...] = jnp.zeros_like(vec)
-    wait_all(loads)
 
     def pays(c):
-        return small[z.small(c, z.pay - z.mid, z.r), :t]
+        return terms[z.small(c, z.pay, z.r), :t]
 
     def enter(c):
         rows = z.chunk(c)
@@ -510,11 +481,10 @@
         for a in range(z.features):
             vec[a : a + 1, :] += weight_grad[:, a * z.hd : (a + 1) * z.hd]
 
-    wait_all(later)
     z.each_chunk(enter)
 
     def carry(c, dstate):
-        m = small[z.small(c, 0, 8), :][0:1]
+        m = terms[z.small(c, z.mid, 8), :][0:1]
         rows = z.chunk(c)
         dstate = m * dstate
         dstates[rows, :] = dstate.astype(BF16)
@@ -528,7 +498,6 @@
             dstate = carry(c, dstate)
     else:
         lax.fori_loop(0, n, lambda k, v: carry(n - 1 - k, v), dstate)
-    wait_all(last)
 
     def leave(c):
         rows = z.chunk(c)
@@ -538,7 +507,7 @@
         local = dot_tn(inner, dc) + dot_tn(inner, dl)
         outer = dot(b, dstate_in)
         carried = dot(cp, state_in)
-        grads[rows, :] = (down[rows, :] * (local + outer)).astype(BF16)
+        grads[rows, :] = (terms[z.chunk(c, z.down), :] * (local + outer)).astype(BF16)
         grad_c = dot_nt(dc, state_in) + dot_nt(dl, state_in)
         grad_b = dot_nt(xc, dstate_in)
         down_sum = dot(((dc.astype(F32) + dl.astype(F32)) * carried).astype(BF16), per_head)
@@ -571,13 +540,12 @@
         keep_out[c] = jnp.where(core == 0, grad_b, grad_c)
         give_out[c] = jnp.where(core == 0, grad_c, grad_b).astype(BF16)
         gain_rows = jnp.transpose(gain)[: z.r]
-        step_out[c] = -small[z.rate - z.mid : z.rate - z.mid + z.r, :t] * gain_rows
+        step_out[c] = -terms[z.rate : z.rate + z.r, :t] * gain_rows
         rate_part = jnp.sum(pays(c) * gain_rows, axis=1, keepdims=True)
         lane = (iota((z.r, t), 1) == me * z.h + iota((z.r, t), 0)) & (iota((z.r, t), 0) < z.h)
         vec[z.features : z.features + 1, :] -= jnp.sum(jnp.where(lane, rate_part, 0.0), axis=0, keepdims=True)
 
     z.each_chunk(leave)
-    mover.start(grads, grad_out).wait()
 
 
 def ssd_back(z, lengths, values, terms, bc, saved):
@@ -589,24 +557,18 @@
         SHAPE((z.v, z.t), F32),
     )
     scratch = [
-        pltpu.VMEM((z.s, z.f), F32),
-        pltpu.VMEM((z.term_rows - z.mid, z.f), F32),
-        pltpu.VMEM((z.n, 4, z.t, z.ns), BF16),
-        pltpu.VMEM((6, z.s, z.f), BF16),
         pltpu.VMEM((2, z.s, z.f), BF16),
         pltpu.VMEM((z.n * z.ns, z.f), F32),
         pltpu.VMEM((z.n * z.ns, z.f), BF16),
         pltpu.VMEM((z.n * 8, z.f), F32),
-        pltpu.VMEM((z.s, z.f), BF16),
-        pltpu.SemaphoreType.DMA((10,)),
     ]
     return call(
         z,
         ssd_back_kernel,
         "ssd_back",
         outs,
-        [SM] + [VM] * z.n + [ANY] * 3,
-        [ANY] + [VM] * 4,
+        [SM] + [VM] * (z.n + 3),
+        [VM] * 5,
         scratch,
         (lengths, *values, terms, bc, saved),
         flops=z.s * z.f * z.ns * 20,
@@ -616,17 +578,15 @@
 
 def attend_back_kernel(z, g, *refs):
     n, t, count = z.n, z.t, z.sizes[g]
-    qkv, prob_in, grad_in, refs = *refs[:3], refs[3:]
+    held, prob, grad_in, refs = *refs[:3], refs[3:]
+    grad = grad_in.at[:, z.lanes(g)]
     if g == 0:
         keep, other, step, vec, refs = *refs[:4], refs[4:]
     else:
         refs = refs[1:]
     outs, refs = refs[:n], refs[n:]
-    held, prob, grad, result, dscore, sems = refs
-    mover = Copies(sems)
+    result, dscore = refs
     me = lax.axis_index("context")
-    first = [mover.start(grad_in.at[:, z.lanes(g)], grad), mover.start(qkv, held)]
-    probs = [mover.start(prob_in.at[a], prob.at[a]) for a in range(count)]
     if g == 0:
         end = 3 * count * t
         for j in range(n):
@@ -634,7 +594,6 @@
             result[j, end + t :] = jnp.zeros((z.rp + 2 * z.v, t), BF16)
             result[j, end + t : end + t + z.r] = step[j].astype(BF16)
             result[j, end + t + z.rp :] = jnp.concatenate(split3(vec[...])[:2], axis=0)
-    wait_all(first)
     factor = 1.0 / math.sqrt(z.hd)
     per = z.rows // t
 
@@ -646,7 +605,6 @@
 
     for a in range(count):
         lanes = slice(a * z.hd, (a + 1) * z.hd)
-        probs[a].wait()
 
         def by_query(i):
             width, rows = z.upto(i), z.block(i)
@@ -665,27 +623,24 @@
             store(2, a, j, dot_tn(prob[a, start:, cols], grad[start:, lanes]))
 
         z.each_block(by_key)
-    wait_all([mover.start(result.at[lax.rem(me + s, n)], outs[s]) for s in range(n)])
+    for s in range(n):
+        outs[s][...] = result[lax.rem(me + z.back_shifts[s], n)]
 
 
 def attend_back(z, g, qkv, prob, grad, small):
     count = z.sizes[g]
     rows = z.back_rows(g)
     scratch = [
-        pltpu.VMEM((z.n, 3 * count * z.t, z.hd), BF16),
-        pltpu.VMEM((count, z.s, z.s), BF16),
-        pltpu.VMEM((z.s, count * z.hd), BF16),
         pltpu.VMEM((z.n, rows, z.hd), BF16),
         pltpu.VMEM((count, z.s, z.s), BF16),
-        pltpu.SemaphoreType.DMA((2 + z.n + count,)),
     ]
     return call(
         z,
         lambda z, *refs: attend_back_kernel(z, g, *refs),
         "attend_back_%d" % g,
         [SHAPE((rows, z.hd), BF16)] * z.n,
-        [ANY] * 3 + ([ANY] if g else [VM] * len(small)),
-        [ANY] * z.n,
+        [VM] * 3 + ([ANY] if g else [VM] * len(small)),
+        [VM] * z.n,
         scratch,
         (qkv, prob, grad, *small),
         flops=count * z.s * z.s * z.hd * 8,
@@ -695,20 +650,18 @@
 
 def unpack_kernel(z, *refs):
     n, t = z.n, z.t
-    ins, (proj, step, vecs, parts, sems) = refs[:n], refs[n:]
+    ins, (proj, step, vecs) = refs[:n], refs[n:]
     me = lax.axis_index("context")
-    mover = Copies(sems)
-    rows = pl.ds(3 * z.sizes[0] * t, t + z.rp + 2 * z.v)
-    wait_all([mover.start(ins[s].at[rows], parts.at[s]) for s in range(n)])
+    parts = [ins[s][3 * z.sizes[0] * t :] for s in range(n)]
     total = jnp.zeros((t, z.ns), F32)
     steps = jnp.zeros((n * z.h, t), F32)
     for s in range(n):
-        total = total + parts[s, :t].astype(F32)
-        source = lax.rem(me + n - s, n)
+        total = total + parts[s][:t].astype(F32)
+        source = lax.rem(me + n - z.back_shifts[s], n)
         row, col = iota((n * z.h, z.r), 0), iota((n * z.h, z.r), 1)
         place = mat((row == source * z.h + col) & (col < z.h)).astype(BF16)
-        steps = steps + dot(place, parts[s, t : t + z.r])
-        vec = parts[s, t + z.rp :].astype(F32)
+        steps = steps + dot(place, parts[s][t : t + z.r])
+        vec = parts[s][t + z.rp :].astype(F32)
         vecs[source] = vec[: z.v] + vec[z.v :]
     proj[...] = total
     step[0] = steps
@@ -720,9 +673,9 @@
         unpack_kernel,
         "unpack",
         (SHAPE((z.t, z.ns), F32), SHAPE((1, z.n * z.h, z.t), F32), SHAPE((z.n, z.v, z.t), F32)),
-        [ANY] * z.n,
+        [VM] * z.n,
         [VM] * 3,
-        [pltpu.VMEM((z.n, z.t + z.rp + 2 * z.v, z.t), BF16), pltpu.SemaphoreType.DMA((z.n,))],
+        [],
         parts,
     )
 
@@ -764,16 +717,13 @@
 
 def finish_kernel(z, *refs):
     count = z.n * z.groups
-    ins, out, refs = refs[:count], refs[count + 1], refs[count + 2 :]
+    ins, out, refs = refs[:count], refs[count], refs[count + 1 :]
     held, (turned, sems) = refs[: z.groups], refs[z.groups :]
     me = lax.axis_index("context")
     mover = Copies(sems)
-    loads = []
     for g in range(z.groups):
         for s in range(z.n):
-            rows = pl.ds(0, 3 * z.sizes[g] * z.t)
-            loads.append(mover.start(ins[g * z.n + s].at[rows], held[g].at[lax.rem(me + z.n - s, z.n)]))
-    wait_all(loads)
+            held[g][lax.rem(me + z.n - z.back_shifts[s], z.n)] = ins[g * z.n + s][: 3 * z.sizes[g] * z.t]
     stores = []
     for k in range(3):
         heads = [
@@ -787,20 +737,20 @@
     wait_all(stores)
 
 
-def finish(z, parts, after):
+def finish(z, parts):
     return call(
         z,
         finish_kernel,
         "finish",
         SHAPE((3, 1, z.t, z.hl, z.hd), BF16),
-        [ANY] * (z.n * z.groups + 1),
+        [VM] * (z.n * z.groups),
         ANY,
         [
             *[pltpu.VMEM((z.n, 3 * k * z.t, z.hd), BF16) for k in z.sizes],
             pltpu.VMEM((3, z.t, z.hl, z.hd), BF16),
-            pltpu.SemaphoreType.DMA((z.n * z.groups + 3,)),
+            pltpu.SemaphoreType.DMA((3,)),
         ],
-        (*parts, after),
+        parts,
         nbytes=12 * z.t * z.hl * z.hd,
     )
 
@@ -809,8 +759,12 @@
     return lax.ppermute(x, axis, [(i, (i + step) % size) for i in range(size)])
 
 
-def spread(parts, axis):
-    return [parts[0]] + [shift(x, axis, len(parts), s) for s, x in enumerate(parts) if s]
+def spread(parts, axis, shifts):
+    return [parts[0]] + [shift(x, axis, len(parts), s) for x, s in zip(parts[1:], shifts[1:])]
+
+
+def partners(x, axis, step):
+    return lax.ppermute(x, axis, [(i, i ^ step) for i in range(lax.axis_size(axis))])
 
 
 def local(qkv, ssd_b, ssd_c, step_size, decay_rate, value_weight, returns, step_labels, lengths):
@@ -818,7 +772,7 @@
     z = Sizes(n, qkv.shape[2], qkv.shape[3], qkv.shape[4], step_size.shape[2], ssd_b.shape[2])
 
     sends = prep(z, qkv, ssd_b, ssd_c, jnp.swapaxes(step_size, 1, 2), step_labels, returns)
-    arrived = [spread(sends[g * n : (g + 1) * n], "context") for g in range(z.groups)]
+    arrived = [spread(sends[g * n : (g + 1) * n], "context", z.shifts) for g in range(z.groups)]
     mine, pay = pick(z, arrived[0])
     theirs = shift(mine, "head", 2, 1)
     attended = [attend(z, 0, arrived[0], [])]
@@ -827,22 +781,21 @@
         attended.append(attend(z, g, arrived[g], [bc]))
     saved, value = ssd(z, [x[1] for x in attended], terms, bc)
     value = value + shift(value, "head", 2, 1)
-    values = spread([value] * n, "context")
+    values = [value] + [partners(value, "context", s) for s in range(1, n)]
     grad, keep, give, steps, vec = ssd_back(z, lengths, values, terms, bc, saved)
     finals, small = [], [keep, shift(give, "head", 2, 1), steps, vec]
     for g in range(z.groups):
         back = attend_back(z, g, attended[g][2], attended[g][0], grad, small)
-        finals.append(spread(back, "context"))
+        finals.append(spread(back, "context", z.back_shifts))
         small = back[:1]
     proj, step_grad, vecs = unpack(z, finals[0])
     other = shift(proj, "head", 2, 1)
     step = 1
     while step < lax.axis_size("rollout"):
-        pairs = [(i, i ^ step) for i in range(lax.axis_size("rollout"))]
-        vecs = vecs + lax.ppermute(vecs, "rollout", pairs)
+        vecs = vecs + partners(vecs, "rollout", step)
         step *= 2
     b_grad, c_grad, weight_grad, rate_grad, loss = choose(z, lengths, proj, other, vecs)
-    qkv_grad = finish(z, [x for part in finals for x in part], rate_grad)
+    qkv_grad = finish(z, [x for part in finals for x in part])
     return (
         loss.reshape(()),
         qkv_grad,

time: 120 us -> 112 us (0.933)
  the two profiles are of different devices: /device:TPU:10 before, /device:TPU:0 now
where the time goes in v3:
time: 112 us; the launch traced here: 111 us
  waiting for transfers between devices  48.6 us (43%)
  starting transfers between devices  38.4 us (34%)
  Pallas kernels  23.6 us (21%)
    ppermute x16, waiting for transfers between devices, shift(): return lax.ppermute(x, axis, [(i, (i + step) % size) for i in range(size)])  42.5 us
    ppermute x16, starting transfers between devices, shift(): return lax.ppermute(x, axis, [(i, (i + step) % size) for i in range(size)])  29.1 us
    pallas_call x12, Pallas kernels, call(): pl.pallas_call(functools.partial(kernel, z), name=name, out_shape=out_sha...  23.6 us
    ppermute x5, starting transfers between devices, partners(): lax.ppermute(x, axis, [(i, i ^ step) for i in range(lax.axis_size(axis))])  9.3 us
    ppermute x5, waiting for transfers between devices, partners(): lax.ppermute(x, axis, [(i, i ^ step) for i in range(lax.axis_size(axis))])  6.1 us
  transfers between devices with their start and end apart: 21, of which 12 were waited for; matrix products, arithmetic and copies ran while one was open for 0% of the time, Pallas kernels for 7%

profile of v3, /device:TPU:0, one launch (start us, length us, event | category | flops | bytes accessed | tf_op | source)
XLA Modules:
  0.0 111.4 jit_solution(10420038460749605113)
XLA Ops:
  0.7 2.0 %prep.1 = (bf16[928,128]{1,0:T(8,128)(2,1)S(1)}, bf16[928,128]{1,0:T(8,128)(2,1)S(1)}, bf16[928,128]{1,0:T(8,128)(2,1)S(1)}, bf16[928,128]{1,0:T(8,128)(2,1)S(1)...) custom-call(bf16[3,1,128,16,128]{4,3,2,1,0:T(8,128)(2,1)} %qkv.1, ...), custom_call_target="tpu_custom_call" | custom-call | bytes 3145728 | tf_op jit(solution)/shard_map/prep/pallas_call | solution.py:127
  2.7 3.1 %collective-permute-start = (bf16[928,128]{1,0:T(8,128)(2,1)S(1)}, bf16[928,128]{1,0:T(8,128)(2,1)S(1)}, u32[]{:S(2)}, u32[]{:S(2)}) collective-permute-start(bf16[928,128]{1,0:T(8,128)(2,1)S(1)} %get-tuple-element.49), channel_id=1, source_target_pairs={{0,2},{2,4},{4,6},{6,0},{1,3},{3,5},{5,7},{7,1},{8,10},{10,12},{12... | collective-permute-start | bytes 712712 | tf_op jit(solution)/shard_map/ppermute | solution.py:759
  5.7 2.6 %collective-permute-start.1 = (bf16[928,128]{1,0:T(8,128)(2,1)S(1)}, bf16[928,128]{1,0:T(8,128)(2,1)S(1)}, u32[]{:S(2)}, u32[]{:S(2)}) collective-permute-start(bf16[928,128]{1,0:T(8,128)(2,1)S(1)} %get-tuple-element.50), channel_id=1, source_target_pairs={{0,4},{2,6},{4,0},{6,2},{1,5},{3,7},{5,1},{7,3},{8,12},{10,14},{12... | collective-permute-start | bytes 712712 | tf_op jit(solution)/shard_map/ppermute | solution.py:759
  8.3 1.3 %collective-permute-start.2 = (bf16[928,128]{1,0:T(8,128)(2,1)S(1)}, bf16[928,128]{1,0:T(8,128)(2,1)S(1)}, u32[]{:S(2)}, u32[]{:S(2)}) collective-permute-start(bf16[928,128]{1,0:T(8,128)(2,1)S(1)} %get-tuple-element.51), channel_id=1, source_target_pairs={{0,6},{2,0},{4,2},{6,4},{1,7},{3,1},{5,3},{7,5},{8,14},{10,8},{12,... | collective-permute-start | bytes 712712 | tf_op jit(solution)/shard_map/ppermute | solution.py:759
  9.7 0.7 collective-permute-start.3
  10.4 0.3 collective-permute-start.4
  10.7 3.8 %collective-permute-done.refs_1_ = bf16[928,128]{1,0:T(8,128)(2,1)S(1)} collective-permute-done((bf16[928,128]{1,0:T(8,128)(2,1)S(1)}, bf16[928,128]{1,0:T(8,128)(2,1)S(1)}, u32[]{:S(2)}, u32[]{:S(2)}) %collective-permute-start) | collective-permute-done | bytes 237600 | tf_op jit(solution)/shard_map/ppermute | solution.py:759
  14.5 2.5 %collective-permute-start.5 = (bf16[768,128]{1,0:T(8,128)(2,1)S(1)}, bf16[768,128]{1,0:T(8,128)(2,1)S(1)}, u32[]{:S(2)}, u32[]{:S(2)}) collective-permute-start(bf16[768,128]{1,0:T(8,128)(2,1)S(1)} %get-tuple-element.58), channel_id=1, source_target_pairs={{0,6},{2,0},{4,2},{6,4},{1,7},{3,1},{5,3},{7,5},{8,14},{10,8},{12,... | collective-permute-start | bytes 589832 | tf_op jit(solution)/shard_map/ppermute | solution.py:759
  17.0 7.7 %collective-permute-done.1.refs_2_ = bf16[928,128]{1,0:T(8,128)(2,1)S(1)} collective-permute-done((bf16[928,128]{1,0:T(8,128)(2,1)S(1)}, bf16[928,128]{1,0:T(8,128)(2,1)S(1)}, u32[]{:S(2)}, u32[]{:S(2)}) %collective-permute-start.1) | collective-permute-done | bytes 237600 | tf_op jit(solution)/shard_map/ppermute | solution.py:759
  24.8 0.1 collective-permute-start.6
  24.9 1.8 %attend_0.1 = (bf16[2,512,512]{2,1,0:T(8,128)(2,1)S(1)}, bf16[512,256]{1,0:T(8,128)(2,1)S(1)}, bf16[4,768,128]{2,1,0:T(8,128)(2,1)S(1)}) custom-call(bf16[928,128]{1,0:T(8,128)(2,1)S(1)} %get-tuple-element.48.refs_0_, bf16[928,128]{1,0:T(8,128)(2,1)S(1)} %collective-permute-done.refs_1_, bf16[928,128]{1,0:T(8,128)(2,1)S(1)} %collective-permute-done.1.refs_2_, ...), custom_call_target="tpu_custom_call" | custom-call | flops 268435456 | bytes 4194304 | tf_op jit(solution)/shard_map/attend_0/pallas_call | solution.py:127
  26.7 2.0 %decay.1 = (f32[1144,512]{1,0:T(8,128)S(1)}, bf16[4,4,128,128]{3,2,1,0:T(8,128)(2,1)S(1)}) custom-call(bf16[4,128,128]{2,1,0:T(8,128)(2,1)S(1)} %get-tuple-element.59.mine, bf16[4,128,128]{2,1,0:T(8,128)(2,1)S(1)} %collective-permute-done.6.theirs, f32[4,16,128]{2,1,0:T(8,128)S(1)} %get-tuple-element.60.pay, f32[1,32]{1,0:T(1,128)S(1)} %bitcast.8, ...), custom_call_target="tpu_custom_call" | custom-call | bytes 2097152 | tf_op jit(solution)/shard_map/decay/pallas_call | solution.py:127
  28.7 0.2 collective-permute-done.3.refs_1_
  29.0 12.7 %collective-permute-done.4.refs_2_ = bf16[768,128]{1,0:T(8,128)(2,1)S(1)} collective-permute-done((bf16[768,128]{1,0:T(8,128)(2,1)S(1)}, bf16[768,128]{1,0:T(8,128)(2,1)S(1)}, u32[]{:S(2)}, u32[]{:S(2)}) %collective-permute-start.4) | collective-permute-done | bytes 196640 | tf_op jit(solution)/shard_map/ppermute | solution.py:759
  41.6 1.8 %attend_1.1 = (bf16[2,512,512]{2,1,0:T(8,128)(2,1)S(1)}, bf16[512,256]{1,0:T(8,128)(2,1)S(1)}, bf16[4,768,128]{2,1,0:T(8,128)(2,1)S(1)}) custom-call(bf16[768,128]{1,0:T(8,128)(2,1)S(1)} %get-tuple-element.55.refs_0_, bf16[768,128]{1,0:T(8,128)(2,1)S(1)} %collective-permute-done.3.refs_1_, bf16[768,128]{1,0:T(8,128)(2,1)S(1)} %collective-permute-done.4.refs_2_, ...), custom_call_target="tpu_custom_call" | custom-call | flops 268435456 | bytes 4194304 | tf_op jit(solution)/shard_map/attend_1/pallas_call | solution.py:127
  43.5 2.7 %ssd.1 = (bf16[6,512,512]{2,1,0:T(8,128)(2,1)S(1)}, f32[1,512]{1,0:T(1,128)S(1)}) custom-call(bf16[512,256]{1,0:T(8,128)(2,1)S(1)} %get-tuple-element.54.refs_0_, bf16[512,256]{1,0:T(8,128)(2,1)S(1)} %get-tuple-element.62.refs_1_, f32[1144,512]{1,0:T(8,128)S(1)} %get-tuple-element.63.refs_2_.refs_5_, ...), custom_call_target="tpu_custom_call" | custom-call | flops 671088640 | bytes 8388608 | tf_op jit(solution)/shard_map/ssd/pallas_call | solution.py:127
  46.2 0.1 collective-permute-start.7
  46.3 1.1 %collective-permute-done.7 = f32[1,512]{1,0:T(1,128)S(1)} collective-permute-done((f32[1,512]{1,0:T(1,128)S(1)}, f32[1,512]{1,0:T(1,128)S(1)}, u32[]{:S(2)}, u32[]{:S(2)}) %collective-permute-start.7) | collective-permute-done | bytes 2080 | tf_op jit(solution)/shard_map/ppermute | solution.py:759
  47.4 5.7 %collective-permute-start.10 = (f32[1,512]{1,0:T(1,128)S(1)}, f32[1,512]{1,0:T(1,128)S(1)}, u32[]{:S(2)}, u32[]{:S(2)}) collective-permute-start(f32[1,512]{1,0:T(1,128)S(1)} %add.9.refs_1_), channel_id=1, source_target_pairs={{0,6},{2,4},{4,2},{6,0},{1,7},{3,5},{5,3},{7,1},{8,14},{10,12},{12... | collective-permute-start | bytes 6152 | tf_op jit(solution)/shard_map/ppermute | solution.py:767
  53.1 0.5 collective-permute-start.9
  53.6 0.2 collective-permute-start.8
  53.7 0.9 collective-permute-done.10.refs_4_
  54.7 2.9 %collective-permute-done.9.refs_3_ = f32[1,512]{1,0:T(1,128)S(1)} collective-permute-done((f32[1,512]{1,0:T(1,128)S(1)}, f32[1,512]{1,0:T(1,128)S(1)}, u32[]{:S(2)}, u32[]{:S(2)}) %collective-permute-start.9) | collective-permute-done | bytes 2080 | tf_op jit(solution)/shard_map/ppermute | solution.py:767
  57.6 0.0 collective-permute-done.8.refs_2_
  57.6 5.8 %ssd_back.1 = (bf16[512,512]{1,0:T(8,128)(2,1)S(1)}, f32[4,128,128]{2,1,0:T(8,128)S(1)}, bf16[4,128,128]{2,1,0:T(8,128)(2,1)S(1)}, f32[4,16,128]{2,1,0:T(8,128)S(1)}, f32[8,128]{1,0:T(8,128)S(1)}) custom-call(s32[4]{0:T(128)S(1)} %copy-done.1, f32[1,512]{1,0:T(1,128)S(1)} %add.9.refs_1_, f32[1,512]{1,0:T(1,128)S(1)} %collective-permute-done.8.refs_2_, ...), custom_call_target="tpu_custom_call" | custom-call | flops 671088640 | bytes 8388608 | tf_op jit(solution)/shard_map/ssd_back/pallas_call | solution.py:127
  63.4 0.1 collective-permute-start.11
  63.5 1.3 %collective-permute-done.11.refs_4_ = bf16[4,128,128]{2,1,0:T(8,128)(2,1)S(1)} collective-permute-done((bf16[4,128,128]{2,1,0:T(8,128)(2,1)S(1)}, bf16[4,128,128]{2,1,0:T(8,128)(2,1)S(1)}, u32[]{:S(2)}, u32[]{:S(2)}) %collective-permute-start.11) | collective-permute-done | bytes 131104 | tf_op jit(solution)/shard_map/ppermute | solution.py:759
  64.8 2.0 %attend_back_0.1 = (bf16[928,128]{1,0:T(8,128)(2,1)S(1)}, bf16[928,128]{1,0:T(8,128)(2,1)S(1)}, bf16[928,128]{1,0:T(8,128)(2,1)S(1)}, bf16[928,128]{1,0:T(8,128)(2,1)S(1)}) custom-call(bf16[4,768,128]{2,1,0:T(8,128)(2,1)S(1)} %get-tuple-element.52.refs_0_, bf16[2,512,512]{2,1,0:T(8,128)(2,1)S(1)} %get-tuple-element.53.refs_1_, ...), custom_call_target="tpu_custom_call" | custom-call | flops 536870912 | bytes 4194304 | tf_op jit(solution)/shard_map/attend_back_0/pallas_call | solution.py:127
  66.8 0.1 collective-permute-start.12
  66.9 3.8 %collective-permute-start.13 = (bf16[928,128]{1,0:T(8,128)(2,1)S(1)}, bf16[928,128]{1,0:T(8,128)(2,1)S(1)}, u32[]{:S(2)}, u32[]{:S(2)}) collective-permute-start(bf16[928,128]{1,0:T(8,128)(2,1)S(1)} %get-tuple-element.73), channel_id=1, source_target_pairs={{0,6},{2,0},{4,2},{6,4},{1,7},{3,1},{5,3},{7,5},{8,14},{10,8},{12,... | collective-permute-start | bytes 712712 | tf_op jit(solution)/shard_map/ppermute | solution.py:759
  70.7 0.2 collective-permute-start.14
  71.0 1.8 %attend_back_1.1 = (bf16[768,128]{1,0:T(8,128)(2,1)S(1)}, bf16[768,128]{1,0:T(8,128)(2,1)S(1)}, bf16[768,128]{1,0:T(8,128)(2,1)S(1)}, bf16[768,128]{1,0:T(8,128)(2,1)S(1)}) custom-call(bf16[4,768,128]{2,1,0:T(8,128)(2,1)S(1)} %get-tuple-element.78.refs_0_, bf16[2,512,512]{2,1,0:T(8,128)(2,1)S(1)} %get-tuple-element.79.refs_1_, ...), custom_call_target="tpu_custom_call" | custom-call | flops 536870912 | bytes 4194304 | tf_op jit(solution)/shard_map/attend_back_1/pallas_call | solution.py:127
  72.8 0.4 collective-permute-start.18
  73.2 3.5 %collective-permute-start.19 = (bf16[768,128]{1,0:T(8,128)(2,1)S(1)}, bf16[768,128]{1,0:T(8,128)(2,1)S(1)}, u32[]{:S(2)}, u32[]{:S(2)}) collective-permute-start(bf16[768,128]{1,0:T(8,128)(2,1)S(1)} %get-tuple-element.82), channel_id=1, source_target_pairs={{0,6},{2,0},{4,2},{6,4},{1,7},{3,1},{5,3},{7,5},{8,14},{10,8},{12,... | collective-permute-start | bytes 589832 | tf_op jit(solution)/shard_map/ppermute | solution.py:759
  76.7 0.7 collective-permute-done.12.refs_1_
  77.4 10.4 %collective-permute-start.20 = (bf16[768,128]{1,0:T(8,128)(2,1)S(1)}, bf16[768,128]{1,0:T(8,128)(2,1)S(1)}, u32[]{:S(2)}, u32[]{:S(2)}) collective-permute-start(bf16[768,128]{1,0:T(8,128)(2,1)S(1)} %get-tuple-element.83), channel_id=1, source_target_pairs={{0,4},{2,6},{4,0},{6,2},{1,5},{3,7},{5,1},{7,3},{8,12},{10,14},{12... | collective-permute-start | bytes 589832 | tf_op jit(solution)/shard_map/ppermute | solution.py:759
  87.7 0.0 collective-permute-done.13.refs_2_
  87.7 12.6 %collective-permute-done.14.refs_3_ = bf16[928,128]{1,0:T(8,128)(2,1)S(1)} collective-permute-done((bf16[928,128]{1,0:T(8,128)(2,1)S(1)}, bf16[928,128]{1,0:T(8,128)(2,1)S(1)}, u32[]{:S(2)}, u32[]{:S(2)}) %collective-permute-start.14) | collective-permute-done | bytes 237600 | tf_op jit(solution)/shard_map/ppermute | solution.py:759
  100.3 0.8 unpack.1
  101.1 0.0 collective-permute-start.15
  101.1 1.5 %collective-permute-start.16 = (f32[4,8,128]{2,1,0:T(8,128)S(1)}, f32[4,8,128]{2,1,0:T(8,128)S(1)}, u32[]{:S(2)}, u32[]{:S(2)}) collective-permute-start(f32[4,8,128]{2,1,0:T(8,128)S(1)} %get-tuple-element.76), channel_id=1, source_target_pairs={{0,8},{8,0},{16,24},{24,16},{1,9},{9,1},{17,25},{25,17},{2,10},{10... | collective-permute-start | bytes 49160 | tf_op jit(solution)/shard_map/ppermute | solution.py:767
  102.6 2.2 %collective-permute-done.16 = f32[4,8,128]{2,1,0:T(8,128)S(1)} collective-permute-done((f32[4,8,128]{2,1,0:T(8,128)S(1)}, f32[4,8,128]{2,1,0:T(8,128)S(1)}, u32[]{:S(2)}, u32[]{:S(2)}) %collective-permute-start.16) | collective-permute-done | bytes 16416 | tf_op jit(solution)/shard_map/ppermute | solution.py:767
  104.8 1.5 %collective-permute-start.17 = (f32[4,8,128]{2,1,0:T(8,128)S(1)}, f32[4,8,128]{2,1,0:T(8,128)S(1)}, u32[]{:S(2)}, u32[]{:S(2)}) collective-permute-start(f32[4,8,128]{2,1,0:T(8,128)S(1)} %add.10), channel_id=1, source_target_pairs={{0,16},{8,24},{16,0},{24,8},{1,17},{9,25},{17,1},{25,9},{2,18},{10... | collective-permute-start | bytes 49160 | tf_op jit(solution)/shard_map/ppermute | solution.py:767
  106.3 0.0 collective-permute-done.18.refs_5_
  106.3 0.0 collective-permute-done.19.refs_6_
  106.3 2.3 %collective-permute-done.20.refs_7_ = bf16[768,128]{1,0:T(8,128)(2,1)S(1)} collective-permute-done((bf16[768,128]{1,0:T(8,128)(2,1)S(1)}, bf16[768,128]{1,0:T(8,128)(2,1)S(1)}, u32[]{:S(2)}, u32[]{:S(2)}) %collective-permute-start.20) | collective-permute-done | bytes 196640 | tf_op jit(solution)/shard_map/ppermute | solution.py:759
  108.6 1.5 %finish.1 = bf16[3,1,128,16,128]{4,3,2,1,0:T(8,128)(2,1)} custom-call(bf16[928,128]{1,0:T(8,128)(2,1)S(1)} %get-tuple-element.71.refs_0_.refs_3_, bf16[928,128]{1,0:T(8,128)(2,1)S(1)} %collective-permute-done.12.refs_1_, bf16[928,128]{1,0:T(8,128)(2,1)S(1)} %collective-permute-done.13.refs_2_, bf16[928,128]{1,0:T(8,128)(2,1)S(1)} %collective-permute-done.14.refs_3_, ...), custom_call_target="tpu_custom_call" | custom-call | bytes 3145728 | tf_op jit(solution)/shard_map/finish/pallas_call | solution.py:127
  110.1 1.2 %choose.1 = (f32[1,128,128]{2,1,0:T(8,128)}, f32[1,128,128]{2,1,0:T(8,128)}, f32[4,4,128]{2,1,0:T(4,128)}, f32[1,32]{1,0:T(1,128)}, f32[1,1]{1,0:T(1,128)}) custom-call(s32[4]{0:T(128)S(1)} %copy-done.1, f32[128,128]{1,0:T(8,128)S(1)} %get-tuple-element.75.mine, f32[128,128]{1,0:T(8,128)S(1)} %collective-permute-done.15.theirs, f32[4,8,128]{2,1,0:T(8,128)S(1)} %add.11.vecs), custom_call_target="tpu_custom_call" | custom-call | tf_op jit(solution)/shard_map/choose/pallas_call | solution.py:127
  (15 shorter events, 0.1 us)
Async XLA Ops:
  0.6 26.1 %copy-start = (bf16[2048]{0:T(1024)(128)(2,1)S(1)}, bf16[2048]{0:T(1024)(128)(2,1)}, u32[]{:S(2)}) copy-start(bf16[2048]{0:T(1024)(128)(2,1)} %param.14) | copy-start | bytes 12292
  0.6 26.1 %copy-start.2 = (f32[32]{0:T(128)S(1)}, f32[32]{0:T(128)}, u32[]{:S(2)}) copy-start(f32[32]{0:T(128)} %param.13) | copy-start | bytes 388
  2.7 11.9 %collective-permute-start = (bf16[928,128]{1,0:T(8,128)(2,1)S(1)}, bf16[928,128]{1,0:T(8,128)(2,1)S(1)}, u32[]{:S(2)}, u32[]{:S(2)}) collective-permute-start(bf16[928,128]{1,0:T(8,128)(2,1)S(1)} %get-tuple-element.49), channel_id=1, source_target_pairs={{0,2},{2,4},{4,6},{6,0},{1,3},{3,5},{5,7},{7,1},{8,10},{10,12},{12... | collective-permute-start | bytes 712712 | tf_op jit(solution)/shard_map/ppermute | solution.py:759
  5.7 19.0 %collective-permute-start.1 = (bf16[928,128]{1,0:T(8,128)(2,1)S(1)}, bf16[928,128]{1,0:T(8,128)(2,1)S(1)}, u32[]{:S(2)}, u32[]{:S(2)}) collective-permute-start(bf16[928,128]{1,0:T(8,128)(2,1)S(1)} %get-tuple-element.50), channel_id=1, source_target_pairs={{0,4},{2,6},{4,0},{6,2},{1,5},{3,7},{5,1},{7,3},{8,12},{10,14},{12... | collective-permute-start | bytes 712712 | tf_op jit(solution)/shard_map/ppermute | solution.py:759
  8.3 16.4 %collective-permute-start.2 = (bf16[928,128]{1,0:T(8,128)(2,1)S(1)}, bf16[928,128]{1,0:T(8,128)(2,1)S(1)}, u32[]{:S(2)}, u32[]{:S(2)}) collective-permute-start(bf16[928,128]{1,0:T(8,128)(2,1)S(1)} %get-tuple-element.51), channel_id=1, source_target_pairs={{0,6},{2,0},{4,2},{6,4},{1,7},{3,1},{5,3},{7,5},{8,14},{10,8},{12,... | collective-permute-start | bytes 712712 | tf_op jit(solution)/shard_map/ppermute | solution.py:759
  9.7 19.3 %collective-permute-start.3 = (bf16[768,128]{1,0:T(8,128)(2,1)S(1)}, bf16[768,128]{1,0:T(8,128)(2,1)S(1)}, u32[]{:S(2)}, u32[]{:S(2)}) collective-permute-start(bf16[768,128]{1,0:T(8,128)(2,1)S(1)} %get-tuple-element.56), channel_id=1, source_target_pairs={{0,2},{2,4},{4,6},{6,0},{1,3},{3,5},{5,7},{7,1},{8,10},{10,12},{12... | collective-permute-start | bytes 589832 | tf_op jit(solution)/shard_map/ppermute | solution.py:759
  10.4 31.3 %collective-permute-start.4 = (bf16[768,128]{1,0:T(8,128)(2,1)S(1)}, bf16[768,128]{1,0:T(8,128)(2,1)S(1)}, u32[]{:S(2)}, u32[]{:S(2)}) collective-permute-start(bf16[768,128]{1,0:T(8,128)(2,1)S(1)} %get-tuple-element.57), channel_id=1, source_target_pairs={{0,4},{2,6},{4,0},{6,2},{1,5},{3,7},{5,1},{7,3},{8,12},{10,14},{12... | collective-permute-start | bytes 589832 | tf_op jit(solution)/shard_map/ppermute | solution.py:759
  14.5 27.1 %collective-permute-start.5 = (bf16[768,128]{1,0:T(8,128)(2,1)S(1)}, bf16[768,128]{1,0:T(8,128)(2,1)S(1)}, u32[]{:S(2)}, u32[]{:S(2)}) collective-permute-start(bf16[768,128]{1,0:T(8,128)(2,1)S(1)} %get-tuple-element.58), channel_id=1, source_target_pairs={{0,6},{2,0},{4,2},{6,4},{1,7},{3,1},{5,3},{7,5},{8,14},{10,8},{12,... | collective-permute-start | bytes 589832 | tf_op jit(solution)/shard_map/ppermute | solution.py:759
  24.8 1.9 %collective-permute-start.6 = (bf16[4,128,128]{2,1,0:T(8,128)(2,1)S(1)}, bf16[4,128,128]{2,1,0:T(8,128)(2,1)S(1)}, u32[]{:S(2)}, u32[]{:S(2)}) collective-permute-start(bf16[4,128,128]{2,1,0:T(8,128)(2,1)S(1)} %get-tuple-element.59.mine), channel_id=1, source_target_pairs={{0,1},{1,0},{2,3},{3,2},{4,5},{5,4},{6,7},{7,6},{8,9},{9,8},{10,11... | collective-permute-start | bytes 393224 | tf_op jit(solution)/shard_map/ppermute | solution.py:759
  41.6 15.9 %copy-start.1 = (s32[4]{0:T(128)S(1)}, s32[4]{0:T(128)}, u32[]{:S(2)}) copy-start(s32[4]{0:T(128)} %lengths.1) | copy-start | bytes 52
  46.2 1.2 %collective-permute-start.7 = (f32[1,512]{1,0:T(1,128)S(1)}, f32[1,512]{1,0:T(1,128)S(1)}, u32[]{:S(2)}, u32[]{:S(2)}) collective-permute-start(f32[1,512]{1,0:T(1,128)S(1)} %get-tuple-element.64), channel_id=1, source_target_pairs={{0,1},{1,0},{2,3},{3,2},{4,5},{5,4},{6,7},{7,6},{8,9},{9,8},{10,11... | collective-permute-start | bytes 6152 | tf_op jit(solution)/shard_map/ppermute | solution.py:759
  47.4 7.2 %collective-permute-start.10 = (f32[1,512]{1,0:T(1,128)S(1)}, f32[1,512]{1,0:T(1,128)S(1)}, u32[]{:S(2)}, u32[]{:S(2)}) collective-permute-start(f32[1,512]{1,0:T(1,128)S(1)} %add.9.refs_1_), channel_id=1, source_target_pairs={{0,6},{2,4},{4,2},{6,0},{1,7},{3,5},{5,3},{7,1},{8,14},{10,12},{12... | collective-permute-start | bytes 6152 | tf_op jit(solution)/shard_map/ppermute | solution.py:767
  53.1 4.5 %collective-permute-start.9 = (f32[1,512]{1,0:T(1,128)S(1)}, f32[1,512]{1,0:T(1,128)S(1)}, u32[]{:S(2)}, u32[]{:S(2)}) collective-permute-start(f32[1,512]{1,0:T(1,128)S(1)} %add.9.refs_1_), channel_id=1, source_target_pairs={{0,4},{2,6},{4,0},{6,2},{1,5},{3,7},{5,1},{7,3},{8,12},{10,14},{12... | collective-permute-start | bytes 6152 | tf_op jit(solution)/shard_map/ppermute | solution.py:767
  53.6 4.0 %collective-permute-start.8 = (f32[1,512]{1,0:T(1,128)S(1)}, f32[1,512]{1,0:T(1,128)S(1)}, u32[]{:S(2)}, u32[]{:S(2)}) collective-permute-start(f32[1,512]{1,0:T(1,128)S(1)} %add.9.refs_1_), channel_id=1, source_target_pairs={{0,2},{2,0},{4,6},{6,4},{1,3},{3,1},{5,7},{7,5},{8,10},{10,8},{12,... | collective-permute-start | bytes 6152 | tf_op jit(solution)/shard_map/ppermute | solution.py:767
  63.4 1.4 %collective-permute-start.11 = (bf16[4,128,128]{2,1,0:T(8,128)(2,1)S(1)}, bf16[4,128,128]{2,1,0:T(8,128)(2,1)S(1)}, u32[]{:S(2)}, u32[]{:S(2)}) collective-permute-start(bf16[4,128,128]{2,1,0:T(8,128)(2,1)S(1)} %get-tuple-element.68), channel_id=1, source_target_pairs={{0,1},{1,0},{2,3},{3,2},{4,5},{5,4},{6,7},{7,6},{8,9},{9,8},{10,11... | collective-permute-start | bytes 393224 | tf_op jit(solution)/shard_map/ppermute | solution.py:759
  66.8 10.5 %collective-permute-start.12 = (bf16[928,128]{1,0:T(8,128)(2,1)S(1)}, bf16[928,128]{1,0:T(8,128)(2,1)S(1)}, u32[]{:S(2)}, u32[]{:S(2)}) collective-permute-start(bf16[928,128]{1,0:T(8,128)(2,1)S(1)} %get-tuple-element.72), channel_id=1, source_target_pairs={{0,2},{2,4},{4,6},{6,0},{1,3},{3,5},{5,7},{7,1},{8,10},{10,12},{12... | collective-permute-start | bytes 712712 | tf_op jit(solution)/shard_map/ppermute | solution.py:759
  66.9 20.8 %collective-permute-start.13 = (bf16[928,128]{1,0:T(8,128)(2,1)S(1)}, bf16[928,128]{1,0:T(8,128)(2,1)S(1)}, u32[]{:S(2)}, u32[]{:S(2)}) collective-permute-start(bf16[928,128]{1,0:T(8,128)(2,1)S(1)} %get-tuple-element.73), channel_id=1, source_target_pairs={{0,6},{2,0},{4,2},{6,4},{1,7},{3,1},{5,3},{7,5},{8,14},{10,8},{12,... | collective-permute-start | bytes 712712 | tf_op jit(solution)/shard_map/ppermute | solution.py:759
  70.7 29.6 %collective-permute-start.14 = (bf16[928,128]{1,0:T(8,128)(2,1)S(1)}, bf16[928,128]{1,0:T(8,128)(2,1)S(1)}, u32[]{:S(2)}, u32[]{:S(2)}) collective-permute-start(bf16[928,128]{1,0:T(8,128)(2,1)S(1)} %get-tuple-element.74), channel_id=1, source_target_pairs={{0,4},{2,6},{4,0},{6,2},{1,5},{3,7},{5,1},{7,3},{8,12},{10,14},{12... | collective-permute-start | bytes 712712 | tf_op jit(solution)/shard_map/ppermute | solution.py:759
  72.8 33.6 %collective-permute-start.18 = (bf16[768,128]{1,0:T(8,128)(2,1)S(1)}, bf16[768,128]{1,0:T(8,128)(2,1)S(1)}, u32[]{:S(2)}, u32[]{:S(2)}) collective-permute-start(bf16[768,128]{1,0:T(8,128)(2,1)S(1)} %get-tuple-element.81), channel_id=1, source_target_pairs={{0,2},{2,4},{4,6},{6,0},{1,3},{3,5},{5,7},{7,1},{8,10},{10,12},{12... | collective-permute-start | bytes 589832 | tf_op jit(solution)/shard_map/ppermute | solution.py:759
  73.2 33.2 %collective-permute-start.19 = (bf16[768,128]{1,0:T(8,128)(2,1)S(1)}, bf16[768,128]{1,0:T(8,128)(2,1)S(1)}, u32[]{:S(2)}, u32[]{:S(2)}) collective-permute-start(bf16[768,128]{1,0:T(8,128)(2,1)S(1)} %get-tuple-element.82), channel_id=1, source_target_pairs={{0,6},{2,0},{4,2},{6,4},{1,7},{3,1},{5,3},{7,5},{8,14},{10,8},{12,... | collective-permute-start | bytes 589832 | tf_op jit(solution)/shard_map/ppermute | solution.py:759
  77.4 31.3 %collective-permute-start.20 = (bf16[768,128]{1,0:T(8,128)(2,1)S(1)}, bf16[768,128]{1,0:T(8,128)(2,1)S(1)}, u32[]{:S(2)}, u32[]{:S(2)}) collective-permute-start(bf16[768,128]{1,0:T(8,128)(2,1)S(1)} %get-tuple-element.83), channel_id=1, source_target_pairs={{0,4},{2,6},{4,0},{6,2},{1,5},{3,7},{5,1},{7,3},{8,12},{10,14},{12... | collective-permute-start | bytes 589832 | tf_op jit(solution)/shard_map/ppermute | solution.py:759
  101.1 9.1 %collective-permute-start.15 = (f32[128,128]{1,0:T(8,128)S(1)}, f32[128,128]{1,0:T(8,128)S(1)}, u32[]{:S(2)}, u32[]{:S(2)}) collective-permute-start(f32[128,128]{1,0:T(8,128)S(1)} %get-tuple-element.75.mine), channel_id=1, source_target_pairs={{0,1},{1,0},{2,3},{3,2},{4,5},{5,4},{6,7},{7,6},{8,9},{9,8},{10,11... | collective-permute-start | bytes 196616 | tf_op jit(solution)/shard_map/ppermute | solution.py:759
  101.1 3.7 %collective-permute-start.16 = (f32[4,8,128]{2,1,0:T(8,128)S(1)}, f32[4,8,128]{2,1,0:T(8,128)S(1)}, u32[]{:S(2)}, u32[]{:S(2)}) collective-permute-start(f32[4,8,128]{2,1,0:T(8,128)S(1)} %get-tuple-element.76), channel_id=1, source_target_pairs={{0,8},{8,0},{16,24},{24,16},{1,9},{9,1},{17,25},{25,17},{2,10},{10... | collective-permute-start | bytes 49160 | tf_op jit(solution)/shard_map/ppermute | solution.py:767
  104.8 5.3 %collective-permute-start.17 = (f32[4,8,128]{2,1,0:T(8,128)S(1)}, f32[4,8,128]{2,1,0:T(8,128)S(1)}, u32[]{:S(2)}, u32[]{:S(2)}) collective-permute-start(f32[4,8,128]{2,1,0:T(8,128)S(1)} %add.10), channel_id=1, source_target_pairs={{0,16},{8,24},{16,0},{24,8},{1,17},{9,25},{17,1},{25,9},{2,18},{10... | collective-permute-start | bytes 49160 | tf_op jit(solution)/shard_map/ppermute | solution.py:767

commit v4 on v3

--- a/solution.py
+++ b/solution.py
@@ -47,12 +47,12 @@
     def __init__(self, n, tokens, heads_local, head_dim, ssd_local, state):
         self.n, self.t, self.hl, self.hd, self.ns = n, tokens, heads_local, head_dim, state
         self.s = n * tokens
-        self.shifts = list(range(n))
-        self.back_shifts = sorted(range(n), key=lambda s: (min(s, n - s), s))
         self.a = heads_local // n
         self.sizes = GROUPS if sum(GROUPS) == self.a else (self.a,)
         self.first = [sum(self.sizes[:g]) for g in range(len(self.sizes))]
         self.groups = len(self.sizes)
+        self.shifts = [list(range(n)) for _ in range(self.groups)]
+        self.back_shifts = self.shifts
         self.h = ssd_local // n
         self.hl_ssd = ssd_local
         self.mp = heads_local * head_dim // ssd_local
@@ -205,7 +205,7 @@
                     held[g][j, z.rows_of(g, k, a), :] = turned[j * z.a + z.first[g] + a]
     for g in range(z.groups):
         for s in range(z.n):
-            outs[g * z.n + s][...] = held[g][lax.rem(me + z.shifts[s], z.n)]
+            outs[g * z.n + s][...] = held[g][lax.rem(me + z.shifts[g][s], z.n)]
 
 
 def prep(z, qkv, b, c, step, labels, table):
@@ -237,7 +237,7 @@
     me = lax.axis_index("context")
     first = 3 * z.sizes[0] * z.t
     for s in range(z.n):
-        source = lax.rem(me + z.n - z.shifts[s], z.n)
+        source = lax.rem(me + z.n - z.shifts[0][s], z.n)
         mine[source] = ins[s][first : first + z.t]
         start = first + z.t
         terms = [ins[s][start + k * z.rp : start + k * z.rp + z.r].astype(F32) for k in range(2)]
@@ -311,7 +311,7 @@
     prob, attended, held = refs
     me = lax.axis_index("context")
     for s in range(n):
-        held[lax.rem(me + n - z.shifts[s], n)] = ins[s][: 3 * count * t]
+        held[lax.rem(me + n - z.shifts[g][s], n)] = ins[s][: 3 * count * t]
 
     def rows_upto(k, a, width):
         return held[: width // t, z.rows_of(g, k, a), :].reshape(width, z.hd)
@@ -434,19 +434,60 @@
     )
 
 
+def ssd_pre_kernel(z, bc, saved, w_sums, straddled, down_sums):
+    t = z.t
+    causal = iota((t, t), 0) >= iota((t, t), 1)
+    per_head = mat(iota((z.f, t), 1) == iota((z.f, t), 0) // z.mp).astype(BF16)
+
+    def chunk(c):
+        rows = z.chunk(c)
+        sc, sl, xc, xl = saved[2, rows, :], saved[4, rows, :], saved[0, rows, :], saved[5, rows, :]
+        carried = dot(bc[c, 1], saved[3, rows, :])
+        down_sums[rows, :] = dot(((sc.astype(F32) + sl.astype(F32)) * carried).astype(BF16), per_head)
+        inner = bc[c, 2].astype(F32)
+        w_sum = jnp.zeros((t, t), F32)
+        for k in range(z.h):
+            first = k * z.mp // z.hd * z.hd
+            mine = iota((t, z.hd), 1) // z.mp == k % (z.hd // z.mp)
+            pair = slice(first, first + z.hd)
+            x_head = jnp.where(mine, xc[:, pair], jnp.zeros((), BF16))
+            x_low = jnp.where(mine, xl[:, pair], jnp.zeros((), BF16))
+            left = jnp.concatenate([sc[:, pair], sl[:, pair], sc[:, pair]], axis=1)
+            w = jnp.where(causal, dot_nt(left, jnp.concatenate([x_head, x_head, x_low], axis=1)), 0.0)
+            w_sum += w
+            straddled[rows, k * t : (k + 1) * t] = (w * inner).astype(BF16)
+        w_sums[rows, :] = w_sum
+
+    z.each_chunk(chunk)
+
+
+def ssd_pre(z, bc, saved):
+    return call(
+        z,
+        ssd_pre_kernel,
+        "ssd_pre",
+        (SHAPE((z.s, z.t), F32), SHAPE((z.s, z.h * z.t), BF16), SHAPE((z.s, z.t), F32)),
+        [VM] * 2,
+        [VM] * 3,
+        [],
+        (bc, saved),
+        flops=z.s * z.f * z.ns * 20,
+        nbytes=z.s * z.f * 8,
+    )
+
+
 def ssd_back_kernel(z, *refs):
     n, t = z.n, z.t
     lengths, values, refs = refs[0], refs[1 : n + 1], refs[n + 1 :]
-    terms, bc, saved, refs = *refs[:3], refs[3:]
+    terms, bc, saved, w_sums, straddled, down_sums, refs = *refs[:6], refs[6:]
     grads, keep_out, give_out, step_out, vec, refs = *refs[:5], refs[5:]
-    d, adds, dstates, through = refs
+    d, adds, dstates, through, errors = refs
     me, core = lax.axis_index("context"), lax.axis_index("head")
     length = lengths[lax.axis_index("rollout")]
     value = values[0][...]
     for s in range(1, n):
         value = value + values[s][...]
     row_id, col_id = iota((t, t), 0), iota((t, t), 1)
-    causal = row_id >= col_id
     strict = row_id > col_id
     after = mat(col_id >= row_id).astype(BF16)
     before = mat(strict).astype(BF16)
@@ -469,6 +510,8 @@
         error = jnp.where(valid, value_row - pays(c)[z.h : z.h + 1], 0.0)
         vec[z.features + 1 : z.features + 2, :] += 0.5 * error * error
         column = jnp.transpose(jnp.broadcast_to(error, (t, t)))
+        errors[0, rows, :] = jnp.broadcast_to(error, (t, t))
+        errors[1, rows, :] = column
         wide = jnp.concatenate([column] * (z.f // t), axis=1)
         dc = split3(wide * (saved[2, rows, :].astype(F32) + saved[4, rows, :].astype(F32)))[:2]
         d[0, rows, :] = dc[0]
@@ -503,29 +546,15 @@
         rows = z.chunk(c)
         b, cp, inner = bc[c, 0], bc[c, 1], bc[c, 2]
         dc, dl = d[0, rows, :], d[1, rows, :]
-        xc, xl, state_in, dstate_in = saved[0, rows, :], saved[5, rows, :], saved[3, rows, :], dstates[rows, :]
+        xc, state_in, dstate_in = saved[0, rows, :], saved[3, rows, :], dstates[rows, :]
         local = dot_tn(inner, dc) + dot_tn(inner, dl)
         outer = dot(b, dstate_in)
-        carried = dot(cp, state_in)
         grads[rows, :] = (terms[z.chunk(c, z.down), :] * (local + outer)).astype(BF16)
         grad_c = dot_nt(dc, state_in) + dot_nt(dl, state_in)
         grad_b = dot_nt(xc, dstate_in)
-        down_sum = dot(((dc.astype(F32) + dl.astype(F32)) * carried).astype(BF16), per_head)
+        down_sum = errors[1, rows, :] * down_sums[rows, :]
         up_sum = dot((xc.astype(F32) * outer).astype(BF16), per_head)
-        inner_wide = inner.astype(F32)
-        w_sum = jnp.zeros((t, t), F32)
-        parts = []
-        for k in range(z.h):
-            first = k * z.mp // z.hd * z.hd
-            mine = iota((t, z.hd), 1) // z.mp == k % (z.hd // z.mp)
-            pair = slice(first, first + z.hd)
-            x_head = jnp.where(mine, xc[:, pair], jnp.zeros((), BF16))
-            x_low = jnp.where(mine, xl[:, pair], jnp.zeros((), BF16))
-            left = jnp.concatenate([dc[:, pair], dl[:, pair], dc[:, pair]], axis=1)
-            w = jnp.where(causal, dot_nt(left, jnp.concatenate([x_head, x_head, x_low], axis=1)), 0.0)
-            w_sum += w
-            parts.append((w * inner_wide).astype(BF16))
-        straddle = dot(after, jnp.concatenate(parts, axis=1))
+        straddle = dot(jnp.where(col_id >= row_id, errors[0, rows, :], 0.0).astype(BF16), straddled[rows, :])
         straddle = jnp.concatenate(
             [jnp.where(strict, straddle[:, k * t : (k + 1) * t], 0.0).astype(BF16) for k in range(z.h)], axis=1
         )
@@ -534,7 +563,7 @@
             jnp.concatenate([after, after, before, before], axis=1), jnp.concatenate(sums, axis=0)
         ) + dot(straddle, per_row)
         gain = gain + split2_dot(through[z.small(c, 0, 8), :], per_head)[0:1]
-        w_low = w_sum.astype(BF16)
+        w_low = (errors[1, rows, :] * w_sums[rows, :]).astype(BF16)
         grad_c += dot(w_low, b)
         grad_b += dot_tn(w_low, cp)
         keep_out[c] = jnp.where(core == 0, grad_b, grad_c)
@@ -548,7 +577,7 @@
     z.each_chunk(leave)
 
 
-def ssd_back(z, lengths, values, terms, bc, saved):
+def ssd_back(z, lengths, values, terms, bc, saved, early):
     outs = (
         SHAPE((z.s, z.f), BF16),
         SHAPE((z.n, z.t, z.ns), F32),
@@ -561,16 +590,17 @@
         pltpu.VMEM((z.n * z.ns, z.f), F32),
         pltpu.VMEM((z.n * z.ns, z.f), BF16),
         pltpu.VMEM((z.n * 8, z.f), F32),
+        pltpu.VMEM((2, z.s, z.t), F32),
     ]
     return call(
         z,
         ssd_back_kernel,
         "ssd_back",
         outs,
-        [SM] + [VM] * (z.n + 3),
+        [SM] + [VM] * (z.n + 6),
         [VM] * 5,
         scratch,
-        (lengths, *values, terms, bc, saved),
+        (lengths, *values, terms, bc, saved, *early),
         flops=z.s * z.f * z.ns * 20,
         nbytes=z.s * z.f * 32,
     )
@@ -624,7 +654,7 @@
 
         z.each_block(by_key)
     for s in range(n):
-        outs[s][...] = result[lax.rem(me + z.back_shifts[s], n)]
+        outs[s][...] = result[lax.rem(me + z.back_shifts[g][s], n)]
 
 
 def attend_back(z, g, qkv, prob, grad, small):
@@ -657,7 +687,7 @@
     steps = jnp.zeros((n * z.h, t), F32)
     for s in range(n):
         total = total + parts[s][:t].astype(F32)
-        source = lax.rem(me + n - z.back_shifts[s], n)
+        source = lax.rem(me + n - z.back_shifts[0][s], n)
         row, col = iota((n * z.h, z.r), 0), iota((n * z.h, z.r), 1)
         place = mat((row == source * z.h + col) & (col < z.h)).astype(BF16)
         steps = steps + dot(place, parts[s][t : t + z.r])
@@ -723,7 +753,7 @@
     mover = Copies(sems)
     for g in range(z.groups):
         for s in range(z.n):
-            held[g][lax.rem(me + z.n - z.back_shifts[s], z.n)] = ins[g * z.n + s][: 3 * z.sizes[g] * z.t]
+            held[g][lax.rem(me + z.n - z.back_shifts[g][s], z.n)] = ins[g * z.n + s][: 3 * z.sizes[g] * z.t]
     stores = []
     for k in range(3):
         heads = [
@@ -772,7 +802,7 @@
     z = Sizes(n, qkv.shape[2], qkv.shape[3], qkv.shape[4], step_size.shape[2], ssd_b.shape[2])
 
     sends = prep(z, qkv, ssd_b, ssd_c, jnp.swapaxes(step_size, 1, 2), step_labels, returns)
-    arrived = [spread(sends[g * n : (g + 1) * n], "context", z.shifts) for g in range(z.groups)]
+    arrived = [spread(sends[g * n : (g + 1) * n], "context", z.shifts[g]) for g in range(z.groups)]
     mine, pay = pick(z, arrived[0])
     theirs = shift(mine, "head", 2, 1)
     attended = [attend(z, 0, arrived[0], [])]
@@ -780,13 +810,14 @@
     for g in range(1, z.groups):
         attended.append(attend(z, g, arrived[g], [bc]))
     saved, value = ssd(z, [x[1] for x in attended], terms, bc)
+    early = ssd_pre(z, bc, saved)
     value = value + shift(value, "head", 2, 1)
     values = [value] + [partners(value, "context", s) for s in range(1, n)]
-    grad, keep, give, steps, vec = ssd_back(z, lengths, values, terms, bc, saved)
+    grad, keep, give, steps, vec = ssd_back(z, lengths, values, terms, bc, saved, early)
     finals, small = [], [keep, shift(give, "head", 2, 1), steps, vec]
     for g in range(z.groups):
         back = attend_back(z, g, attended[g][2], attended[g][0], grad, small)
-        finals.append(spread(back, "context", z.back_shifts))
+        finals.append(spread(back, "context", z.back_shifts[g]))
         small = back[:1]
     proj, step_grad, vecs = unpack(z, finals[0])
     other = shift(proj, "head", 2, 1)

time: 112 us -> 107 us (0.955)
  starting transfers between devices: 38.4 us -> 26.2 us
  waiting for transfers between devices: 48.6 us -> 54.6 us
    ppermute x16, starting transfers between devices: 29.1 us -> 16.9 us  [shift(): return lax.ppermute(x, axis, [(i, (i + step) % size) for i in range(size)])]
    ppermute x16, waiting for transfers between devices: 42.5 us -> 50.6 us  [shift(): return lax.ppermute(x, axis, [(i, (i + step) % size) for i in range(size)])]
    ppermute x5, waiting for transfers between devices: 6.1 us -> 4 us  [partners(): lax.ppermute(x, axis, [(i, i ^ step) for i in range(lax.axis_size(axis))])]
    pallas_call x12 -> x13, Pallas kernels: 23.6 us -> 23.8 us  [call(): pl.pallas_call(functools.partial(kernel, z), name=name, out_shape=out_sha...]
  transfers between devices with their start and end apart: 21 -> 21, of which waited for: 12 -> 11; matrix products, arithmetic and copies ran while one was open for 0% -> 0% of each run, Pallas kernels for 7% -> 10%
where the time goes in v4:
time: 107 us; the launch traced here: 105 us
  waiting for transfers between devices  54.6 us (51%)
  starting transfers between devices  26.2 us (24%)
  Pallas kernels  23.8 us (22%)
    ppermute x16, waiting for transfers between devices, shift(): return lax.ppermute(x, axis, [(i, (i + step) % size) for i in range(size)])  50.6 us
    pallas_call x13, Pallas kernels, call(): pl.pallas_call(functools.partial(kernel, z), name=name, out_shape=out_sha...  23.8 us
    ppermute x16, starting transfers between devices, shift(): return lax.ppermute(x, axis, [(i, (i + step) % size) for i in range(size)])  16.9 us
    ppermute x5, starting transfers between devices, partners(): lax.ppermute(x, axis, [(i, i ^ step) for i in range(lax.axis_size(axis))])  9.29 us
    ppermute x5, waiting for transfers between devices, partners(): lax.ppermute(x, axis, [(i, i ^ step) for i in range(lax.axis_size(axis))])  4 us
  transfers between devices with their start and end apart: 21, of which 11 were waited for; matrix products, arithmetic and copies ran while one was open for 0% of the time, Pallas kernels for 10%

profile of v4, /device:TPU:0, one launch (start us, length us, event | category | flops | bytes accessed | tf_op | source)
XLA Modules:
  0.0 105.5 jit_solution(817777703585487001)
XLA Ops:
  0.7 2.0 %prep.1 = (bf16[928,128]{1,0:T(8,128)(2,1)S(1)}, bf16[928,128]{1,0:T(8,128)(2,1)S(1)}, bf16[928,128]{1,0:T(8,128)(2,1)S(1)}, bf16[928,128]{1,0:T(8,128)(2,1)S(1)...) custom-call(bf16[3,1,128,16,128]{4,3,2,1,0:T(8,128)(2,1)} %qkv.1, ...), custom_call_target="tpu_custom_call" | custom-call | bytes 3145728 | tf_op jit(solution)/shard_map/prep/pallas_call | solution.py:127
  2.7 3.1 %collective-permute-start = (bf16[928,128]{1,0:T(8,128)(2,1)S(1)}, bf16[928,128]{1,0:T(8,128)(2,1)S(1)}, u32[]{:S(2)}, u32[]{:S(2)}) collective-permute-start(bf16[928,128]{1,0:T(8,128)(2,1)S(1)} %get-tuple-element.52), channel_id=1, source_target_pairs={{0,2},{2,4},{4,6},{6,0},{1,3},{3,5},{5,7},{7,1},{8,10},{10,12},{12... | collective-permute-start | bytes 712712 | tf_op jit(solution)/shard_map/ppermute | solution.py:789
  5.7 2.6 %collective-permute-start.1 = (bf16[928,128]{1,0:T(8,128)(2,1)S(1)}, bf16[928,128]{1,0:T(8,128)(2,1)S(1)}, u32[]{:S(2)}, u32[]{:S(2)}) collective-permute-start(bf16[928,128]{1,0:T(8,128)(2,1)S(1)} %get-tuple-element.53), channel_id=1, source_target_pairs={{0,4},{2,6},{4,0},{6,2},{1,5},{3,7},{5,1},{7,3},{8,12},{10,14},{12... | collective-permute-start | bytes 712712 | tf_op jit(solution)/shard_map/ppermute | solution.py:789
  8.3 1.3 %collective-permute-start.2 = (bf16[928,128]{1,0:T(8,128)(2,1)S(1)}, bf16[928,128]{1,0:T(8,128)(2,1)S(1)}, u32[]{:S(2)}, u32[]{:S(2)}) collective-permute-start(bf16[928,128]{1,0:T(8,128)(2,1)S(1)} %get-tuple-element.54), channel_id=1, source_target_pairs={{0,6},{2,0},{4,2},{6,4},{1,7},{3,1},{5,3},{7,5},{8,14},{10,8},{12,... | collective-permute-start | bytes 712712 | tf_op jit(solution)/shard_map/ppermute | solution.py:789
  9.7 0.7 collective-permute-start.3
  10.4 0.3 collective-permute-start.4
  10.7 3.8 %collective-permute-done.refs_1_ = bf16[928,128]{1,0:T(8,128)(2,1)S(1)} collective-permute-done((bf16[928,128]{1,0:T(8,128)(2,1)S(1)}, bf16[928,128]{1,0:T(8,128)(2,1)S(1)}, u32[]{:S(2)}, u32[]{:S(2)}) %collective-permute-start) | collective-permute-done | bytes 237600 | tf_op jit(solution)/shard_map/ppermute | solution.py:789
  14.5 2.5 %collective-permute-start.5 = (bf16[768,128]{1,0:T(8,128)(2,1)S(1)}, bf16[768,128]{1,0:T(8,128)(2,1)S(1)}, u32[]{:S(2)}, u32[]{:S(2)}) collective-permute-start(bf16[768,128]{1,0:T(8,128)(2,1)S(1)} %get-tuple-element.61), channel_id=1, source_target_pairs={{0,6},{2,0},{4,2},{6,4},{1,7},{3,1},{5,3},{7,5},{8,14},{10,8},{12,... | collective-permute-start | bytes 589832 | tf_op jit(solution)/shard_map/ppermute | solution.py:789
  17.0 7.7 %collective-permute-done.1.refs_2_ = bf16[928,128]{1,0:T(8,128)(2,1)S(1)} collective-permute-done((bf16[928,128]{1,0:T(8,128)(2,1)S(1)}, bf16[928,128]{1,0:T(8,128)(2,1)S(1)}, u32[]{:S(2)}, u32[]{:S(2)}) %collective-permute-start.1) | collective-permute-done | bytes 237600 | tf_op jit(solution)/shard_map/ppermute | solution.py:789
  24.7 0.0 collective-permute-done.2.refs_3_
  24.8 0.1 collective-permute-start.6
  24.9 1.8 %attend_0.1 = (bf16[2,512,512]{2,1,0:T(8,128)(2,1)S(1)}, bf16[512,256]{1,0:T(8,128)(2,1)S(1)}, bf16[4,768,128]{2,1,0:T(8,128)(2,1)S(1)}) custom-call(bf16[928,128]{1,0:T(8,128)(2,1)S(1)} %get-tuple-element.51.refs_0_, bf16[928,128]{1,0:T(8,128)(2,1)S(1)} %collective-permute-done.refs_1_, bf16[928,128]{1,0:T(8,128)(2,1)S(1)} %collective-permute-done.1.refs_2_, ...), custom_call_target="tpu_custom_call" | custom-call | flops 268435456 | bytes 4194304 | tf_op jit(solution)/shard_map/attend_0/pallas_call | solution.py:127
  26.7 0.0 collective-permute-done.6.theirs
  26.7 2.0 %decay.1 = (f32[1144,512]{1,0:T(8,128)S(1)}, bf16[4,4,128,128]{3,2,1,0:T(8,128)(2,1)S(1)}) custom-call(bf16[4,128,128]{2,1,0:T(8,128)(2,1)S(1)} %get-tuple-element.62.mine, bf16[4,128,128]{2,1,0:T(8,128)(2,1)S(1)} %collective-permute-done.6.theirs, f32[4,16,128]{2,1,0:T(8,128)S(1)} %get-tuple-element.63.pay, f32[1,32]{1,0:T(1,128)S(1)} %bitcast.8, ...), custom_call_target="tpu_custom_call" | custom-call | bytes 2097152 | tf_op jit(solution)/shard_map/decay/pallas_call | solution.py:127
  28.7 0.2 collective-permute-done.3.refs_1_
  29.0 12.7 %collective-permute-done.4.refs_2_ = bf16[768,128]{1,0:T(8,128)(2,1)S(1)} collective-permute-done((bf16[768,128]{1,0:T(8,128)(2,1)S(1)}, bf16[768,128]{1,0:T(8,128)(2,1)S(1)}, u32[]{:S(2)}, u32[]{:S(2)}) %collective-permute-start.4) | collective-permute-done | bytes 196640 | tf_op jit(solution)/shard_map/ppermute | solution.py:789
  41.6 0.0 collective-permute-done.5.refs_3_
  41.6 1.8 %attend_1.1 = (bf16[2,512,512]{2,1,0:T(8,128)(2,1)S(1)}, bf16[512,256]{1,0:T(8,128)(2,1)S(1)}, bf16[4,768,128]{2,1,0:T(8,128)(2,1)S(1)}) custom-call(bf16[768,128]{1,0:T(8,128)(2,1)S(1)} %get-tuple-element.58.refs_0_, bf16[768,128]{1,0:T(8,128)(2,1)S(1)} %collective-permute-done.3.refs_1_, bf16[768,128]{1,0:T(8,128)(2,1)S(1)} %collective-permute-done.4.refs_2_, ...), custom_call_target="tpu_custom_call" | custom-call | flops 268435456 | bytes 4194304 | tf_op jit(solution)/shard_map/attend_1/pallas_call | solution.py:127
  43.5 2.7 %ssd.1 = (bf16[6,512,512]{2,1,0:T(8,128)(2,1)S(1)}, f32[1,512]{1,0:T(1,128)S(1)}) custom-call(bf16[512,256]{1,0:T(8,128)(2,1)S(1)} %get-tuple-element.57.refs_0_, bf16[512,256]{1,0:T(8,128)(2,1)S(1)} %get-tuple-element.65.refs_1_, f32[1144,512]{1,0:T(8,128)S(1)} %get-tuple-element.66.refs_2_.refs_5_, ...), custom_call_target="tpu_custom_call" | custom-call | flops 671088640 | bytes 8388608 | tf_op jit(solution)/shard_map/ssd/pallas_call | solution.py:127
  46.2 0.1 collective-permute-start.7
  46.3 1.1 %collective-permute-done.7 = f32[1,512]{1,0:T(1,128)S(1)} collective-permute-done((f32[1,512]{1,0:T(1,128)S(1)}, f32[1,512]{1,0:T(1,128)S(1)}, u32[]{:S(2)}, u32[]{:S(2)}) %collective-permute-start.7) | collective-permute-done | bytes 2080 | tf_op jit(solution)/shard_map/ppermute | solution.py:789
  47.4 5.7 %collective-permute-start.10 = (f32[1,512]{1,0:T(1,128)S(1)}, f32[1,512]{1,0:T(1,128)S(1)}, u32[]{:S(2)}, u32[]{:S(2)}) collective-permute-start(f32[1,512]{1,0:T(1,128)S(1)} %add.9.refs_1_), channel_id=1, source_target_pairs={{0,6},{2,4},{4,2},{6,0},{1,7},{3,5},{5,3},{7,1},{8,14},{10,12},{12... | collective-permute-start | bytes 6152 | tf_op jit(solution)/shard_map/ppermute | solution.py:797
  53.1 0.5 collective-permute-start.9
  53.6 0.2 collective-permute-start.8
  53.7 2.1 %ssd_pre.1 = (f32[512,128]{1,0:T(8,128)S(1)}, bf16[512,1024]{1,0:T(8,128)(2,1)S(1)}, f32[512,128]{1,0:T(8,128)S(1)}) custom-call(bf16[4,4,128,128]{3,2,1,0:T(8,128)(2,1)S(1)} %get-tuple-element.64.refs_4_.refs_3_.bc.refs_6_, bf16[6,512,512]{2,1,0:T(8,128)(2,1)S(1)} %get-tuple-element.68.saved.refs_7_), custom_call_target="tpu_custom_call" | custom-call | flops 671088640 | bytes 2097152 | tf_op jit(solution)/shard_map/ssd_pre/pallas_call | solution.py:127
  55.8 0.0 collective-permute-done.10.refs_4_
  55.8 1.7 %collective-permute-done.9.refs_3_ = f32[1,512]{1,0:T(1,128)S(1)} collective-permute-done((f32[1,512]{1,0:T(1,128)S(1)}, f32[1,512]{1,0:T(1,128)S(1)}, u32[]{:S(2)}, u32[]{:S(2)}) %collective-permute-start.9) | collective-permute-done | bytes 2080 | tf_op jit(solution)/shard_map/ppermute | solution.py:797
  57.6 0.0 collective-permute-done.8.refs_2_
  57.6 4.0 %ssd_back.1 = (bf16[512,512]{1,0:T(8,128)(2,1)S(1)}, f32[4,128,128]{2,1,0:T(8,128)S(1)}, bf16[4,128,128]{2,1,0:T(8,128)(2,1)S(1)}, f32[4,16,128]{2,1,0:T(8,128)S(1)}, f32[8,128]{1,0:T(8,128)S(1)}) custom-call(s32[4]{0:T(128)S(1)} %copy-done.1, f32[1,512]{1,0:T(1,128)S(1)} %add.9.refs_1_, f32[1,512]{1,0:T(1,128)S(1)} %collective-permute-done.8.refs_2_, ...), custom_call_target="tpu_custom_call" | custom-call | flops 671088640 | bytes 8388608 | tf_op jit(solution)/shard_map/ssd_back/pallas_call | solution.py:127
  61.6 0.1 collective-permute-start.11
  61.6 1.3 %collective-permute-done.11.refs_4_ = bf16[4,128,128]{2,1,0:T(8,128)(2,1)S(1)} collective-permute-done((bf16[4,128,128]{2,1,0:T(8,128)(2,1)S(1)}, bf16[4,128,128]{2,1,0:T(8,128)(2,1)S(1)}, u32[]{:S(2)}, u32[]{:S(2)}) %collective-permute-start.11) | collective-permute-done | bytes 131104 | tf_op jit(solution)/shard_map/ppermute | solution.py:789
  63.0 2.0 %attend_back_0.1 = (bf16[928,128]{1,0:T(8,128)(2,1)S(1)}, bf16[928,128]{1,0:T(8,128)(2,1)S(1)}, bf16[928,128]{1,0:T(8,128)(2,1)S(1)}, bf16[928,128]{1,0:T(8,128)(2,1)S(1)}) custom-call(bf16[4,768,128]{2,1,0:T(8,128)(2,1)S(1)} %get-tuple-element.55.refs_0_, bf16[2,512,512]{2,1,0:T(8,128)(2,1)S(1)} %get-tuple-element.56.refs_1_, ...), custom_call_target="tpu_custom_call" | custom-call | flops 536870912 | bytes 4194304 | tf_op jit(solution)/shard_map/attend_back_0/pallas_call | solution.py:127
  65.0 0.2 collective-permute-start.12
  65.2 2.5 %collective-permute-start.13 = (bf16[928,128]{1,0:T(8,128)(2,1)S(1)}, bf16[928,128]{1,0:T(8,128)(2,1)S(1)}, u32[]{:S(2)}, u32[]{:S(2)}) collective-permute-start(bf16[928,128]{1,0:T(8,128)(2,1)S(1)} %get-tuple-element.79), channel_id=1, source_target_pairs={{0,4},{2,6},{4,0},{6,2},{1,5},{3,7},{5,1},{7,3},{8,12},{10,14},{12... | collective-permute-start | bytes 712712 | tf_op jit(solution)/shard_map/ppermute | solution.py:789
  67.7 2.3 %collective-permute-start.14 = (bf16[928,128]{1,0:T(8,128)(2,1)S(1)}, bf16[928,128]{1,0:T(8,128)(2,1)S(1)}, u32[]{:S(2)}, u32[]{:S(2)}) collective-permute-start(bf16[928,128]{1,0:T(8,128)(2,1)S(1)} %get-tuple-element.80), channel_id=1, source_target_pairs={{0,6},{2,0},{4,2},{6,4},{1,7},{3,1},{5,3},{7,5},{8,14},{10,8},{12,... | collective-permute-start | bytes 712712 | tf_op jit(solution)/shard_map/ppermute | solution.py:789
  70.0 1.8 %attend_back_1.1 = (bf16[768,128]{1,0:T(8,128)(2,1)S(1)}, bf16[768,128]{1,0:T(8,128)(2,1)S(1)}, bf16[768,128]{1,0:T(8,128)(2,1)S(1)}, bf16[768,128]{1,0:T(8,128)(2,1)S(1)}) custom-call(bf16[4,768,128]{2,1,0:T(8,128)(2,1)S(1)} %get-tuple-element.84.refs_0_, bf16[2,512,512]{2,1,0:T(8,128)(2,1)S(1)} %get-tuple-element.85.refs_1_, ...), custom_call_target="tpu_custom_call" | custom-call | flops 536870912 | bytes 4194304 | tf_op jit(solution)/shard_map/attend_back_1/pallas_call | solution.py:127
  71.8 0.1 collective-permute-start.18
  71.9 1.0 collective-permute-start.19
  72.9 2.7 %collective-permute-done.12.refs_1_ = bf16[928,128]{1,0:T(8,128)(2,1)S(1)} collective-permute-done((bf16[928,128]{1,0:T(8,128)(2,1)S(1)}, bf16[928,128]{1,0:T(8,128)(2,1)S(1)}, u32[]{:S(2)}, u32[]{:S(2)}) %collective-permute-start.12) | collective-permute-done | bytes 237600 | tf_op jit(solution)/shard_map/ppermute | solution.py:789
  75.6 0.1 collective-permute-start.20
  75.7 10.0 %collective-permute-done.13.refs_2_ = bf16[928,128]{1,0:T(8,128)(2,1)S(1)} collective-permute-done((bf16[928,128]{1,0:T(8,128)(2,1)S(1)}, bf16[928,128]{1,0:T(8,128)(2,1)S(1)}, u32[]{:S(2)}, u32[]{:S(2)}) %collective-permute-start.13) | collective-permute-done | bytes 237600 | tf_op jit(solution)/shard_map/ppermute | solution.py:789
  85.8 0.8 unpack.1
  86.5 1.5 %collective-permute-start.16 = (f32[4,8,128]{2,1,0:T(8,128)S(1)}, f32[4,8,128]{2,1,0:T(8,128)S(1)}, u32[]{:S(2)}, u32[]{:S(2)}) collective-permute-start(f32[4,8,128]{2,1,0:T(8,128)S(1)} %get-tuple-element.82), channel_id=1, source_target_pairs={{0,8},{8,0},{16,24},{24,16},{1,9},{9,1},{17,25},{25,17},{2,10},{10... | collective-permute-start | bytes 49160 | tf_op jit(solution)/shard_map/ppermute | solution.py:797
  88.0 2.2 %collective-permute-done.16 = f32[4,8,128]{2,1,0:T(8,128)S(1)} collective-permute-done((f32[4,8,128]{2,1,0:T(8,128)S(1)}, f32[4,8,128]{2,1,0:T(8,128)S(1)}, u32[]{:S(2)}, u32[]{:S(2)}) %collective-permute-start.16) | collective-permute-done | bytes 16416 | tf_op jit(solution)/shard_map/ppermute | solution.py:797
  90.3 1.5 %collective-permute-start.17 = (f32[4,8,128]{2,1,0:T(8,128)S(1)}, f32[4,8,128]{2,1,0:T(8,128)S(1)}, u32[]{:S(2)}, u32[]{:S(2)}) collective-permute-start(f32[4,8,128]{2,1,0:T(8,128)S(1)} %add.10), channel_id=1, source_target_pairs={{0,16},{8,24},{16,0},{24,8},{1,17},{9,25},{17,1},{25,9},{2,18},{10... | collective-permute-start | bytes 49160 | tf_op jit(solution)/shard_map/ppermute | solution.py:797
  91.8 10.9 %collective-permute-done.19.refs_6_ = bf16[768,128]{1,0:T(8,128)(2,1)S(1)} collective-permute-done((bf16[768,128]{1,0:T(8,128)(2,1)S(1)}, bf16[768,128]{1,0:T(8,128)(2,1)S(1)}, u32[]{:S(2)}, u32[]{:S(2)}) %collective-permute-start.19) | collective-permute-done | bytes 196640 | tf_op jit(solution)/shard_map/ppermute | solution.py:789
  102.7 1.5 %finish.1 = bf16[3,1,128,16,128]{4,3,2,1,0:T(8,128)(2,1)} custom-call(bf16[928,128]{1,0:T(8,128)(2,1)S(1)} %get-tuple-element.77.refs_0_.refs_3_, bf16[928,128]{1,0:T(8,128)(2,1)S(1)} %collective-permute-done.12.refs_1_, bf16[928,128]{1,0:T(8,128)(2,1)S(1)} %collective-permute-done.13.refs_2_, bf16[928,128]{1,0:T(8,128)(2,1)S(1)} %collective-permute-done.14.refs_3_, ...), custom_call_target="tpu_custom_call" | custom-call | bytes 3145728 | tf_op jit(solution)/shard_map/finish/pallas_call | solution.py:127
  104.2 1.2 %choose.1 = (f32[1,128,128]{2,1,0:T(8,128)}, f32[1,128,128]{2,1,0:T(8,128)}, f32[4,4,128]{2,1,0:T(4,128)}, f32[1,32]{1,0:T(1,128)}, f32[1,1]{1,0:T(1,128)}) custom-call(s32[4]{0:T(128)S(1)} %copy-done.1, f32[128,128]{1,0:T(8,128)S(1)} %get-tuple-element.81.mine, f32[128,128]{1,0:T(8,128)S(1)} %collective-permute-done.15.theirs, f32[4,8,128]{2,1,0:T(8,128)S(1)} %add.11.vecs), custom_call_target="tpu_custom_call" | custom-call | tf_op jit(solution)/shard_map/choose/pallas_call | solution.py:127
  (16 shorter events, 0.1 us)
Async XLA Ops:
  0.6 26.1 %copy-start = (bf16[2048]{0:T(1024)(128)(2,1)S(1)}, bf16[2048]{0:T(1024)(128)(2,1)}, u32[]{:S(2)}) copy-start(bf16[2048]{0:T(1024)(128)(2,1)} %param.14) | copy-start | bytes 12292
  0.6 26.1 %copy-start.2 = (f32[32]{0:T(128)S(1)}, f32[32]{0:T(128)}, u32[]{:S(2)}) copy-start(f32[32]{0:T(128)} %param.13) | copy-start | bytes 388
  2.7 11.9 %collective-permute-start = (bf16[928,128]{1,0:T(8,128)(2,1)S(1)}, bf16[928,128]{1,0:T(8,128)(2,1)S(1)}, u32[]{:S(2)}, u32[]{:S(2)}) collective-permute-start(bf16[928,128]{1,0:T(8,128)(2,1)S(1)} %get-tuple-element.52), channel_id=1, source_target_pairs={{0,2},{2,4},{4,6},{6,0},{1,3},{3,5},{5,7},{7,1},{8,10},{10,12},{12... | collective-permute-start | bytes 712712 | tf_op jit(solution)/shard_map/ppermute | solution.py:789
  5.7 19.0 %collective-permute-start.1 = (bf16[928,128]{1,0:T(8,128)(2,1)S(1)}, bf16[928,128]{1,0:T(8,128)(2,1)S(1)}, u32[]{:S(2)}, u32[]{:S(2)}) collective-permute-start(bf16[928,128]{1,0:T(8,128)(2,1)S(1)} %get-tuple-element.53), channel_id=1, source_target_pairs={{0,4},{2,6},{4,0},{6,2},{1,5},{3,7},{5,1},{7,3},{8,12},{10,14},{12... | collective-permute-start | bytes 712712 | tf_op jit(solution)/shard_map/ppermute | solution.py:789
  8.3 16.4 %collective-permute-start.2 = (bf16[928,128]{1,0:T(8,128)(2,1)S(1)}, bf16[928,128]{1,0:T(8,128)(2,1)S(1)}, u32[]{:S(2)}, u32[]{:S(2)}) collective-permute-start(bf16[928,128]{1,0:T(8,128)(2,1)S(1)} %get-tuple-element.54), channel_id=1, source_target_pairs={{0,6},{2,0},{4,2},{6,4},{1,7},{3,1},{5,3},{7,5},{8,14},{10,8},{12,... | collective-permute-start | bytes 712712 | tf_op jit(solution)/shard_map/ppermute | solution.py:789
  9.7 19.3 %collective-permute-start.3 = (bf16[768,128]{1,0:T(8,128)(2,1)S(1)}, bf16[768,128]{1,0:T(8,128)(2,1)S(1)}, u32[]{:S(2)}, u32[]{:S(2)}) collective-permute-start(bf16[768,128]{1,0:T(8,128)(2,1)S(1)} %get-tuple-element.59), channel_id=1, source_target_pairs={{0,2},{2,4},{4,6},{6,0},{1,3},{3,5},{5,7},{7,1},{8,10},{10,12},{12... | collective-permute-start | bytes 589832 | tf_op jit(solution)/shard_map/ppermute | solution.py:789
  10.4 31.3 %collective-permute-start.4 = (bf16[768,128]{1,0:T(8,128)(2,1)S(1)}, bf16[768,128]{1,0:T(8,128)(2,1)S(1)}, u32[]{:S(2)}, u32[]{:S(2)}) collective-permute-start(bf16[768,128]{1,0:T(8,128)(2,1)S(1)} %get-tuple-element.60), channel_id=1, source_target_pairs={{0,4},{2,6},{4,0},{6,2},{1,5},{3,7},{5,1},{7,3},{8,12},{10,14},{12... | collective-permute-start | bytes 589832 | tf_op jit(solution)/shard_map/ppermute | solution.py:789
  14.5 27.1 %collective-permute-start.5 = (bf16[768,128]{1,0:T(8,128)(2,1)S(1)}, bf16[768,128]{1,0:T(8,128)(2,1)S(1)}, u32[]{:S(2)}, u32[]{:S(2)}) collective-permute-start(bf16[768,128]{1,0:T(8,128)(2,1)S(1)} %get-tuple-element.61), channel_id=1, source_target_pairs={{0,6},{2,0},{4,2},{6,4},{1,7},{3,1},{5,3},{7,5},{8,14},{10,8},{12,... | collective-permute-start | bytes 589832 | tf_op jit(solution)/shard_map/ppermute | solution.py:789
  24.8 1.9 %collective-permute-start.6 = (bf16[4,128,128]{2,1,0:T(8,128)(2,1)S(1)}, bf16[4,128,128]{2,1,0:T(8,128)(2,1)S(1)}, u32[]{:S(2)}, u32[]{:S(2)}) collective-permute-start(bf16[4,128,128]{2,1,0:T(8,128)(2,1)S(1)} %get-tuple-element.62.mine), channel_id=1, source_target_pairs={{0,1},{1,0},{2,3},{3,2},{4,5},{5,4},{6,7},{7,6},{8,9},{9,8},{10,11... | collective-permute-start | bytes 393224 | tf_op jit(solution)/shard_map/ppermute | solution.py:789
  46.2 11.4 %copy-start.1 = (s32[4]{0:T(128)S(1)}, s32[4]{0:T(128)}, u32[]{:S(2)}) copy-start(s32[4]{0:T(128)} %lengths.1) | copy-start | bytes 52
  46.2 1.2 %collective-permute-start.7 = (f32[1,512]{1,0:T(1,128)S(1)}, f32[1,512]{1,0:T(1,128)S(1)}, u32[]{:S(2)}, u32[]{:S(2)}) collective-permute-start(f32[1,512]{1,0:T(1,128)S(1)} %get-tuple-element.67), channel_id=1, source_target_pairs={{0,1},{1,0},{2,3},{3,2},{4,5},{5,4},{6,7},{7,6},{8,9},{9,8},{10,11... | collective-permute-start | bytes 6152 | tf_op jit(solution)/shard_map/ppermute | solution.py:789
  47.4 8.4 %collective-permute-start.10 = (f32[1,512]{1,0:T(1,128)S(1)}, f32[1,512]{1,0:T(1,128)S(1)}, u32[]{:S(2)}, u32[]{:S(2)}) collective-permute-start(f32[1,512]{1,0:T(1,128)S(1)} %add.9.refs_1_), channel_id=1, source_target_pairs={{0,6},{2,4},{4,2},{6,0},{1,7},{3,5},{5,3},{7,1},{8,14},{10,12},{12... | collective-permute-start | bytes 6152 | tf_op jit(solution)/shard_map/ppermute | solution.py:797
  53.1 4.5 %collective-permute-start.9 = (f32[1,512]{1,0:T(1,128)S(1)}, f32[1,512]{1,0:T(1,128)S(1)}, u32[]{:S(2)}, u32[]{:S(2)}) collective-permute-start(f32[1,512]{1,0:T(1,128)S(1)} %add.9.refs_1_), channel_id=1, source_target_pairs={{0,4},{2,6},{4,0},{6,2},{1,5},{3,7},{5,1},{7,3},{8,12},{10,14},{12... | collective-permute-start | bytes 6152 | tf_op jit(solution)/shard_map/ppermute | solution.py:797
  53.6 4.0 %collective-permute-start.8 = (f32[1,512]{1,0:T(1,128)S(1)}, f32[1,512]{1,0:T(1,128)S(1)}, u32[]{:S(2)}, u32[]{:S(2)}) collective-permute-start(f32[1,512]{1,0:T(1,128)S(1)} %add.9.refs_1_), channel_id=1, source_target_pairs={{0,2},{2,0},{4,6},{6,4},{1,3},{3,1},{5,7},{7,5},{8,10},{10,8},{12,... | collective-permute-start | bytes 6152 | tf_op jit(solution)/shard_map/ppermute | solution.py:797
  61.6 1.4 %collective-permute-start.11 = (bf16[4,128,128]{2,1,0:T(8,128)(2,1)S(1)}, bf16[4,128,128]{2,1,0:T(8,128)(2,1)S(1)}, u32[]{:S(2)}, u32[]{:S(2)}) collective-permute-start(bf16[4,128,128]{2,1,0:T(8,128)(2,1)S(1)} %get-tuple-element.74), channel_id=1, source_target_pairs={{0,1},{1,0},{2,3},{3,2},{4,5},{5,4},{6,7},{7,6},{8,9},{9,8},{10,11... | collective-permute-start | bytes 393224 | tf_op jit(solution)/shard_map/ppermute | solution.py:789
  65.0 10.6 %collective-permute-start.12 = (bf16[928,128]{1,0:T(8,128)(2,1)S(1)}, bf16[928,128]{1,0:T(8,128)(2,1)S(1)}, u32[]{:S(2)}, u32[]{:S(2)}) collective-permute-start(bf16[928,128]{1,0:T(8,128)(2,1)S(1)} %get-tuple-element.78), channel_id=1, source_target_pairs={{0,2},{2,4},{4,6},{6,0},{1,3},{3,5},{5,7},{7,1},{8,10},{10,12},{12... | collective-permute-start | bytes 712712 | tf_op jit(solution)/shard_map/ppermute | solution.py:789
  65.2 20.6 %collective-permute-start.13 = (bf16[928,128]{1,0:T(8,128)(2,1)S(1)}, bf16[928,128]{1,0:T(8,128)(2,1)S(1)}, u32[]{:S(2)}, u32[]{:S(2)}) collective-permute-start(bf16[928,128]{1,0:T(8,128)(2,1)S(1)} %get-tuple-element.79), channel_id=1, source_target_pairs={{0,4},{2,6},{4,0},{6,2},{1,5},{3,7},{5,1},{7,3},{8,12},{10,14},{12... | collective-permute-start | bytes 712712 | tf_op jit(solution)/shard_map/ppermute | solution.py:789
  67.7 18.1 %collective-permute-start.14 = (bf16[928,128]{1,0:T(8,128)(2,1)S(1)}, bf16[928,128]{1,0:T(8,128)(2,1)S(1)}, u32[]{:S(2)}, u32[]{:S(2)}) collective-permute-start(bf16[928,128]{1,0:T(8,128)(2,1)S(1)} %get-tuple-element.80), channel_id=1, source_target_pairs={{0,6},{2,0},{4,2},{6,4},{1,7},{3,1},{5,3},{7,5},{8,14},{10,8},{12,... | collective-permute-start | bytes 712712 | tf_op jit(solution)/shard_map/ppermute | solution.py:789
  71.8 19.9 %collective-permute-start.18 = (bf16[768,128]{1,0:T(8,128)(2,1)S(1)}, bf16[768,128]{1,0:T(8,128)(2,1)S(1)}, u32[]{:S(2)}, u32[]{:S(2)}) collective-permute-start(bf16[768,128]{1,0:T(8,128)(2,1)S(1)} %get-tuple-element.87), channel_id=1, source_target_pairs={{0,2},{2,4},{4,6},{6,0},{1,3},{3,5},{5,7},{7,1},{8,10},{10,12},{12... | collective-permute-start | bytes 589832 | tf_op jit(solution)/shard_map/ppermute | solution.py:789
  71.9 30.8 %collective-permute-start.19 = (bf16[768,128]{1,0:T(8,128)(2,1)S(1)}, bf16[768,128]{1,0:T(8,128)(2,1)S(1)}, u32[]{:S(2)}, u32[]{:S(2)}) collective-permute-start(bf16[768,128]{1,0:T(8,128)(2,1)S(1)} %get-tuple-element.88), channel_id=1, source_target_pairs={{0,4},{2,6},{4,0},{6,2},{1,5},{3,7},{5,1},{7,3},{8,12},{10,14},{12... | collective-permute-start | bytes 589832 | tf_op jit(solution)/shard_map/ppermute | solution.py:789
  75.6 27.1 %collective-permute-start.20 = (bf16[768,128]{1,0:T(8,128)(2,1)S(1)}, bf16[768,128]{1,0:T(8,128)(2,1)S(1)}, u32[]{:S(2)}, u32[]{:S(2)}) collective-permute-start(bf16[768,128]{1,0:T(8,128)(2,1)S(1)} %get-tuple-element.89), channel_id=1, source_target_pairs={{0,6},{2,0},{4,2},{6,4},{1,7},{3,1},{5,3},{7,5},{8,14},{10,8},{12,... | collective-permute-start | bytes 589832 | tf_op jit(solution)/shard_map/ppermute | solution.py:789
  86.5 17.7 %collective-permute-start.15 = (f32[128,128]{1,0:T(8,128)S(1)}, f32[128,128]{1,0:T(8,128)S(1)}, u32[]{:S(2)}, u32[]{:S(2)}) collective-permute-start(f32[128,128]{1,0:T(8,128)S(1)} %get-tuple-element.81.mine), channel_id=1, source_target_pairs={{0,1},{1,0},{2,3},{3,2},{4,5},{5,4},{6,7},{7,6},{8,9},{9,8},{10,11... | collective-permute-start | bytes 196616 | tf_op jit(solution)/shard_map/ppermute | solution.py:789
  86.5 3.7 %collective-permute-start.16 = (f32[4,8,128]{2,1,0:T(8,128)S(1)}, f32[4,8,128]{2,1,0:T(8,128)S(1)}, u32[]{:S(2)}, u32[]{:S(2)}) collective-permute-start(f32[4,8,128]{2,1,0:T(8,128)S(1)} %get-tuple-element.82), channel_id=1, source_target_pairs={{0,8},{8,0},{16,24},{24,16},{1,9},{9,1},{17,25},{25,17},{2,10},{10... | collective-permute-start | bytes 49160 | tf_op jit(solution)/shard_map/ppermute | solution.py:797
  90.3 13.9 %collective-permute-start.17 = (f32[4,8,128]{2,1,0:T(8,128)S(1)}, f32[4,8,128]{2,1,0:T(8,128)S(1)}, u32[]{:S(2)}, u32[]{:S(2)}) collective-permute-start(f32[4,8,128]{2,1,0:T(8,128)S(1)} %add.10), channel_id=1, source_target_pairs={{0,16},{8,24},{16,0},{24,8},{1,17},{9,25},{17,1},{25,9},{2,18},{10... | collective-permute-start | bytes 49160 | tf_op jit(solution)/shard_map/ppermute | solution.py:797

commit v5 on v4

--- a/solution.py
+++ b/solution.py
@@ -51,8 +51,10 @@
         self.sizes = GROUPS if sum(GROUPS) == self.a else (self.a,)
         self.first = [sum(self.sizes[:g]) for g in range(len(self.sizes))]
         self.groups = len(self.sizes)
-        self.shifts = [list(range(n)) for _ in range(self.groups)]
-        self.back_shifts = self.shifts
+        natural = list(range(n))
+        half_first = sorted(natural, key=lambda s: (s != 0, s != n // 2, s))
+        self.shifts = [natural for _ in self.sizes]
+        self.back_shifts = [half_first for _ in self.sizes]
         self.h = ssd_local // n
         self.hl_ssd = ssd_local
         self.mp = heads_local * head_dim // ssd_local
@@ -64,6 +66,8 @@
         self.rows = min(256, self.s)
         self.blocks = self.s // self.rows
         self.static = self.blocks <= 2
+        self.parts = 2 if self.static and n % 2 == 0 else 1
+        self.per = n // self.parts
         self.up, self.down, self.mid = 0, self.s, 2 * self.s
         self.pay = self.mid + 8 * n
         self.rate = self.pay + self.r * n
@@ -307,7 +311,7 @@
 
 def attend_kernel(z, g, *refs):
     n, t, count = z.n, z.t, z.sizes[g]
-    ins, refs = refs[:n], refs[n + (1 if g else 0) :]
+    ins, refs = refs[:n], refs[n:]
     prob, attended, held = refs
     me = lax.axis_index("context")
     for s in range(n):
@@ -337,7 +341,7 @@
         z.each_block(attend)
 
 
-def attend(z, g, ins, after):
+def attend(z, g, ins):
     count = z.sizes[g]
     outs = (
         SHAPE((count, z.s, z.s), BF16),
@@ -349,10 +353,10 @@
         lambda z, *refs: attend_kernel(z, g, *refs),
         "attend_%d" % g,
         outs,
-        [VM] * z.n + [ANY] * len(after),
+        [VM] * z.n,
         [VM] * 3,
         [],
-        (*ins, *after),
+        ins,
         flops=count * z.s * z.s * z.hd * 4,
         nbytes=count * z.s * z.s * 8,
     )
@@ -416,34 +420,49 @@
     z.each_chunk(leave)
 
 
-def ssd(z, ins, terms, bc):
-    return call(
-        z,
-        ssd_kernel,
-        "ssd",
-        (SHAPE((6, z.s, z.f), BF16), SHAPE((1, z.s), F32)),
-        [VM] * (z.groups + 2),
-        [VM] * 2,
+def last_kernel(z, *refs):
+    n, g = z.n, z.groups - 1
+    ins, before, refs = refs[:n], refs[n : n + g], refs[n + g :]
+    terms, bc, prob, attended, held, *rest = refs
+    attend_kernel(z, g, *ins, prob, attended, held)
+    ssd_kernel(z, *before, attended, terms, bc, *rest)
+
+
+def attend_and_ssd(z, ins, before, terms, bc):
+    count = z.sizes[-1]
+    return call(
+        z,
+        last_kernel,
+        "attend_and_ssd",
+        (
+            SHAPE((count, z.s, z.s), BF16),
+            SHAPE((z.s, count * z.hd), BF16),
+            SHAPE((z.n, 3 * count * z.t, z.hd), BF16),
+            SHAPE((6, z.s, z.f), BF16),
+            SHAPE((1, z.s), F32),
+        ),
+        [VM] * (z.n + z.groups + 1),
+        [VM] * 5,
         [
             pltpu.VMEM((z.s, z.f), BF16),
             pltpu.VMEM((z.n * z.ns, z.f), F32),
         ],
-        (*ins, terms, bc),
+        (*ins, *before, terms, bc),
         flops=z.s * z.f * z.ns * 20,
         nbytes=z.s * z.f * 32,
     )
 
 
-def ssd_pre_kernel(z, bc, saved, w_sums, straddled, down_sums):
+def ssd_pre_kernel(z, part, bc, saved, w_sums, straddled, down_sums):
     t = z.t
     causal = iota((t, t), 0) >= iota((t, t), 1)
     per_head = mat(iota((z.f, t), 1) == iota((z.f, t), 0) // z.mp).astype(BF16)
 
     def chunk(c):
-        rows = z.chunk(c)
+        rows, here = z.chunk(c), z.chunk(c - part * z.per)
         sc, sl, xc, xl = saved[2, rows, :], saved[4, rows, :], saved[0, rows, :], saved[5, rows, :]
         carried = dot(bc[c, 1], saved[3, rows, :])
-        down_sums[rows, :] = dot(((sc.astype(F32) + sl.astype(F32)) * carried).astype(BF16), per_head)
+        down_sums[here, :] = dot(((sc.astype(F32) + sl.astype(F32)) * carried).astype(BF16), per_head)
         inner = bc[c, 2].astype(F32)
         w_sum = jnp.zeros((t, t), F32)
         for k in range(z.h):
@@ -455,31 +474,42 @@
             left = jnp.concatenate([sc[:, pair], sl[:, pair], sc[:, pair]], axis=1)
             w = jnp.where(causal, dot_nt(left, jnp.concatenate([x_head, x_head, x_low], axis=1)), 0.0)
             w_sum += w
-            straddled[rows, k * t : (k + 1) * t] = (w * inner).astype(BF16)
-        w_sums[rows, :] = w_sum
-
-    z.each_chunk(chunk)
-
-
-def ssd_pre(z, bc, saved):
-    return call(
-        z,
-        ssd_pre_kernel,
-        "ssd_pre",
-        (SHAPE((z.s, z.t), F32), SHAPE((z.s, z.h * z.t), BF16), SHAPE((z.s, z.t), F32)),
+            straddled[here, k * t : (k + 1) * t] = (w * inner).astype(BF16)
+        w_sums[here, :] = w_sum
+
+    if z.parts > 1:
+        for c in range(part * z.per, (part + 1) * z.per):
+            chunk(c)
+    else:
+        z.each_chunk(chunk)
+
+
+def ssd_pre(z, part, bc, saved):
+    rows = z.per * z.t
+    return call(
+        z,
+        lambda z, *refs: ssd_pre_kernel(z, part, *refs),
+        "ssd_pre_%d" % part,
+        (SHAPE((rows, z.t), F32), SHAPE((rows, z.h * z.t), BF16), SHAPE((rows, z.t), F32)),
         [VM] * 2,
         [VM] * 3,
         [],
         (bc, saved),
-        flops=z.s * z.f * z.ns * 20,
-        nbytes=z.s * z.f * 8,
+        flops=rows * z.f * z.ns * 20,
+        nbytes=rows * z.f * 8,
     )
 
 
 def ssd_back_kernel(z, *refs):
     n, t = z.n, z.t
     lengths, values, refs = refs[0], refs[1 : n + 1], refs[n + 1 :]
-    terms, bc, saved, w_sums, straddled, down_sums, refs = *refs[:6], refs[6:]
+    terms, bc, saved, refs = *refs[:3], refs[3:]
+    early, refs = refs[: 3 * z.parts], refs[3 * z.parts :]
+
+    def made(kind, c):
+        part = c // z.per if z.parts > 1 else 0
+        return early[3 * part + kind][z.chunk(c - part * z.per), :]
+
     grads, keep_out, give_out, step_out, vec, refs = *refs[:5], refs[5:]
     d, adds, dstates, through, errors = refs
     me, core = lax.axis_index("context"), lax.axis_index("head")
@@ -552,9 +582,9 @@
         grads[rows, :] = (terms[z.chunk(c, z.down), :] * (local + outer)).astype(BF16)
         grad_c = dot_nt(dc, state_in) + dot_nt(dl, state_in)
         grad_b = dot_nt(xc, dstate_in)
-        down_sum = errors[1, rows, :] * down_sums[rows, :]
+        down_sum = errors[1, rows, :] * made(2, c)
         up_sum = dot((xc.astype(F32) * outer).astype(BF16), per_head)
-        straddle = dot(jnp.where(col_id >= row_id, errors[0, rows, :], 0.0).astype(BF16), straddled[rows, :])
+        straddle = dot(jnp.where(col_id >= row_id, errors[0, rows, :], 0.0).astype(BF16), made(1, c))
         straddle = jnp.concatenate(
             [jnp.where(strict, straddle[:, k * t : (k + 1) * t], 0.0).astype(BF16) for k in range(z.h)], axis=1
         )
@@ -563,7 +593,7 @@
             jnp.concatenate([after, after, before, before], axis=1), jnp.concatenate(sums, axis=0)
         ) + dot(straddle, per_row)
         gain = gain + split2_dot(through[z.small(c, 0, 8), :], per_head)[0:1]
-        w_low = (errors[1, rows, :] * w_sums[rows, :]).astype(BF16)
+        w_low = (errors[1, rows, :] * made(0, c)).astype(BF16)
         grad_c += dot(w_low, b)
         grad_b += dot_tn(w_low, cp)
         keep_out[c] = jnp.where(core == 0, grad_b, grad_c)
@@ -597,7 +627,7 @@
         ssd_back_kernel,
         "ssd_back",
         outs,
-        [SM] + [VM] * (z.n + 6),
+        [SM] + [VM] * (z.n + 3 + 3 * z.parts),
         [VM] * 5,
         scratch,
         (lengths, *values, terms, bc, saved, *early),
@@ -805,13 +835,15 @@
     arrived = [spread(sends[g * n : (g + 1) * n], "context", z.shifts[g]) for g in range(z.groups)]
     mine, pay = pick(z, arrived[0])
     theirs = shift(mine, "head", 2, 1)
-    attended = [attend(z, 0, arrived[0], [])]
+    attended = [attend(z, g, arrived[g]) for g in range(z.groups - 1)]
     terms, bc = decay(z, mine, theirs, pay, decay_rate.reshape(1, -1), value_weight.reshape(z.hl, z.hd))
-    for g in range(1, z.groups):
-        attended.append(attend(z, g, arrived[g], [bc]))
-    saved, value = ssd(z, [x[1] for x in attended], terms, bc)
-    early = ssd_pre(z, bc, saved)
-    value = value + shift(value, "head", 2, 1)
+    *last, saved, value = attend_and_ssd(z, arrived[-1], [x[1] for x in attended], terms, bc)
+    attended.append(last)
+    early = ssd_pre(z, 0, bc, saved)
+    other, *early = lax.optimization_barrier((shift(value, "head", 2, 1), *early))
+    for part in range(1, z.parts):
+        early += ssd_pre(z, part, bc, saved)
+    value = value + other
     values = [value] + [partners(value, "context", s) for s in range(1, n)]
     grad, keep, give, steps, vec = ssd_back(z, lengths, values, terms, bc, saved, early)
     finals, small = [], [keep, shift(give, "head", 2, 1), steps, vec]

time: 107 us -> 106 us (level)
  waiting for transfers between devices: 54.6 us -> 52.4 us
    ppermute x16, waiting for transfers between devices: 50.6 us -> 47.4 us  [shift(): return lax.ppermute(x, axis, [(i, (i + step) % size) for i in range(size)])]
  transfers between devices with their start and end apart: 21 -> 21, of which waited for: 11 -> 10; matrix products, arithmetic and copies ran while one was open for 0% -> 0% of each run, Pallas kernels for 10% -> 10%
where the time goes in v5:
time: 106 us; the launch traced here: 104 us
  waiting for transfers between devices  52.4 us (49%)
  starting transfers between devices  26.7 us (25%)
  Pallas kernels  23.8 us (22%)
    ppermute x16, waiting for transfers between devices, shift(): return lax.ppermute(x, axis, [(i, (i + step) % size) for i in range(size)])  47.4 us
    pallas_call x13, Pallas kernels, call(): pl.pallas_call(functools.partial(kernel, z), name=name, out_shape=out_sha...  23.8 us
    ppermute x16, starting transfers between devices, shift(): return lax.ppermute(x, axis, [(i, (i + step) % size) for i in range(size)])  17.3 us
    ppermute x5, starting transfers between devices, partners(): lax.ppermute(x, axis, [(i, i ^ step) for i in range(lax.axis_size(axis))])  9.37 us
    ppermute x5, waiting for transfers between devices, partners(): lax.ppermute(x, axis, [(i, i ^ step) for i in range(lax.axis_size(axis))])  4.99 us
  transfers between devices with their start and end apart: 21, of which 10 were waited for; matrix products, arithmetic and copies ran while one was open for 0% of the time, Pallas kernels for 10%

profile of v5, /device:TPU:0, one launch (start us, length us, event | category | flops | bytes accessed | tf_op | source)
XLA Modules:
  0.0 103.7 jit_solution(5885013412953034078)
XLA Ops:
  0.7 2.0 %prep.1 = (bf16[928,128]{1,0:T(8,128)(2,1)S(1)}, bf16[928,128]{1,0:T(8,128)(2,1)S(1)}, bf16[928,128]{1,0:T(8,128)(2,1)S(1)}, bf16[928,128]{1,0:T(8,128)(2,1)S(1)...) custom-call(bf16[3,1,128,16,128]{4,3,2,1,0:T(8,128)(2,1)} %qkv.1, ...), custom_call_target="tpu_custom_call" | custom-call | bytes 3145728 | tf_op jit(solution)/shard_map/prep/pallas_call | solution.py:131
  2.7 3.1 %collective-permute-start = (bf16[928,128]{1,0:T(8,128)(2,1)S(1)}, bf16[928,128]{1,0:T(8,128)(2,1)S(1)}, u32[]{:S(2)}, u32[]{:S(2)}) collective-permute-start(bf16[928,128]{1,0:T(8,128)(2,1)S(1)} %get-tuple-element.58), channel_id=1, source_target_pairs={{0,2},{2,4},{4,6},{6,0},{1,3},{3,5},{5,7},{7,1},{8,10},{10,12},{12... | collective-permute-start | bytes 712712 | tf_op jit(solution)/shard_map/ppermute | solution.py:819
  5.7 2.6 %collective-permute-start.1 = (bf16[928,128]{1,0:T(8,128)(2,1)S(1)}, bf16[928,128]{1,0:T(8,128)(2,1)S(1)}, u32[]{:S(2)}, u32[]{:S(2)}) collective-permute-start(bf16[928,128]{1,0:T(8,128)(2,1)S(1)} %get-tuple-element.59), channel_id=1, source_target_pairs={{0,4},{2,6},{4,0},{6,2},{1,5},{3,7},{5,1},{7,3},{8,12},{10,14},{12... | collective-permute-start | bytes 712712 | tf_op jit(solution)/shard_map/ppermute | solution.py:819
  8.3 1.3 %collective-permute-start.2 = (bf16[928,128]{1,0:T(8,128)(2,1)S(1)}, bf16[928,128]{1,0:T(8,128)(2,1)S(1)}, u32[]{:S(2)}, u32[]{:S(2)}) collective-permute-start(bf16[928,128]{1,0:T(8,128)(2,1)S(1)} %get-tuple-element.60), channel_id=1, source_target_pairs={{0,6},{2,0},{4,2},{6,4},{1,7},{3,1},{5,3},{7,5},{8,14},{10,8},{12,... | collective-permute-start | bytes 712712 | tf_op jit(solution)/shard_map/ppermute | solution.py:819
  9.7 0.7 collective-permute-start.3
  10.4 0.3 collective-permute-start.4
  10.7 3.8 %collective-permute-done.refs_1_ = bf16[928,128]{1,0:T(8,128)(2,1)S(1)} collective-permute-done((bf16[928,128]{1,0:T(8,128)(2,1)S(1)}, bf16[928,128]{1,0:T(8,128)(2,1)S(1)}, u32[]{:S(2)}, u32[]{:S(2)}) %collective-permute-start) | collective-permute-done | bytes 237600 | tf_op jit(solution)/shard_map/ppermute | solution.py:819
  14.5 2.5 %collective-permute-start.5 = (bf16[768,128]{1,0:T(8,128)(2,1)S(1)}, bf16[768,128]{1,0:T(8,128)(2,1)S(1)}, u32[]{:S(2)}, u32[]{:S(2)}) collective-permute-start(bf16[768,128]{1,0:T(8,128)(2,1)S(1)} %get-tuple-element.66), channel_id=1, source_target_pairs={{0,6},{2,0},{4,2},{6,4},{1,7},{3,1},{5,3},{7,5},{8,14},{10,8},{12,... | collective-permute-start | bytes 589832 | tf_op jit(solution)/shard_map/ppermute | solution.py:819
  17.0 7.7 %collective-permute-done.1.refs_2_ = bf16[928,128]{1,0:T(8,128)(2,1)S(1)} collective-permute-done((bf16[928,128]{1,0:T(8,128)(2,1)S(1)}, bf16[928,128]{1,0:T(8,128)(2,1)S(1)}, u32[]{:S(2)}, u32[]{:S(2)}) %collective-permute-start.1) | collective-permute-done | bytes 237600 | tf_op jit(solution)/shard_map/ppermute | solution.py:819
  24.8 0.1 collective-permute-start.6
  24.9 1.8 %attend_0.1 = (bf16[2,512,512]{2,1,0:T(8,128)(2,1)S(1)}, bf16[512,256]{1,0:T(8,128)(2,1)S(1)}, bf16[4,768,128]{2,1,0:T(8,128)(2,1)S(1)}) custom-call(bf16[928,128]{1,0:T(8,128)(2,1)S(1)} %get-tuple-element.57.refs_0_, bf16[928,128]{1,0:T(8,128)(2,1)S(1)} %collective-permute-done.refs_1_, bf16[928,128]{1,0:T(8,128)(2,1)S(1)} %collective-permute-done.1.refs_2_, ...), custom_call_target="tpu_custom_call" | custom-call | flops 268435456 | bytes 4194304 | tf_op jit(solution)/shard_map/attend_0/pallas_call | solution.py:131
  26.7 2.0 %decay.1 = (f32[1144,512]{1,0:T(8,128)S(1)}, bf16[4,4,128,128]{3,2,1,0:T(8,128)(2,1)S(1)}) custom-call(bf16[4,128,128]{2,1,0:T(8,128)(2,1)S(1)} %get-tuple-element.68.mine, bf16[4,128,128]{2,1,0:T(8,128)(2,1)S(1)} %collective-permute-done.6.theirs, f32[4,16,128]{2,1,0:T(8,128)S(1)} %get-tuple-element.69.pay, f32[1,32]{1,0:T(1,128)S(1)} %bitcast.8, ...), custom_call_target="tpu_custom_call" | custom-call | bytes 2097152 | tf_op jit(solution)/shard_map/decay/pallas_call | solution.py:131
  28.7 0.2 collective-permute-done.3.refs_1_
  29.0 12.7 %collective-permute-done.4.refs_2_ = bf16[768,128]{1,0:T(8,128)(2,1)S(1)} collective-permute-done((bf16[768,128]{1,0:T(8,128)(2,1)S(1)}, bf16[768,128]{1,0:T(8,128)(2,1)S(1)}, u32[]{:S(2)}, u32[]{:S(2)}) %collective-permute-start.4) | collective-permute-done | bytes 196640 | tf_op jit(solution)/shard_map/ppermute | solution.py:819
  41.6 0.0 collective-permute-done.5.refs_3_
  41.6 4.4 %attend_and_ssd.1 = (bf16[2,512,512]{2,1,0:T(8,128)(2,1)S(1)}, bf16[512,256]{1,0:T(8,128)(2,1)}, bf16[4,768,128]{2,1,0:T(8,128)(2,1)S(1)}, bf16[6,512,512]{2,1,0:T(8,128)(2,1)S(1)}, f32[1,512]{1,0:T(1,128)S(1)}) custom-call(bf16[768,128]{1,0:T(8,128)(2,1)S(1)} %get-tuple-element.63.refs_0_, bf16[768,128]{1,0:T(8,128)(2,1)S(1)} %collective-permute-done.3.refs_1_, ...), custom_call_target="tpu_custom_call" | custom-call | flops 671088640 | bytes 8388608 | tf_op jit(solution)/shard_map/attend_and_ssd/pallas_call | solution.py:131
  46.0 0.1 collective-permute-start.7
  46.1 1.1 %ssd_pre_0.1 = (f32[256,128]{1,0:T(8,128)S(1)}, bf16[256,1024]{1,0:T(8,128)(2,1)S(1)}, f32[256,128]{1,0:T(8,128)S(1)}) custom-call(bf16[4,4,128,128]{3,2,1,0:T(8,128)(2,1)S(1)} %get-tuple-element.71.refs_6_.refs_0_, bf16[6,512,512]{2,1,0:T(8,128)(2,1)S(1)} %get-tuple-element.73.refs_1_.refs_7_), custom_call_target="tpu_custom_call" | custom-call | flops 335544320 | bytes 1048576 | tf_op jit(solution)/shard_map/ssd_pre_0/pallas_call | solution.py:131
  47.2 0.0 copy-start.1
  47.2 0.0 collective-permute-done.7
  47.3 5.7 %collective-permute-start.10 = (f32[1,512]{1,0:T(1,128)S(1)}, f32[1,512]{1,0:T(1,128)S(1)}, u32[]{:S(2)}, u32[]{:S(2)}) collective-permute-start(f32[1,512]{1,0:T(1,128)S(1)} %add.9.refs_1_), channel_id=1, source_target_pairs={{0,6},{2,4},{4,2},{6,0},{1,7},{3,5},{5,3},{7,1},{8,14},{10,12},{12... | collective-permute-start | bytes 6152 | tf_op jit(solution)/shard_map/ppermute | solution.py:827
  53.0 0.5 collective-permute-start.9
  53.5 0.2 collective-permute-start.8
  53.6 1.1 %ssd_pre_1.1 = (f32[256,128]{1,0:T(8,128)S(1)}, bf16[256,1024]{1,0:T(8,128)(2,1)S(1)}, f32[256,128]{1,0:T(8,128)S(1)}) custom-call(bf16[4,4,128,128]{3,2,1,0:T(8,128)(2,1)S(1)} %get-tuple-element.71.refs_6_.refs_0_, bf16[6,512,512]{2,1,0:T(8,128)(2,1)S(1)} %get-tuple-element.73.refs_1_.refs_7_), custom_call_target="tpu_custom_call" | custom-call | flops 335544320 | bytes 1048576 | tf_op jit(solution)/shard_map/ssd_pre_1/pallas_call | solution.py:131
  54.7 0.0 collective-permute-done.10.refs_4_
  54.7 2.7 %collective-permute-done.9.refs_3_ = f32[1,512]{1,0:T(1,128)S(1)} collective-permute-done((f32[1,512]{1,0:T(1,128)S(1)}, f32[1,512]{1,0:T(1,128)S(1)}, u32[]{:S(2)}, u32[]{:S(2)}) %collective-permute-start.9) | collective-permute-done | bytes 2080 | tf_op jit(solution)/shard_map/ppermute | solution.py:827
  57.5 4.0 %ssd_back.1 = (bf16[512,512]{1,0:T(8,128)(2,1)S(1)}, f32[4,128,128]{2,1,0:T(8,128)S(1)}, bf16[4,128,128]{2,1,0:T(8,128)(2,1)S(1)}, f32[4,16,128]{2,1,0:T(8,128)S(1)}, f32[8,128]{1,0:T(8,128)S(1)}) custom-call(s32[4]{0:T(128)S(1)} %copy-done.1, f32[1,512]{1,0:T(1,128)S(1)} %add.9.refs_1_, f32[1,512]{1,0:T(1,128)S(1)} %collective-permute-done.8.refs_2_, ...), custom_call_target="tpu_custom_call" | custom-call | flops 671088640 | bytes 8388608 | tf_op jit(solution)/shard_map/ssd_back/pallas_call | solution.py:131
  61.5 0.1 collective-permute-start.11
  61.6 1.3 %collective-permute-done.11.refs_4_ = bf16[4,128,128]{2,1,0:T(8,128)(2,1)S(1)} collective-permute-done((bf16[4,128,128]{2,1,0:T(8,128)(2,1)S(1)}, bf16[4,128,128]{2,1,0:T(8,128)(2,1)S(1)}, u32[]{:S(2)}, u32[]{:S(2)}) %collective-permute-start.11) | collective-permute-done | bytes 131104 | tf_op jit(solution)/shard_map/ppermute | solution.py:819
  62.9 2.0 %attend_back_0.1 = (bf16[928,128]{1,0:T(8,128)(2,1)S(1)}, bf16[928,128]{1,0:T(8,128)(2,1)S(1)}, bf16[928,128]{1,0:T(8,128)(2,1)S(1)}, bf16[928,128]{1,0:T(8,128)(2,1)S(1)}) custom-call(bf16[4,768,128]{2,1,0:T(8,128)(2,1)S(1)} %get-tuple-element.61.refs_0_, bf16[2,512,512]{2,1,0:T(8,128)(2,1)S(1)} %get-tuple-element.62.refs_1_, ...), custom_call_target="tpu_custom_call" | custom-call | flops 536870912 | bytes 4194304 | tf_op jit(solution)/shard_map/attend_back_0/pallas_call | solution.py:131
  64.9 2.1 %collective-permute-start.12 = (bf16[928,128]{1,0:T(8,128)(2,1)S(1)}, bf16[928,128]{1,0:T(8,128)(2,1)S(1)}, u32[]{:S(2)}, u32[]{:S(2)}) collective-permute-start(bf16[928,128]{1,0:T(8,128)(2,1)S(1)} %get-tuple-element.90), channel_id=1, source_target_pairs={{0,4},{2,6},{4,0},{6,2},{1,5},{3,7},{5,1},{7,3},{8,12},{10,14},{12... | collective-permute-start | bytes 712712 | tf_op jit(solution)/shard_map/ppermute | solution.py:819
  67.0 0.0 collective-permute-start.13
  67.0 3.8 %collective-permute-start.14 = (bf16[928,128]{1,0:T(8,128)(2,1)S(1)}, bf16[928,128]{1,0:T(8,128)(2,1)S(1)}, u32[]{:S(2)}, u32[]{:S(2)}) collective-permute-start(bf16[928,128]{1,0:T(8,128)(2,1)S(1)} %get-tuple-element.92), channel_id=1, source_target_pairs={{0,6},{2,0},{4,2},{6,4},{1,7},{3,1},{5,3},{7,5},{8,14},{10,8},{12,... | collective-permute-start | bytes 712712 | tf_op jit(solution)/shard_map/ppermute | solution.py:819
  70.8 1.8 %attend_back_1.1 = (bf16[768,128]{1,0:T(8,128)(2,1)S(1)}, bf16[768,128]{1,0:T(8,128)(2,1)S(1)}, bf16[768,128]{1,0:T(8,128)(2,1)S(1)}, bf16[768,128]{1,0:T(8,128)(2,1)S(1)}) custom-call(bf16[4,768,128]{2,1,0:T(8,128)(2,1)S(1)} %get-tuple-element.96.refs_0_, bf16[2,512,512]{2,1,0:T(8,128)(2,1)S(1)} %get-tuple-element.97.refs_1_, ...), custom_call_target="tpu_custom_call" | custom-call | flops 536870912 | bytes 4194304 | tf_op jit(solution)/shard_map/attend_back_1/pallas_call | solution.py:131
  72.7 0.1 collective-permute-start.18
  72.8 0.6 collective-permute-start.19
  73.3 10.7 %collective-permute-done.12.refs_1_ = bf16[928,128]{1,0:T(8,128)(2,1)S(1)} collective-permute-done((bf16[928,128]{1,0:T(8,128)(2,1)S(1)}, bf16[928,128]{1,0:T(8,128)(2,1)S(1)}, u32[]{:S(2)}, u32[]{:S(2)}) %collective-permute-start.12) | collective-permute-done | bytes 237600 | tf_op jit(solution)/shard_map/ppermute | solution.py:819
  84.0 0.0 collective-permute-start.20
  84.0 0.0 collective-permute-done.13.refs_2_
  84.0 0.6 collective-permute-done.14.refs_3_
  84.7 0.8 unpack.1
  85.4 0.0 collective-permute-start.15
  85.4 1.5 %collective-permute-start.16 = (f32[4,8,128]{2,1,0:T(8,128)S(1)}, f32[4,8,128]{2,1,0:T(8,128)S(1)}, u32[]{:S(2)}, u32[]{:S(2)}) collective-permute-start(f32[4,8,128]{2,1,0:T(8,128)S(1)} %get-tuple-element.94), channel_id=1, source_target_pairs={{0,8},{8,0},{16,24},{24,16},{1,9},{9,1},{17,25},{25,17},{2,10},{10... | collective-permute-start | bytes 49160 | tf_op jit(solution)/shard_map/ppermute | solution.py:827
  86.9 2.2 %collective-permute-done.16 = f32[4,8,128]{2,1,0:T(8,128)S(1)} collective-permute-done((f32[4,8,128]{2,1,0:T(8,128)S(1)}, f32[4,8,128]{2,1,0:T(8,128)S(1)}, u32[]{:S(2)}, u32[]{:S(2)}) %collective-permute-start.16) | collective-permute-done | bytes 16416 | tf_op jit(solution)/shard_map/ppermute | solution.py:827
  89.2 1.5 %collective-permute-start.17 = (f32[4,8,128]{2,1,0:T(8,128)S(1)}, f32[4,8,128]{2,1,0:T(8,128)S(1)}, u32[]{:S(2)}, u32[]{:S(2)}) collective-permute-start(f32[4,8,128]{2,1,0:T(8,128)S(1)} %add.10), channel_id=1, source_target_pairs={{0,16},{8,24},{16,0},{24,8},{1,17},{9,25},{17,1},{25,9},{2,18},{10... | collective-permute-start | bytes 49160 | tf_op jit(solution)/shard_map/ppermute | solution.py:827
  90.7 10.3 %collective-permute-done.18.refs_5_ = bf16[768,128]{1,0:T(8,128)(2,1)S(1)} collective-permute-done((bf16[768,128]{1,0:T(8,128)(2,1)S(1)}, bf16[768,128]{1,0:T(8,128)(2,1)S(1)}, u32[]{:S(2)}, u32[]{:S(2)}) %collective-permute-start.18) | collective-permute-done | bytes 196640 | tf_op jit(solution)/shard_map/ppermute | solution.py:819
  101.0 1.5 %finish.1 = bf16[3,1,128,16,128]{4,3,2,1,0:T(8,128)(2,1)} custom-call(bf16[928,128]{1,0:T(8,128)(2,1)S(1)} %get-tuple-element.89.refs_0_.refs_3_, bf16[928,128]{1,0:T(8,128)(2,1)S(1)} %collective-permute-done.12.refs_1_, bf16[928,128]{1,0:T(8,128)(2,1)S(1)} %collective-permute-done.13.refs_2_, bf16[928,128]{1,0:T(8,128)(2,1)S(1)} %collective-permute-done.14.refs_3_, ...), custom_call_target="tpu_custom_call" | custom-call | bytes 3145728 | tf_op jit(solution)/shard_map/finish/pallas_call | solution.py:131
  102.5 1.2 %choose.1 = (f32[1,128,128]{2,1,0:T(8,128)}, f32[1,128,128]{2,1,0:T(8,128)}, f32[4,4,128]{2,1,0:T(4,128)}, f32[1,32]{1,0:T(1,128)}, f32[1,1]{1,0:T(1,128)}) custom-call(s32[4]{0:T(128)S(1)} %copy-done.1, f32[128,128]{1,0:T(8,128)S(1)} %get-tuple-element.93.mine, f32[128,128]{1,0:T(8,128)S(1)} %collective-permute-done.15.theirs, f32[4,8,128]{2,1,0:T(8,128)S(1)} %add.11.vecs), custom_call_target="tpu_custom_call" | custom-call | tf_op jit(solution)/shard_map/choose/pallas_call | solution.py:131
  (16 shorter events, 0.1 us)
Async XLA Ops:
  0.6 26.1 %copy-start = (bf16[2048]{0:T(1024)(128)(2,1)S(1)}, bf16[2048]{0:T(1024)(128)(2,1)}, u32[]{:S(2)}) copy-start(bf16[2048]{0:T(1024)(128)(2,1)} %param.14) | copy-start | bytes 12292
  0.6 26.1 %copy-start.2 = (f32[32]{0:T(128)S(1)}, f32[32]{0:T(128)}, u32[]{:S(2)}) copy-start(f32[32]{0:T(128)} %param.13) | copy-start | bytes 388
  2.7 11.9 %collective-permute-start = (bf16[928,128]{1,0:T(8,128)(2,1)S(1)}, bf16[928,128]{1,0:T(8,128)(2,1)S(1)}, u32[]{:S(2)}, u32[]{:S(2)}) collective-permute-start(bf16[928,128]{1,0:T(8,128)(2,1)S(1)} %get-tuple-element.58), channel_id=1, source_target_pairs={{0,2},{2,4},{4,6},{6,0},{1,3},{3,5},{5,7},{7,1},{8,10},{10,12},{12... | collective-permute-start | bytes 712712 | tf_op jit(solution)/shard_map/ppermute | solution.py:819
  5.7 19.0 %collective-permute-start.1 = (bf16[928,128]{1,0:T(8,128)(2,1)S(1)}, bf16[928,128]{1,0:T(8,128)(2,1)S(1)}, u32[]{:S(2)}, u32[]{:S(2)}) collective-permute-start(bf16[928,128]{1,0:T(8,128)(2,1)S(1)} %get-tuple-element.59), channel_id=1, source_target_pairs={{0,4},{2,6},{4,0},{6,2},{1,5},{3,7},{5,1},{7,3},{8,12},{10,14},{12... | collective-permute-start | bytes 712712 | tf_op jit(solution)/shard_map/ppermute | solution.py:819
  8.3 16.4 %collective-permute-start.2 = (bf16[928,128]{1,0:T(8,128)(2,1)S(1)}, bf16[928,128]{1,0:T(8,128)(2,1)S(1)}, u32[]{:S(2)}, u32[]{:S(2)}) collective-permute-start(bf16[928,128]{1,0:T(8,128)(2,1)S(1)} %get-tuple-element.60), channel_id=1, source_target_pairs={{0,6},{2,0},{4,2},{6,4},{1,7},{3,1},{5,3},{7,5},{8,14},{10,8},{12,... | collective-permute-start | bytes 712712 | tf_op jit(solution)/shard_map/ppermute | solution.py:819
  9.7 19.3 %collective-permute-start.3 = (bf16[768,128]{1,0:T(8,128)(2,1)S(1)}, bf16[768,128]{1,0:T(8,128)(2,1)S(1)}, u32[]{:S(2)}, u32[]{:S(2)}) collective-permute-start(bf16[768,128]{1,0:T(8,128)(2,1)S(1)} %get-tuple-element.64), channel_id=1, source_target_pairs={{0,2},{2,4},{4,6},{6,0},{1,3},{3,5},{5,7},{7,1},{8,10},{10,12},{12... | collective-permute-start | bytes 589832 | tf_op jit(solution)/shard_map/ppermute | solution.py:819
  10.4 31.3 %collective-permute-start.4 = (bf16[768,128]{1,0:T(8,128)(2,1)S(1)}, bf16[768,128]{1,0:T(8,128)(2,1)S(1)}, u32[]{:S(2)}, u32[]{:S(2)}) collective-permute-start(bf16[768,128]{1,0:T(8,128)(2,1)S(1)} %get-tuple-element.65), channel_id=1, source_target_pairs={{0,4},{2,6},{4,0},{6,2},{1,5},{3,7},{5,1},{7,3},{8,12},{10,14},{12... | collective-permute-start | bytes 589832 | tf_op jit(solution)/shard_map/ppermute | solution.py:819
  14.5 27.1 %collective-permute-start.5 = (bf16[768,128]{1,0:T(8,128)(2,1)S(1)}, bf16[768,128]{1,0:T(8,128)(2,1)S(1)}, u32[]{:S(2)}, u32[]{:S(2)}) collective-permute-start(bf16[768,128]{1,0:T(8,128)(2,1)S(1)} %get-tuple-element.66), channel_id=1, source_target_pairs={{0,6},{2,0},{4,2},{6,4},{1,7},{3,1},{5,3},{7,5},{8,14},{10,8},{12,... | collective-permute-start | bytes 589832 | tf_op jit(solution)/shard_map/ppermute | solution.py:819
  24.8 1.9 %collective-permute-start.6 = (bf16[4,128,128]{2,1,0:T(8,128)(2,1)S(1)}, bf16[4,128,128]{2,1,0:T(8,128)(2,1)S(1)}, u32[]{:S(2)}, u32[]{:S(2)}) collective-permute-start(bf16[4,128,128]{2,1,0:T(8,128)(2,1)S(1)} %get-tuple-element.68.mine), channel_id=1, source_target_pairs={{0,1},{1,0},{2,3},{3,2},{4,5},{5,4},{6,7},{7,6},{8,9},{9,8},{10,11... | collective-permute-start | bytes 393224 | tf_op jit(solution)/shard_map/ppermute | solution.py:819
  46.0 1.2 %collective-permute-start.7 = (f32[1,512]{1,0:T(1,128)S(1)}, f32[1,512]{1,0:T(1,128)S(1)}, u32[]{:S(2)}, u32[]{:S(2)}) collective-permute-start(f32[1,512]{1,0:T(1,128)S(1)} %get-tuple-element.72), channel_id=1, source_target_pairs={{0,1},{1,0},{2,3},{3,2},{4,5},{5,4},{6,7},{7,6},{8,9},{9,8},{10,11... | collective-permute-start | bytes 6152 | tf_op jit(solution)/shard_map/ppermute | solution.py:819
  47.2 10.2 %copy-start.1 = (s32[4]{0:T(128)S(1)}, s32[4]{0:T(128)}, u32[]{:S(2)}) copy-start(s32[4]{0:T(128)} %lengths.1) | copy-start | bytes 52
  47.3 7.5 %collective-permute-start.10 = (f32[1,512]{1,0:T(1,128)S(1)}, f32[1,512]{1,0:T(1,128)S(1)}, u32[]{:S(2)}, u32[]{:S(2)}) collective-permute-start(f32[1,512]{1,0:T(1,128)S(1)} %add.9.refs_1_), channel_id=1, source_target_pairs={{0,6},{2,4},{4,2},{6,0},{1,7},{3,5},{5,3},{7,1},{8,14},{10,12},{12... | collective-permute-start | bytes 6152 | tf_op jit(solution)/shard_map/ppermute | solution.py:827
  53.0 4.5 %collective-permute-start.9 = (f32[1,512]{1,0:T(1,128)S(1)}, f32[1,512]{1,0:T(1,128)S(1)}, u32[]{:S(2)}, u32[]{:S(2)}) collective-permute-start(f32[1,512]{1,0:T(1,128)S(1)} %add.9.refs_1_), channel_id=1, source_target_pairs={{0,4},{2,6},{4,0},{6,2},{1,5},{3,7},{5,1},{7,3},{8,12},{10,14},{12... | collective-permute-start | bytes 6152 | tf_op jit(solution)/shard_map/ppermute | solution.py:827
  53.5 4.0 %collective-permute-start.8 = (f32[1,512]{1,0:T(1,128)S(1)}, f32[1,512]{1,0:T(1,128)S(1)}, u32[]{:S(2)}, u32[]{:S(2)}) collective-permute-start(f32[1,512]{1,0:T(1,128)S(1)} %add.9.refs_1_), channel_id=1, source_target_pairs={{0,2},{2,0},{4,6},{6,4},{1,3},{3,1},{5,7},{7,5},{8,10},{10,8},{12,... | collective-permute-start | bytes 6152 | tf_op jit(solution)/shard_map/ppermute | solution.py:827
  61.5 1.4 %collective-permute-start.11 = (bf16[4,128,128]{2,1,0:T(8,128)(2,1)S(1)}, bf16[4,128,128]{2,1,0:T(8,128)(2,1)S(1)}, u32[]{:S(2)}, u32[]{:S(2)}) collective-permute-start(bf16[4,128,128]{2,1,0:T(8,128)(2,1)S(1)} %get-tuple-element.86), channel_id=1, source_target_pairs={{0,1},{1,0},{2,3},{3,2},{4,5},{5,4},{6,7},{7,6},{8,9},{9,8},{10,11... | collective-permute-start | bytes 393224 | tf_op jit(solution)/shard_map/ppermute | solution.py:819
  64.9 19.1 %collective-permute-start.12 = (bf16[928,128]{1,0:T(8,128)(2,1)S(1)}, bf16[928,128]{1,0:T(8,128)(2,1)S(1)}, u32[]{:S(2)}, u32[]{:S(2)}) collective-permute-start(bf16[928,128]{1,0:T(8,128)(2,1)S(1)} %get-tuple-element.90), channel_id=1, source_target_pairs={{0,4},{2,6},{4,0},{6,2},{1,5},{3,7},{5,1},{7,3},{8,12},{10,14},{12... | collective-permute-start | bytes 712712 | tf_op jit(solution)/shard_map/ppermute | solution.py:819
  67.0 17.0 %collective-permute-start.13 = (bf16[928,128]{1,0:T(8,128)(2,1)S(1)}, bf16[928,128]{1,0:T(8,128)(2,1)S(1)}, u32[]{:S(2)}, u32[]{:S(2)}) collective-permute-start(bf16[928,128]{1,0:T(8,128)(2,1)S(1)} %get-tuple-element.91), channel_id=1, source_target_pairs={{0,2},{2,4},{4,6},{6,0},{1,3},{3,5},{5,7},{7,1},{8,10},{10,12},{12... | collective-permute-start | bytes 712712 | tf_op jit(solution)/shard_map/ppermute | solution.py:819
  67.0 17.6 %collective-permute-start.14 = (bf16[928,128]{1,0:T(8,128)(2,1)S(1)}, bf16[928,128]{1,0:T(8,128)(2,1)S(1)}, u32[]{:S(2)}, u32[]{:S(2)}) collective-permute-start(bf16[928,128]{1,0:T(8,128)(2,1)S(1)} %get-tuple-element.92), channel_id=1, source_target_pairs={{0,6},{2,0},{4,2},{6,4},{1,7},{3,1},{5,3},{7,5},{8,14},{10,8},{12,... | collective-permute-start | bytes 712712 | tf_op jit(solution)/shard_map/ppermute | solution.py:819
  72.7 28.3 %collective-permute-start.18 = (bf16[768,128]{1,0:T(8,128)(2,1)S(1)}, bf16[768,128]{1,0:T(8,128)(2,1)S(1)}, u32[]{:S(2)}, u32[]{:S(2)}) collective-permute-start(bf16[768,128]{1,0:T(8,128)(2,1)S(1)} %get-tuple-element.99), channel_id=1, source_target_pairs={{0,4},{2,6},{4,0},{6,2},{1,5},{3,7},{5,1},{7,3},{8,12},{10,14},{12... | collective-permute-start | bytes 589832 | tf_op jit(solution)/shard_map/ppermute | solution.py:819
  72.8 28.2 %collective-permute-start.19 = (bf16[768,128]{1,0:T(8,128)(2,1)S(1)}, bf16[768,128]{1,0:T(8,128)(2,1)S(1)}, u32[]{:S(2)}, u32[]{:S(2)}) collective-permute-start(bf16[768,128]{1,0:T(8,128)(2,1)S(1)} %get-tuple-element.100), channel_id=1, source_target_pairs={{0,2},{2,4},{4,6},{6,0},{1,3},{3,5},{5,7},{7,1},{8,10},{10,12},{12... | collective-permute-start | bytes 589832 | tf_op jit(solution)/shard_map/ppermute | solution.py:819
  84.0 16.9 %collective-permute-start.20 = (bf16[768,128]{1,0:T(8,128)(2,1)S(1)}, bf16[768,128]{1,0:T(8,128)(2,1)S(1)}, u32[]{:S(2)}, u32[]{:S(2)}) collective-permute-start(bf16[768,128]{1,0:T(8,128)(2,1)S(1)} %get-tuple-element.101), channel_id=1, source_target_pairs={{0,6},{2,0},{4,2},{6,4},{1,7},{3,1},{5,3},{7,5},{8,14},{10,8},{12,... | collective-permute-start | bytes 589832 | tf_op jit(solution)/shard_map/ppermute | solution.py:819
  85.4 17.1 %collective-permute-start.15 = (f32[128,128]{1,0:T(8,128)S(1)}, f32[128,128]{1,0:T(8,128)S(1)}, u32[]{:S(2)}, u32[]{:S(2)}) collective-permute-start(f32[128,128]{1,0:T(8,128)S(1)} %get-tuple-element.93.mine), channel_id=1, source_target_pairs={{0,1},{1,0},{2,3},{3,2},{4,5},{5,4},{6,7},{7,6},{8,9},{9,8},{10,11... | collective-permute-start | bytes 196616 | tf_op jit(solution)/shard_map/ppermute | solution.py:819
  85.4 3.7 %collective-permute-start.16 = (f32[4,8,128]{2,1,0:T(8,128)S(1)}, f32[4,8,128]{2,1,0:T(8,128)S(1)}, u32[]{:S(2)}, u32[]{:S(2)}) collective-permute-start(f32[4,8,128]{2,1,0:T(8,128)S(1)} %get-tuple-element.94), channel_id=1, source_target_pairs={{0,8},{8,0},{16,24},{24,16},{1,9},{9,1},{17,25},{25,17},{2,10},{10... | collective-permute-start | bytes 49160 | tf_op jit(solution)/shard_map/ppermute | solution.py:827
  89.2 13.3 %collective-permute-start.17 = (f32[4,8,128]{2,1,0:T(8,128)S(1)}, f32[4,8,128]{2,1,0:T(8,128)S(1)}, u32[]{:S(2)}, u32[]{:S(2)}) collective-permute-start(f32[4,8,128]{2,1,0:T(8,128)S(1)} %add.10), channel_id=1, source_target_pairs={{0,16},{8,24},{16,0},{24,8},{1,17},{9,25},{17,1},{25,9},{2,18},{10... | collective-permute-start | bytes 49160 | tf_op jit(solution)/shard_map/ppermute | solution.py:827

commit v6 on v5

--- a/solution.py
+++ b/solution.py
@@ -740,7 +740,9 @@
     )
 
 
-def choose_kernel(z, lengths, mine, theirs, vecs, b, c, weight, rate, loss):
+def choose_kernel(z, lengths, mine, theirs, *refs):
+    vecs, (b, c, weight, rate, loss) = refs[:-5], refs[-5:]
+    vecs = sum([one[...] for one in vecs[1:]], vecs[0][...])
     core = lax.axis_index("head")
     b[0] = jnp.where(core == 0, mine[...], theirs[...])
     c[0] = jnp.where(core == 0, theirs[...], mine[...])
@@ -768,10 +770,10 @@
             SHAPE((1, z.n * z.h), F32),
             SHAPE((1, 1), F32),
         ),
-        [SM] + [VM] * 3,
+        [SM] + [VM] * (2 + len(vecs)),
         [VM] * 5,
         [],
-        (lengths, mine, theirs, vecs),
+        (lengths, mine, theirs, *vecs),
     )
 
 
@@ -854,8 +856,10 @@
     proj, step_grad, vecs = unpack(z, finals[0])
     other = shift(proj, "head", 2, 1)
     step = 1
+    vecs = [vecs]
     while step < lax.axis_size("rollout"):
-        vecs = vecs + partners(vecs, "rollout", step)
+        total = sum(vecs[1:], vecs[0])
+        vecs = [total, partners(total, "rollout", step)]
         step *= 2
     b_grad, c_grad, weight_grad, rate_grad, loss = choose(z, lengths, proj, other, vecs)
     qkv_grad = finish(z, [x for part in finals for x in part])

time: 106 us -> 106 us (level)
  no operation moved by 1% of the time
where the time goes in v6:
time: 106 us; the launch traced here: 104 us
  waiting for transfers between devices  52.4 us (49%)
  starting transfers between devices  26.7 us (25%)
  Pallas kernels  23.8 us (22%)
    ppermute x16, waiting for transfers between devices, shift(): return lax.ppermute(x, axis, [(i, (i + step) % size) for i in range(size)])  47.4 us
    pallas_call x13, Pallas kernels, call(): pl.pallas_call(functools.partial(kernel, z), name=name, out_shape=out_sha...  23.8 us
    ppermute x16, starting transfers between devices, shift(): return lax.ppermute(x, axis, [(i, (i + step) % size) for i in range(size)])  17.3 us
    ppermute x5, starting transfers between devices, partners(): lax.ppermute(x, axis, [(i, i ^ step) for i in range(lax.axis_size(axis))])  9.37 us
    ppermute x5, waiting for transfers between devices, partners(): lax.ppermute(x, axis, [(i, i ^ step) for i in range(lax.axis_size(axis))])  4.99 us
  transfers between devices with their start and end apart: 21, of which 10 were waited for; matrix products, arithmetic and copies ran while one was open for 0% of the time, Pallas kernels for 10%

profile of v6, /device:TPU:0, one launch (start us, length us, event | category | flops | bytes accessed | tf_op | source)
XLA Modules:
  0.0 103.7 jit_solution(4469236971912105420)
XLA Ops:
  0.7 2.0 %prep.1 = (bf16[928,128]{1,0:T(8,128)(2,1)S(1)}, bf16[928,128]{1,0:T(8,128)(2,1)S(1)}, bf16[928,128]{1,0:T(8,128)(2,1)S(1)}, bf16[928,128]{1,0:T(8,128)(2,1)S(1)...) custom-call(bf16[3,1,128,16,128]{4,3,2,1,0:T(8,128)(2,1)} %qkv.1, ...), custom_call_target="tpu_custom_call" | custom-call | bytes 3145728 | tf_op jit(solution)/shard_map/prep/pallas_call | solution.py:131
  2.7 3.1 %collective-permute-start = (bf16[928,128]{1,0:T(8,128)(2,1)S(1)}, bf16[928,128]{1,0:T(8,128)(2,1)S(1)}, u32[]{:S(2)}, u32[]{:S(2)}) collective-permute-start(bf16[928,128]{1,0:T(8,128)(2,1)S(1)} %get-tuple-element.58), channel_id=1, source_target_pairs={{0,2},{2,4},{4,6},{6,0},{1,3},{3,5},{5,7},{7,1},{8,10},{10,12},{12... | collective-permute-start | bytes 712712 | tf_op jit(solution)/shard_map/ppermute | solution.py:821
  5.7 2.6 %collective-permute-start.1 = (bf16[928,128]{1,0:T(8,128)(2,1)S(1)}, bf16[928,128]{1,0:T(8,128)(2,1)S(1)}, u32[]{:S(2)}, u32[]{:S(2)}) collective-permute-start(bf16[928,128]{1,0:T(8,128)(2,1)S(1)} %get-tuple-element.59), channel_id=1, source_target_pairs={{0,4},{2,6},{4,0},{6,2},{1,5},{3,7},{5,1},{7,3},{8,12},{10,14},{12... | collective-permute-start | bytes 712712 | tf_op jit(solution)/shard_map/ppermute | solution.py:821
  8.3 1.3 %collective-permute-start.2 = (bf16[928,128]{1,0:T(8,128)(2,1)S(1)}, bf16[928,128]{1,0:T(8,128)(2,1)S(1)}, u32[]{:S(2)}, u32[]{:S(2)}) collective-permute-start(bf16[928,128]{1,0:T(8,128)(2,1)S(1)} %get-tuple-element.60), channel_id=1, source_target_pairs={{0,6},{2,0},{4,2},{6,4},{1,7},{3,1},{5,3},{7,5},{8,14},{10,8},{12,... | collective-permute-start | bytes 712712 | tf_op jit(solution)/shard_map/ppermute | solution.py:821
  9.7 0.7 collective-permute-start.3
  10.4 0.3 collective-permute-start.4
  10.7 3.8 %collective-permute-done.refs_1_ = bf16[928,128]{1,0:T(8,128)(2,1)S(1)} collective-permute-done((bf16[928,128]{1,0:T(8,128)(2,1)S(1)}, bf16[928,128]{1,0:T(8,128)(2,1)S(1)}, u32[]{:S(2)}, u32[]{:S(2)}) %collective-permute-start) | collective-permute-done | bytes 237600 | tf_op jit(solution)/shard_map/ppermute | solution.py:821
  14.5 2.5 %collective-permute-start.5 = (bf16[768,128]{1,0:T(8,128)(2,1)S(1)}, bf16[768,128]{1,0:T(8,128)(2,1)S(1)}, u32[]{:S(2)}, u32[]{:S(2)}) collective-permute-start(bf16[768,128]{1,0:T(8,128)(2,1)S(1)} %get-tuple-element.66), channel_id=1, source_target_pairs={{0,6},{2,0},{4,2},{6,4},{1,7},{3,1},{5,3},{7,5},{8,14},{10,8},{12,... | collective-permute-start | bytes 589832 | tf_op jit(solution)/shard_map/ppermute | solution.py:821
  17.0 7.7 %collective-permute-done.1.refs_2_ = bf16[928,128]{1,0:T(8,128)(2,1)S(1)} collective-permute-done((bf16[928,128]{1,0:T(8,128)(2,1)S(1)}, bf16[928,128]{1,0:T(8,128)(2,1)S(1)}, u32[]{:S(2)}, u32[]{:S(2)}) %collective-permute-start.1) | collective-permute-done | bytes 237600 | tf_op jit(solution)/shard_map/ppermute | solution.py:821
  24.8 0.1 collective-permute-start.6
  24.9 1.8 %attend_0.1 = (bf16[2,512,512]{2,1,0:T(8,128)(2,1)S(1)}, bf16[512,256]{1,0:T(8,128)(2,1)S(1)}, bf16[4,768,128]{2,1,0:T(8,128)(2,1)S(1)}) custom-call(bf16[928,128]{1,0:T(8,128)(2,1)S(1)} %get-tuple-element.57.refs_0_, bf16[928,128]{1,0:T(8,128)(2,1)S(1)} %collective-permute-done.refs_1_, bf16[928,128]{1,0:T(8,128)(2,1)S(1)} %collective-permute-done.1.refs_2_, ...), custom_call_target="tpu_custom_call" | custom-call | flops 268435456 | bytes 4194304 | tf_op jit(solution)/shard_map/attend_0/pallas_call | solution.py:131
  26.7 2.0 %decay.1 = (f32[1144,512]{1,0:T(8,128)S(1)}, bf16[4,4,128,128]{3,2,1,0:T(8,128)(2,1)S(1)}) custom-call(bf16[4,128,128]{2,1,0:T(8,128)(2,1)S(1)} %get-tuple-element.68.mine, bf16[4,128,128]{2,1,0:T(8,128)(2,1)S(1)} %collective-permute-done.6.theirs, f32[4,16,128]{2,1,0:T(8,128)S(1)} %get-tuple-element.69.pay, f32[1,32]{1,0:T(1,128)S(1)} %bitcast.8, ...), custom_call_target="tpu_custom_call" | custom-call | bytes 2097152 | tf_op jit(solution)/shard_map/decay/pallas_call | solution.py:131
  28.7 0.2 collective-permute-done.3.refs_1_
  29.0 12.7 %collective-permute-done.4.refs_2_ = bf16[768,128]{1,0:T(8,128)(2,1)S(1)} collective-permute-done((bf16[768,128]{1,0:T(8,128)(2,1)S(1)}, bf16[768,128]{1,0:T(8,128)(2,1)S(1)}, u32[]{:S(2)}, u32[]{:S(2)}) %collective-permute-start.4) | collective-permute-done | bytes 196640 | tf_op jit(solution)/shard_map/ppermute | solution.py:821
  41.6 0.0 collective-permute-done.5.refs_3_
  41.6 4.4 %attend_and_ssd.1 = (bf16[2,512,512]{2,1,0:T(8,128)(2,1)S(1)}, bf16[512,256]{1,0:T(8,128)(2,1)}, bf16[4,768,128]{2,1,0:T(8,128)(2,1)S(1)}, bf16[6,512,512]{2,1,0:T(8,128)(2,1)S(1)}, f32[1,512]{1,0:T(1,128)S(1)}) custom-call(bf16[768,128]{1,0:T(8,128)(2,1)S(1)} %get-tuple-element.63.refs_0_, bf16[768,128]{1,0:T(8,128)(2,1)S(1)} %collective-permute-done.3.refs_1_, ...), custom_call_target="tpu_custom_call" | custom-call | flops 671088640 | bytes 8388608 | tf_op jit(solution)/shard_map/attend_and_ssd/pallas_call | solution.py:131
  46.0 0.1 collective-permute-start.7
  46.1 1.1 %ssd_pre_0.1 = (f32[256,128]{1,0:T(8,128)S(1)}, bf16[256,1024]{1,0:T(8,128)(2,1)S(1)}, f32[256,128]{1,0:T(8,128)S(1)}) custom-call(bf16[4,4,128,128]{3,2,1,0:T(8,128)(2,1)S(1)} %get-tuple-element.71.refs_6_.refs_0_, bf16[6,512,512]{2,1,0:T(8,128)(2,1)S(1)} %get-tuple-element.73.refs_1_.refs_7_), custom_call_target="tpu_custom_call" | custom-call | flops 335544320 | bytes 1048576 | tf_op jit(solution)/shard_map/ssd_pre_0/pallas_call | solution.py:131
  47.2 0.0 copy-start.1
  47.2 0.0 collective-permute-done.7
  47.3 5.7 %collective-permute-start.10 = (f32[1,512]{1,0:T(1,128)S(1)}, f32[1,512]{1,0:T(1,128)S(1)}, u32[]{:S(2)}, u32[]{:S(2)}) collective-permute-start(f32[1,512]{1,0:T(1,128)S(1)} %add.6.refs_1_), channel_id=1, source_target_pairs={{0,6},{2,4},{4,2},{6,0},{1,7},{3,5},{5,3},{7,1},{8,14},{10,12},{12... | collective-permute-start | bytes 6152 | tf_op jit(solution)/shard_map/ppermute | solution.py:829
  53.0 0.5 collective-permute-start.9
  53.5 0.2 collective-permute-start.8
  53.6 1.1 %ssd_pre_1.1 = (f32[256,128]{1,0:T(8,128)S(1)}, bf16[256,1024]{1,0:T(8,128)(2,1)S(1)}, f32[256,128]{1,0:T(8,128)S(1)}) custom-call(bf16[4,4,128,128]{3,2,1,0:T(8,128)(2,1)S(1)} %get-tuple-element.71.refs_6_.refs_0_, bf16[6,512,512]{2,1,0:T(8,128)(2,1)S(1)} %get-tuple-element.73.refs_1_.refs_7_), custom_call_target="tpu_custom_call" | custom-call | flops 335544320 | bytes 1048576 | tf_op jit(solution)/shard_map/ssd_pre_1/pallas_call | solution.py:131
  54.7 0.0 collective-permute-done.10.refs_4_
  54.7 2.7 %collective-permute-done.9.refs_3_ = f32[1,512]{1,0:T(1,128)S(1)} collective-permute-done((f32[1,512]{1,0:T(1,128)S(1)}, f32[1,512]{1,0:T(1,128)S(1)}, u32[]{:S(2)}, u32[]{:S(2)}) %collective-permute-start.9) | collective-permute-done | bytes 2080 | tf_op jit(solution)/shard_map/ppermute | solution.py:829
  57.5 4.0 %ssd_back.1 = (bf16[512,512]{1,0:T(8,128)(2,1)S(1)}, f32[4,128,128]{2,1,0:T(8,128)S(1)}, bf16[4,128,128]{2,1,0:T(8,128)(2,1)S(1)}, f32[4,16,128]{2,1,0:T(8,128)S(1)}, f32[8,128]{1,0:T(8,128)S(1)}) custom-call(s32[4]{0:T(128)S(1)} %copy-done.1, f32[1,512]{1,0:T(1,128)S(1)} %add.6.refs_1_, f32[1,512]{1,0:T(1,128)S(1)} %collective-permute-done.8.refs_2_, ...), custom_call_target="tpu_custom_call" | custom-call | flops 671088640 | bytes 8388608 | tf_op jit(solution)/shard_map/ssd_back/pallas_call | solution.py:131
  61.5 0.1 collective-permute-start.11
  61.6 1.3 %collective-permute-done.11.refs_4_ = bf16[4,128,128]{2,1,0:T(8,128)(2,1)S(1)} collective-permute-done((bf16[4,128,128]{2,1,0:T(8,128)(2,1)S(1)}, bf16[4,128,128]{2,1,0:T(8,128)(2,1)S(1)}, u32[]{:S(2)}, u32[]{:S(2)}) %collective-permute-start.11) | collective-permute-done | bytes 131104 | tf_op jit(solution)/shard_map/ppermute | solution.py:821
  62.9 2.0 %attend_back_0.1 = (bf16[928,128]{1,0:T(8,128)(2,1)S(1)}, bf16[928,128]{1,0:T(8,128)(2,1)S(1)}, bf16[928,128]{1,0:T(8,128)(2,1)S(1)}, bf16[928,128]{1,0:T(8,128)(2,1)S(1)}) custom-call(bf16[4,768,128]{2,1,0:T(8,128)(2,1)S(1)} %get-tuple-element.61.refs_0_, bf16[2,512,512]{2,1,0:T(8,128)(2,1)S(1)} %get-tuple-element.62.refs_1_, ...), custom_call_target="tpu_custom_call" | custom-call | flops 536870912 | bytes 4194304 | tf_op jit(solution)/shard_map/attend_back_0/pallas_call | solution.py:131
  64.9 2.1 %collective-permute-start.12 = (bf16[928,128]{1,0:T(8,128)(2,1)S(1)}, bf16[928,128]{1,0:T(8,128)(2,1)S(1)}, u32[]{:S(2)}, u32[]{:S(2)}) collective-permute-start(bf16[928,128]{1,0:T(8,128)(2,1)S(1)} %get-tuple-element.90), channel_id=1, source_target_pairs={{0,4},{2,6},{4,0},{6,2},{1,5},{3,7},{5,1},{7,3},{8,12},{10,14},{12... | collective-permute-start | bytes 712712 | tf_op jit(solution)/shard_map/ppermute | solution.py:821
  67.0 0.0 collective-permute-start.13
  67.0 3.8 %collective-permute-start.14 = (bf16[928,128]{1,0:T(8,128)(2,1)S(1)}, bf16[928,128]{1,0:T(8,128)(2,1)S(1)}, u32[]{:S(2)}, u32[]{:S(2)}) collective-permute-start(bf16[928,128]{1,0:T(8,128)(2,1)S(1)} %get-tuple-element.92), channel_id=1, source_target_pairs={{0,6},{2,0},{4,2},{6,4},{1,7},{3,1},{5,3},{7,5},{8,14},{10,8},{12,... | collective-permute-start | bytes 712712 | tf_op jit(solution)/shard_map/ppermute | solution.py:821
  70.8 1.8 %attend_back_1.1 = (bf16[768,128]{1,0:T(8,128)(2,1)S(1)}, bf16[768,128]{1,0:T(8,128)(2,1)S(1)}, bf16[768,128]{1,0:T(8,128)(2,1)S(1)}, bf16[768,128]{1,0:T(8,128)(2,1)S(1)}) custom-call(bf16[4,768,128]{2,1,0:T(8,128)(2,1)S(1)} %get-tuple-element.96.refs_0_, bf16[2,512,512]{2,1,0:T(8,128)(2,1)S(1)} %get-tuple-element.97.refs_1_, ...), custom_call_target="tpu_custom_call" | custom-call | flops 536870912 | bytes 4194304 | tf_op jit(solution)/shard_map/attend_back_1/pallas_call | solution.py:131
  72.7 0.1 collective-permute-start.18
  72.8 0.6 collective-permute-start.19
  73.3 10.7 %collective-permute-done.12.refs_1_ = bf16[928,128]{1,0:T(8,128)(2,1)S(1)} collective-permute-done((bf16[928,128]{1,0:T(8,128)(2,1)S(1)}, bf16[928,128]{1,0:T(8,128)(2,1)S(1)}, u32[]{:S(2)}, u32[]{:S(2)}) %collective-permute-start.12) | collective-permute-done | bytes 237600 | tf_op jit(solution)/shard_map/ppermute | solution.py:821
  84.0 0.0 collective-permute-start.20
  84.0 0.0 collective-permute-done.13.refs_2_
  84.0 0.6 collective-permute-done.14.refs_3_
  84.7 0.8 unpack.1
  85.4 0.0 collective-permute-start.15
  85.4 1.5 %collective-permute-start.16 = (f32[4,8,128]{2,1,0:T(8,128)S(1)}, f32[4,8,128]{2,1,0:T(8,128)S(1)}, u32[]{:S(2)}, u32[]{:S(2)}) collective-permute-start(f32[4,8,128]{2,1,0:T(8,128)S(1)} %get-tuple-element.94), channel_id=1, source_target_pairs={{0,8},{8,0},{16,24},{24,16},{1,9},{9,1},{17,25},{25,17},{2,10},{10... | collective-permute-start | bytes 49160 | tf_op jit(solution)/shard_map/ppermute | solution.py:829
  86.9 2.2 %collective-permute-done.16 = f32[4,8,128]{2,1,0:T(8,128)S(1)} collective-permute-done((f32[4,8,128]{2,1,0:T(8,128)S(1)}, f32[4,8,128]{2,1,0:T(8,128)S(1)}, u32[]{:S(2)}, u32[]{:S(2)}) %collective-permute-start.16) | collective-permute-done | bytes 16416 | tf_op jit(solution)/shard_map/ppermute | solution.py:829
  89.2 1.5 %collective-permute-start.17 = (f32[4,8,128]{2,1,0:T(8,128)S(1)}, f32[4,8,128]{2,1,0:T(8,128)S(1)}, u32[]{:S(2)}, u32[]{:S(2)}) collective-permute-start(f32[4,8,128]{2,1,0:T(8,128)S(1)} %add.7.refs_0_), channel_id=1, source_target_pairs={{0,16},{8,24},{16,0},{24,8},{1,17},{9,25},{17,1},{25,9},{2,18},{10... | collective-permute-start | bytes 49160 | tf_op jit(solution)/shard_map/ppermute | solution.py:829
  90.7 10.3 %collective-permute-done.18.refs_5_ = bf16[768,128]{1,0:T(8,128)(2,1)S(1)} collective-permute-done((bf16[768,128]{1,0:T(8,128)(2,1)S(1)}, bf16[768,128]{1,0:T(8,128)(2,1)S(1)}, u32[]{:S(2)}, u32[]{:S(2)}) %collective-permute-start.18) | collective-permute-done | bytes 196640 | tf_op jit(solution)/shard_map/ppermute | solution.py:821
  101.0 1.5 %finish.1 = bf16[3,1,128,16,128]{4,3,2,1,0:T(8,128)(2,1)} custom-call(bf16[928,128]{1,0:T(8,128)(2,1)S(1)} %get-tuple-element.89.refs_0_.refs_3_, bf16[928,128]{1,0:T(8,128)(2,1)S(1)} %collective-permute-done.12.refs_1_, bf16[928,128]{1,0:T(8,128)(2,1)S(1)} %collective-permute-done.13.refs_2_, bf16[928,128]{1,0:T(8,128)(2,1)S(1)} %collective-permute-done.14.refs_3_, ...), custom_call_target="tpu_custom_call" | custom-call | bytes 3145728 | tf_op jit(solution)/shard_map/finish/pallas_call | solution.py:131
  102.5 1.2 %choose.1 = (f32[1,128,128]{2,1,0:T(8,128)}, f32[1,128,128]{2,1,0:T(8,128)}, f32[4,4,128]{2,1,0:T(4,128)}, f32[1,32]{1,0:T(1,128)}, f32[1,1]{1,0:T(1,128)}) custom-call(s32[4]{0:T(128)S(1)} %copy-done.1, f32[128,128]{1,0:T(8,128)S(1)} %get-tuple-element.93.mine, f32[128,128]{1,0:T(8,128)S(1)} %collective-permute-done.15.theirs, ...), custom_call_target="tpu_custom_call" | custom-call | tf_op jit(solution)/shard_map/choose/pallas_call | solution.py:131
  (15 shorter events, 0.1 us)
Async XLA Ops:
  0.6 26.1 %copy-start = (bf16[2048]{0:T(1024)(128)(2,1)S(1)}, bf16[2048]{0:T(1024)(128)(2,1)}, u32[]{:S(2)}) copy-start(bf16[2048]{0:T(1024)(128)(2,1)} %param.14) | copy-start | bytes 12292
  0.6 26.1 %copy-start.2 = (f32[32]{0:T(128)S(1)}, f32[32]{0:T(128)}, u32[]{:S(2)}) copy-start(f32[32]{0:T(128)} %param.13) | copy-start | bytes 388
  2.7 11.9 %collective-permute-start = (bf16[928,128]{1,0:T(8,128)(2,1)S(1)}, bf16[928,128]{1,0:T(8,128)(2,1)S(1)}, u32[]{:S(2)}, u32[]{:S(2)}) collective-permute-start(bf16[928,128]{1,0:T(8,128)(2,1)S(1)} %get-tuple-element.58), channel_id=1, source_target_pairs={{0,2},{2,4},{4,6},{6,0},{1,3},{3,5},{5,7},{7,1},{8,10},{10,12},{12... | collective-permute-start | bytes 712712 | tf_op jit(solution)/shard_map/ppermute | solution.py:821
  5.7 19.0 %collective-permute-start.1 = (bf16[928,128]{1,0:T(8,128)(2,1)S(1)}, bf16[928,128]{1,0:T(8,128)(2,1)S(1)}, u32[]{:S(2)}, u32[]{:S(2)}) collective-permute-start(bf16[928,128]{1,0:T(8,128)(2,1)S(1)} %get-tuple-element.59), channel_id=1, source_target_pairs={{0,4},{2,6},{4,0},{6,2},{1,5},{3,7},{5,1},{7,3},{8,12},{10,14},{12... | collective-permute-start | bytes 712712 | tf_op jit(solution)/shard_map/ppermute | solution.py:821
  8.3 16.4 %collective-permute-start.2 = (bf16[928,128]{1,0:T(8,128)(2,1)S(1)}, bf16[928,128]{1,0:T(8,128)(2,1)S(1)}, u32[]{:S(2)}, u32[]{:S(2)}) collective-permute-start(bf16[928,128]{1,0:T(8,128)(2,1)S(1)} %get-tuple-element.60), channel_id=1, source_target_pairs={{0,6},{2,0},{4,2},{6,4},{1,7},{3,1},{5,3},{7,5},{8,14},{10,8},{12,... | collective-permute-start | bytes 712712 | tf_op jit(solution)/shard_map/ppermute | solution.py:821
  9.7 19.3 %collective-permute-start.3 = (bf16[768,128]{1,0:T(8,128)(2,1)S(1)}, bf16[768,128]{1,0:T(8,128)(2,1)S(1)}, u32[]{:S(2)}, u32[]{:S(2)}) collective-permute-start(bf16[768,128]{1,0:T(8,128)(2,1)S(1)} %get-tuple-element.64), channel_id=1, source_target_pairs={{0,2},{2,4},{4,6},{6,0},{1,3},{3,5},{5,7},{7,1},{8,10},{10,12},{12... | collective-permute-start | bytes 589832 | tf_op jit(solution)/shard_map/ppermute | solution.py:821
  10.4 31.3 %collective-permute-start.4 = (bf16[768,128]{1,0:T(8,128)(2,1)S(1)}, bf16[768,128]{1,0:T(8,128)(2,1)S(1)}, u32[]{:S(2)}, u32[]{:S(2)}) collective-permute-start(bf16[768,128]{1,0:T(8,128)(2,1)S(1)} %get-tuple-element.65), channel_id=1, source_target_pairs={{0,4},{2,6},{4,0},{6,2},{1,5},{3,7},{5,1},{7,3},{8,12},{10,14},{12... | collective-permute-start | bytes 589832 | tf_op jit(solution)/shard_map/ppermute | solution.py:821
  14.5 27.1 %collective-permute-start.5 = (bf16[768,128]{1,0:T(8,128)(2,1)S(1)}, bf16[768,128]{1,0:T(8,128)(2,1)S(1)}, u32[]{:S(2)}, u32[]{:S(2)}) collective-permute-start(bf16[768,128]{1,0:T(8,128)(2,1)S(1)} %get-tuple-element.66), channel_id=1, source_target_pairs={{0,6},{2,0},{4,2},{6,4},{1,7},{3,1},{5,3},{7,5},{8,14},{10,8},{12,... | collective-permute-start | bytes 589832 | tf_op jit(solution)/shard_map/ppermute | solution.py:821
  24.8 1.9 %collective-permute-start.6 = (bf16[4,128,128]{2,1,0:T(8,128)(2,1)S(1)}, bf16[4,128,128]{2,1,0:T(8,128)(2,1)S(1)}, u32[]{:S(2)}, u32[]{:S(2)}) collective-permute-start(bf16[4,128,128]{2,1,0:T(8,128)(2,1)S(1)} %get-tuple-element.68.mine), channel_id=1, source_target_pairs={{0,1},{1,0},{2,3},{3,2},{4,5},{5,4},{6,7},{7,6},{8,9},{9,8},{10,11... | collective-permute-start | bytes 393224 | tf_op jit(solution)/shard_map/ppermute | solution.py:821
  46.0 1.2 %collective-permute-start.7 = (f32[1,512]{1,0:T(1,128)S(1)}, f32[1,512]{1,0:T(1,128)S(1)}, u32[]{:S(2)}, u32[]{:S(2)}) collective-permute-start(f32[1,512]{1,0:T(1,128)S(1)} %get-tuple-element.72), channel_id=1, source_target_pairs={{0,1},{1,0},{2,3},{3,2},{4,5},{5,4},{6,7},{7,6},{8,9},{9,8},{10,11... | collective-permute-start | bytes 6152 | tf_op jit(solution)/shard_map/ppermute | solution.py:821
  47.2 10.2 %copy-start.1 = (s32[4]{0:T(128)S(1)}, s32[4]{0:T(128)}, u32[]{:S(2)}) copy-start(s32[4]{0:T(128)} %lengths.1) | copy-start | bytes 52
  47.3 7.5 %collective-permute-start.10 = (f32[1,512]{1,0:T(1,128)S(1)}, f32[1,512]{1,0:T(1,128)S(1)}, u32[]{:S(2)}, u32[]{:S(2)}) collective-permute-start(f32[1,512]{1,0:T(1,128)S(1)} %add.6.refs_1_), channel_id=1, source_target_pairs={{0,6},{2,4},{4,2},{6,0},{1,7},{3,5},{5,3},{7,1},{8,14},{10,12},{12... | collective-permute-start | bytes 6152 | tf_op jit(solution)/shard_map/ppermute | solution.py:829
  53.0 4.5 %collective-permute-start.9 = (f32[1,512]{1,0:T(1,128)S(1)}, f32[1,512]{1,0:T(1,128)S(1)}, u32[]{:S(2)}, u32[]{:S(2)}) collective-permute-start(f32[1,512]{1,0:T(1,128)S(1)} %add.6.refs_1_), channel_id=1, source_target_pairs={{0,4},{2,6},{4,0},{6,2},{1,5},{3,7},{5,1},{7,3},{8,12},{10,14},{12... | collective-permute-start | bytes 6152 | tf_op jit(solution)/shard_map/ppermute | solution.py:829
  53.5 4.0 %collective-permute-start.8 = (f32[1,512]{1,0:T(1,128)S(1)}, f32[1,512]{1,0:T(1,128)S(1)}, u32[]{:S(2)}, u32[]{:S(2)}) collective-permute-start(f32[1,512]{1,0:T(1,128)S(1)} %add.6.refs_1_), channel_id=1, source_target_pairs={{0,2},{2,0},{4,6},{6,4},{1,3},{3,1},{5,7},{7,5},{8,10},{10,8},{12,... | collective-permute-start | bytes 6152 | tf_op jit(solution)/shard_map/ppermute | solution.py:829
  61.5 1.4 %collective-permute-start.11 = (bf16[4,128,128]{2,1,0:T(8,128)(2,1)S(1)}, bf16[4,128,128]{2,1,0:T(8,128)(2,1)S(1)}, u32[]{:S(2)}, u32[]{:S(2)}) collective-permute-start(bf16[4,128,128]{2,1,0:T(8,128)(2,1)S(1)} %get-tuple-element.86), channel_id=1, source_target_pairs={{0,1},{1,0},{2,3},{3,2},{4,5},{5,4},{6,7},{7,6},{8,9},{9,8},{10,11... | collective-permute-start | bytes 393224 | tf_op jit(solution)/shard_map/ppermute | solution.py:821
  64.9 19.1 %collective-permute-start.12 = (bf16[928,128]{1,0:T(8,128)(2,1)S(1)}, bf16[928,128]{1,0:T(8,128)(2,1)S(1)}, u32[]{:S(2)}, u32[]{:S(2)}) collective-permute-start(bf16[928,128]{1,0:T(8,128)(2,1)S(1)} %get-tuple-element.90), channel_id=1, source_target_pairs={{0,4},{2,6},{4,0},{6,2},{1,5},{3,7},{5,1},{7,3},{8,12},{10,14},{12... | collective-permute-start | bytes 712712 | tf_op jit(solution)/shard_map/ppermute | solution.py:821
  67.0 17.0 %collective-permute-start.13 = (bf16[928,128]{1,0:T(8,128)(2,1)S(1)}, bf16[928,128]{1,0:T(8,128)(2,1)S(1)}, u32[]{:S(2)}, u32[]{:S(2)}) collective-permute-start(bf16[928,128]{1,0:T(8,128)(2,1)S(1)} %get-tuple-element.91), channel_id=1, source_target_pairs={{0,2},{2,4},{4,6},{6,0},{1,3},{3,5},{5,7},{7,1},{8,10},{10,12},{12... | collective-permute-start | bytes 712712 | tf_op jit(solution)/shard_map/ppermute | solution.py:821
  67.0 17.6 %collective-permute-start.14 = (bf16[928,128]{1,0:T(8,128)(2,1)S(1)}, bf16[928,128]{1,0:T(8,128)(2,1)S(1)}, u32[]{:S(2)}, u32[]{:S(2)}) collective-permute-start(bf16[928,128]{1,0:T(8,128)(2,1)S(1)} %get-tuple-element.92), channel_id=1, source_target_pairs={{0,6},{2,0},{4,2},{6,4},{1,7},{3,1},{5,3},{7,5},{8,14},{10,8},{12,... | collective-permute-start | bytes 712712 | tf_op jit(solution)/shard_map/ppermute | solution.py:821
  72.7 28.3 %collective-permute-start.18 = (bf16[768,128]{1,0:T(8,128)(2,1)S(1)}, bf16[768,128]{1,0:T(8,128)(2,1)S(1)}, u32[]{:S(2)}, u32[]{:S(2)}) collective-permute-start(bf16[768,128]{1,0:T(8,128)(2,1)S(1)} %get-tuple-element.99), channel_id=1, source_target_pairs={{0,4},{2,6},{4,0},{6,2},{1,5},{3,7},{5,1},{7,3},{8,12},{10,14},{12... | collective-permute-start | bytes 589832 | tf_op jit(solution)/shard_map/ppermute | solution.py:821
  72.8 28.2 %collective-permute-start.19 = (bf16[768,128]{1,0:T(8,128)(2,1)S(1)}, bf16[768,128]{1,0:T(8,128)(2,1)S(1)}, u32[]{:S(2)}, u32[]{:S(2)}) collective-permute-start(bf16[768,128]{1,0:T(8,128)(2,1)S(1)} %get-tuple-element.100), channel_id=1, source_target_pairs={{0,2},{2,4},{4,6},{6,0},{1,3},{3,5},{5,7},{7,1},{8,10},{10,12},{12... | collective-permute-start | bytes 589832 | tf_op jit(solution)/shard_map/ppermute | solution.py:821
  84.0 16.9 %collective-permute-start.20 = (bf16[768,128]{1,0:T(8,128)(2,1)S(1)}, bf16[768,128]{1,0:T(8,128)(2,1)S(1)}, u32[]{:S(2)}, u32[]{:S(2)}) collective-permute-start(bf16[768,128]{1,0:T(8,128)(2,1)S(1)} %get-tuple-element.101), channel_id=1, source_target_pairs={{0,6},{2,0},{4,2},{6,4},{1,7},{3,1},{5,3},{7,5},{8,14},{10,8},{12,... | collective-permute-start | bytes 589832 | tf_op jit(solution)/shard_map/ppermute | solution.py:821
  85.4 17.1 %collective-permute-start.15 = (f32[128,128]{1,0:T(8,128)S(1)}, f32[128,128]{1,0:T(8,128)S(1)}, u32[]{:S(2)}, u32[]{:S(2)}) collective-permute-start(f32[128,128]{1,0:T(8,128)S(1)} %get-tuple-element.93.mine), channel_id=1, source_target_pairs={{0,1},{1,0},{2,3},{3,2},{4,5},{5,4},{6,7},{7,6},{8,9},{9,8},{10,11... | collective-permute-start | bytes 196616 | tf_op jit(solution)/shard_map/ppermute | solution.py:821
  85.4 3.7 %collective-permute-start.16 = (f32[4,8,128]{2,1,0:T(8,128)S(1)}, f32[4,8,128]{2,1,0:T(8,128)S(1)}, u32[]{:S(2)}, u32[]{:S(2)}) collective-permute-start(f32[4,8,128]{2,1,0:T(8,128)S(1)} %get-tuple-element.94), channel_id=1, source_target_pairs={{0,8},{8,0},{16,24},{24,16},{1,9},{9,1},{17,25},{25,17},{2,10},{10... | collective-permute-start | bytes 49160 | tf_op jit(solution)/shard_map/ppermute | solution.py:829
  89.2 13.3 %collective-permute-start.17 = (f32[4,8,128]{2,1,0:T(8,128)S(1)}, f32[4,8,128]{2,1,0:T(8,128)S(1)}, u32[]{:S(2)}, u32[]{:S(2)}) collective-permute-start(f32[4,8,128]{2,1,0:T(8,128)S(1)} %add.7.refs_0_), channel_id=1, source_target_pairs={{0,16},{8,24},{16,0},{24,8},{1,17},{9,25},{17,1},{25,9},{2,18},{10... | collective-permute-start | bytes 49160 | tf_op jit(solution)/shard_map/ppermute | solution.py:829
